TPU v7x, 32 devices: a whole 2x2x4 slice. The times are simulated.
32 devices in a mesh: batch: 8 (over z, core), seq: 4 (over y, x).
Axes of the slice: x: 2, y: 2, z: 4, core: 2. Of those that a mesh axis runs over, the one named last changes fastest.
Arguments:
- inputs: bfloat16 [4096, 7168], P(('batch', 'seq')), parts along dimension 0, may hold values from -6 to 6
- adapter_down: bfloat16 [7168, 384], replicated, may hold values from -0.0625 to 0.0625
- adapter_up: bfloat16 [3, 128, 3584], P(None, None, 'seq'), may hold values from -0.52734375 to 0.52734375
- shared_qkv: bfloat16 [4096, 10752], P(('batch', 'seq')), parts along dimension 0, may hold values from -8 to 8
- sink_logits: float32 [16], P('seq'), may hold values from 0 to 3
- lengths: int32 [64], P('batch'), parts along dimension 0, may hold values from 1 to 384, as said below
- block_table: int32 [64, 24], P('batch'), parts along dimension 0, may hold values from 0 to 39, as said below
Outputs:
- hidden: bfloat16 [4096, 3584], P(('batch', 'seq')), parts along dimension 0
- kv_cache: bfloat16 [16, 320, 2, 3584], P('seq', 'batch'), parts along dimension 1
There are 8 independent parts, one for each index of `batch`. A program takes and returns all parts, laid end to end along the dimension named above; an argument that names none is the same for every part. Nothing has to cross between parts.
Inputs may be any that keep to these rules, and one draw needn't show every extreme that they name: The lengths sum to 512; exactly one prompt has 384 tokens. `block_table`: entry b of row s is the page of positions b * 16 to b * 16 + 15 of prompt s; only entries below ceil(lengths[s] / 16) are read, and all entries that are read are distinct pages.
All inputs are finite; a program needn't handle non-finite values.
Results may differ from a plain program's by a relative error of at most 0.011.
Values may be sent and summed in bfloat16 or wider, within the bound.
No kernel may reach another device: no remote copies, remote signals or barrier semaphores. Data moves between devices by JAX's collectives and lax.ppermute only.
A program may use at most 128 MiB of HBM per device.

v0:
```python
import jax
import jax.numpy as jnp
from jax import lax
from jax.experimental import pallas as pl
from jax.experimental.pallas import tpu as pltpu
from jax.sharding import PartitionSpec as P

HD = 224
RANK = 128
HEADS = 16
SEGS = 8
PAGE = 16


def segment_positions(lengths, total_rows):
    segment_ends = jnp.cumsum(lengths)
    segment_starts = segment_ends - lengths
    places = jnp.arange(total_rows, dtype=jnp.int32)
    segment = jnp.sum((places[:, None] >= segment_ends[None, :]).astype(jnp.int32), axis=1)
    member = segment[:, None] == jnp.arange(SEGS, dtype=jnp.int32)[None, :]
    offsets = jnp.sum(jnp.where(member, segment_starts[None, :], 0), axis=1)
    return (segment, places - offsets)


def per_device_general(inputs, adapter_down, adapter_up, shared_qkv, sink_logits, lengths, block_table):
    group_size = lax.axis_size("seq")
    tok_rows = inputs.shape[0]
    total_rows = tok_rows * group_size
    heads_local = adapter_up.shape[2] // HD
    window_span = total_rows // 2
    low_codes = jnp.dot(inputs, adapter_down, preferred_element_type=jnp.float32).astype(
        jnp.bfloat16
    )
    shared_base = shared_qkv.reshape(tok_rows, 3, HEADS * HD)
    low_rank = jnp.einsum(
        "tcr,crf->tcf",
        low_codes.reshape(tok_rows, 3, RANK),
        lax.all_gather(adapter_up, "seq", axis=2, tiled=True),
        preferred_element_type=jnp.float32,
    )
    merged = (shared_base.astype(jnp.float32) + low_rank).astype(jnp.bfloat16)
    sending = merged.reshape(tok_rows, 3, HEADS, HD)
    arrived = lax.all_to_all(sending, "seq", split_axis=2, concat_axis=0, tiled=True)
    segment, position = segment_positions(lengths, total_rows)
    tile_rows = min(512, total_rows)
    tile_count = total_rows // tile_rows
    scale_factor = HD ** (-0.5)

    def one_head(head_index):
        query_all = arrived[:, 0, head_index]
        key_all = arrived[:, 1, head_index]
        value_all = arrived[:, 2, head_index]
        sink_logit = sink_logits[head_index]

        def query_tile(tile_index):
            query_first = tile_index * tile_rows
            query_rows = lax.dynamic_slice_in_dim(query_all, query_first, tile_rows, 0)
            query_segs = lax.dynamic_slice_in_dim(segment, query_first, tile_rows, 0)
            query_place = query_first + jnp.arange(tile_rows, dtype=jnp.int32)
            start_state = (
                jnp.full((tile_rows,), sink_logit, jnp.float32),
                jnp.zeros((tile_rows,), jnp.float32),
                jnp.zeros((tile_rows, HD), jnp.float32),
            )

            def visit(key_tile, state):
                key_first = key_tile * tile_rows
                running_max, running_sum, weighted = state
                key_rows = lax.dynamic_slice_in_dim(key_all, key_first, tile_rows, 0)
                value_rows = lax.dynamic_slice_in_dim(value_all, key_first, tile_rows, 0)
                key_segs = lax.dynamic_slice_in_dim(segment, key_first, tile_rows, 0)
                key_place = key_first + jnp.arange(tile_rows, dtype=jnp.int32)
                scores = (
                    jnp.dot(query_rows, key_rows.T, preferred_element_type=jnp.float32)
                    * scale_factor
                )
                visible = (
                    (query_segs[:, None] == key_segs[None, :])
                    & (key_place[None, :] <= query_place[:, None])
                    & (query_place[:, None] - key_place[None, :] < window_span)
                )
                scores = jnp.where(visible, scores, -jnp.inf)
                new_max = jnp.maximum(running_max, jnp.max(scores, axis=1))
                rescale = jnp.exp(running_max - new_max)
                weights = jnp.exp(scores - new_max[:, None])
                new_sum = running_sum * rescale + jnp.sum(weights, axis=1)
                new_weighted = weighted * rescale[:, None] + jnp.dot(
                    weights.astype(jnp.bfloat16), value_rows, preferred_element_type=jnp.float32
                )
                return (new_max, new_sum, new_weighted)

            final_max, final_sum, weighted = lax.fori_loop(0, tile_count, visit, start_state)
            denominator = final_sum + jnp.exp(sink_logit - final_max)
            return (weighted / denominator[:, None]).astype(jnp.bfloat16)

        return lax.map(query_tile, jnp.arange(tile_count, dtype=jnp.int32)).reshape(total_rows, HD)

    attended = lax.map(one_head, jnp.arange(heads_local, dtype=jnp.int32))
    returned = lax.all_to_all(attended, "seq", split_axis=1, concat_axis=0, tiled=True)
    hidden = returned.transpose(1, 0, 2).reshape(tok_rows, HEADS * HD)
    page_count = total_rows // PAGE + SEGS
    page_index = block_table.reshape(-1)[segment * block_table.shape[1] + position // PAGE]
    cache_row = page_index * PAGE + position % PAGE

    def place(values_in):
        flat_cache = (
            jnp.zeros((page_count * PAGE, heads_local, HD), jnp.bfloat16)
            .at[cache_row]
            .set(values_in)
        )
        return (
            flat_cache.reshape(page_count, PAGE, heads_local, HD)
            .transpose(2, 0, 1, 3)
            .reshape(heads_local, page_count, PAGE * HD)
        )

    kv_cache = jnp.stack([place(arrived[:, 1]), place(arrived[:, 2])], axis=2)
    return (hidden, kv_cache)


LANES = 128
BF16 = jnp.bfloat16
F32 = jnp.float32
ANYWHERE = pl.BlockSpec(memory_space=pl.ANY)
IN_HBM = pl.BlockSpec(memory_space=pltpu.HBM)
IN_VMEM = pl.BlockSpec(memory_space=pltpu.VMEM)
IN_SMEM = pl.BlockSpec(memory_space=pltpu.SMEM)


def sends(group_size):
    return sorted(range(1, group_size), key=lambda bits: (-bits.bit_count(), bits))


def to_partner(values, bits, group_size):
    return lax.ppermute(values, "seq", [(i, i ^ bits) for i in range(group_size)])


def params(mebibytes=40):
    return pltpu.CompilerParams(vmem_limit_bytes=mebibytes * 1024 * 1024)


def stay(values):
    return pltpu.with_memory_space_constraint(values, pltpu.HBM)


def cost(flops, moved):
    return pl.CostEstimate(flops=flops, bytes_accessed=moved, transcendentals=0)


def column_copies(shared, outs, sem, width, tiles, group_size):
    me = lax.axis_index("seq")
    span = (tiles[1] - tiles[0]) * LANES
    copies = []
    for n, bits in enumerate(sends(group_size) + [0]):
        owner = jnp.bitwise_xor(me, bits)
        for c in range(3):
            first = pl.multiple_of(c * HEADS * HD + owner * width + tiles[0] * LANES, LANES)
            copies.append(
                pltpu.make_async_copy(
                    shared.at[:, pl.ds(first, span)],
                    outs[n].at[:, pl.ds(c * span, span)],
                    sem.at[n, c],
                )
            )
    return copies


def make_codes(inputs, adapter_down, shared_qkv, width, tiles, group_size):
    tok_rows, depth = inputs.shape
    code_width = adapter_down.shape[1]
    steps = 8
    chunk = depth // steps
    span = 3 * (tiles[1] - tiles[0]) * LANES

    def body(inputs_ref, down_ref, shared, *refs):
        outs, (held, down, in_sem, down_sem, sem) = refs[:-5], refs[-5:]
        loads = []
        for step in range(steps):
            at = pl.ds(step * chunk, chunk)
            loads.append(
                (
                    pltpu.make_async_copy(inputs_ref.at[:, at], held.at[:, at], in_sem.at[step]),
                    pltpu.make_async_copy(down_ref.at[at, :], down.at[at, :], down_sem.at[step]),
                )
            )
            for load in loads[-1]:
                load.start()
        copies = column_copies(shared, outs, sem, width, tiles, group_size)
        for copy in copies:
            copy.start()
        total = None
        for step in range(steps):
            for load in loads[step]:
                load.wait()
            at = slice(step * chunk, (step + 1) * chunk)
            term = jnp.dot(held[:, at], down[at, :], preferred_element_type=F32)
            total = term if total is None else total + term
        own_codes = total.astype(BF16)
        for out in outs:
            out[:, span:] = own_codes
        for copy in copies:
            copy.wait()

    return pl.pallas_call(
        body,
        out_shape=[jax.ShapeDtypeStruct((tok_rows, span + code_width), BF16)] * group_size,
        in_specs=[IN_HBM, IN_HBM, IN_HBM],
        out_specs=[IN_VMEM] * group_size,
        scratch_shapes=[
            pltpu.VMEM((tok_rows, depth), BF16),
            pltpu.VMEM((depth, code_width), BF16),
            pltpu.SemaphoreType.DMA((steps,)),
            pltpu.SemaphoreType.DMA((steps,)),
            pltpu.SemaphoreType.DMA((group_size, 3)),
        ],
        compiler_params=params(20),
        cost_estimate=cost(2 * tok_rows * depth * code_width, depth * code_width * 2),
        name="make_codes",
    )(stay(inputs), stay(adapter_down), stay(shared_qkv))


def pack_qkv(shared_qkv, after, width, tiles, group_size):
    tok_rows = shared_qkv.shape[0]
    span = 3 * (tiles[1] - tiles[0]) * LANES

    def body(shared, _, *refs):
        copies = column_copies(shared, refs[:-1], refs[-1], width, tiles, group_size)
        for copy in copies:
            copy.start()
        for copy in copies:
            copy.wait()

    return pl.pallas_call(
        body,
        out_shape=[jax.ShapeDtypeStruct((tok_rows, span), BF16)] * group_size,
        in_specs=[IN_HBM, ANYWHERE],
        out_specs=[IN_VMEM] * group_size,
        scratch_shapes=[pltpu.SemaphoreType.DMA((group_size, 3))],
        compiler_params=params(20),
        cost_estimate=cost(0, 2 * group_size * tok_rows * span * 2),
        name="pack_qkv",
    )(stay(shared_qkv), after)


def head_tiles(h):
    return (h * HD // LANES, -(-(h + 1) * HD // LANES))


def side_by_side(ref, window, rows):
    return jnp.concatenate([ref[tile, rows, :] for tile in window], axis=1)


def attend(up, sink_logits, lengths, low_rank, arrived, carried, after, heads, tiles, done_tiles, group_size):
    tok_rows = arrived[0].shape[0]
    total_rows = tok_rows * group_size
    window_span = total_rows // 2
    scale_factor = HD ** (-0.5)
    span = (tiles[1] - tiles[0]) * LANES
    done_span = (done_tiles[1] - done_tiles[0]) * LANES
    low_tile = min(tiles[0], done_tiles[0])
    kept = (tiles[0] - low_tile) * LANES
    left = (tiles[1] - done_tiles[1]) * LANES
    first_call, last = low_rank is None, left == 0
    all_tiles = (kept + span) // LANES
    given_low = [] if first_call else [low_rank]
    rest = up.shape[2] - tiles[1] * LANES

    def body(*refs):
        refs = list(refs)
        take = lambda n: [refs.pop(0) for _ in range(n)]
        up_ref, sinks, lens = take(3)
        low_refs = take(len(given_low))
        arrived_refs = take(group_size)
        before = take(len(carried))
        take(len(after))
        outs = take(group_size)
        keys, values = take(2)
        carried_out = take(0 if last else 3)
        queries, merged = take(2)
        me = lax.axis_index("seq")
        kept_tiles = kept // LANES
        if kept:
            for target, source in zip((queries, merged, keys, values), before):
                target[:kept_tiles] = source[source.shape[0] - kept_tiles :]
        for bits in range(group_size):
            source = arrived_refs[bits]
            place = pl.ds(pl.multiple_of(jnp.bitwise_xor(me, bits) * tok_rows, tok_rows), tok_rows)
            for c, target in enumerate((queries, keys, values)):
                if first_call:
                    at = 3 * span + c * RANK
                    codes = source[:, at : at + RANK]
                    low = jnp.dot(codes, up_ref[c, :, :span], preferred_element_type=F32)
                    carried_out[0][bits, :, c * rest : (c + 1) * rest] = jnp.dot(
                        codes, up_ref[c, :, span:], preferred_element_type=F32
                    )
                else:
                    low = low_refs[0][bits, :, c * span : (c + 1) * span]
                base = source[:, c * span : (c + 1) * span].astype(F32)
                new = (base + low).astype(BF16)
                for n in range(tiles[1] - tiles[0]):
                    target[kept_tiles + n, place, :] = new[:, n * LANES : (n + 1) * LANES]

        ends = []
        for s in range(SEGS):
            ends.append(lens[s] + (ends[-1] if ends else 0))
        blocks = []
        for b in range(group_size):
            first_query = b * tok_rows
            rows = slice(first_query, first_query + tok_rows)
            first_key = max(0, (first_query - window_span + 1) // tok_rows * tok_rows)
            key_rows = slice(first_key, first_query + tok_rows)
            query_place = first_query + lax.broadcasted_iota(jnp.int32, (tok_rows, 1), 0)
            earliest = query_place - (window_span - 1)
            for s in range(SEGS):
                earliest = jnp.where(ends[s] <= query_place, jnp.maximum(earliest, ends[s]), earliest)
            key_place = first_key + lax.broadcasted_iota(jnp.int32, (tok_rows, key_rows.stop - first_key), 1)
            visible = (key_place >= earliest) & (key_place <= query_place)
            scores = {}
            for h in heads:
                first_tile, end_tile = head_tiles(h)
                window = range(first_tile - low_tile, end_tile - low_tile)
                column = first_tile * LANES + lax.broadcasted_iota(jnp.int32, (1, len(window) * LANES), 1)
                mine = (column >= h * HD) & (column < (h + 1) * HD)
                query = side_by_side(queries, window, rows)
                query = jnp.where(mine, query, jnp.zeros_like(query))
                scores[h] = lax.dot_general(
                    query,
                    side_by_side(keys, window, key_rows),
                    (((1,), (1,)), ((), ())),
                    preferred_element_type=F32,
                )
            blocks.append((rows, key_rows, visible, scores))
        for rows, key_rows, visible, scores in blocks:
            parts = {}
            for tile in range(low_tile, tiles[0]):
                parts[tile] = merged[tile - low_tile, rows, :].astype(F32)
            for h in heads:
                first_tile, end_tile = head_tiles(h)
                window = range(first_tile - low_tile, end_tile - low_tile)
                seen = jnp.where(visible, scores[h] * scale_factor, -jnp.inf)
                top = jnp.maximum(jnp.max(seen, axis=1, keepdims=True), sinks[h])
                weights = jnp.exp(seen - top)
                denominator = jnp.sum(weights, axis=1, keepdims=True) + jnp.exp(sinks[h] - top)
                mixed = jnp.dot(
                    weights.astype(BF16),
                    side_by_side(values, window, key_rows),
                    preferred_element_type=F32,
                ) / denominator
                for tile in range(first_tile, end_tile):
                    at = (tile - first_tile) * LANES
                    piece = mixed[:, at : at + LANES]
                    if tile in parts:
                        lane = tile * LANES + lax.broadcasted_iota(jnp.int32, (1, LANES), 1)
                        piece = jnp.where(lane < h * HD, parts[tile], piece)
                    parts[tile] = piece
            for tile, piece in parts.items():
                merged[tile - low_tile, rows, :] = piece.astype(BF16)
        for bits in range(group_size):
            place = pl.ds(pl.multiple_of(jnp.bitwise_xor(me, bits) * tok_rows, tok_rows), tok_rows)
            outs[bits][...] = side_by_side(merged, range(done_tiles[1] - done_tiles[0]), place)
        if not last:
            carried_out[1][...] = queries[all_tiles - left // LANES :]
            carried_out[2][...] = merged[all_tiles - left // LANES :]

    block = jax.ShapeDtypeStruct((tok_rows, done_span), BF16)
    stream = jax.ShapeDtypeStruct((all_tiles, total_rows, LANES), BF16)
    leftover = jax.ShapeDtypeStruct((left // LANES, total_rows, LANES), BF16)
    next_low = jax.ShapeDtypeStruct((group_size, tok_rows, 3 * rest), F32)
    out_shape = [block] * group_size + [stream] * 2 + ([] if last else [next_low, leftover, leftover])
    results = pl.pallas_call(
        body,
        out_shape=out_shape,
        in_specs=[IN_VMEM, IN_SMEM, IN_SMEM]
        + [IN_VMEM] * (len(given_low) + group_size + len(carried))
        + [ANYWHERE] * len(after),
        out_specs=[IN_VMEM] * len(out_shape),
        scratch_shapes=[pltpu.VMEM((all_tiles, total_rows, LANES), BF16)] * 2,
        compiler_params=params(),
        cost_estimate=cost(4 * total_rows * total_rows * span, 8 * total_rows * span * 2),
        name="attend",
    )(up, sink_logits, lengths, *given_low, *arrived, *carried, *map(stay, after))
    blocks, (keys, values) = results[:group_size], results[group_size : group_size + 2]
    if last:
        return blocks, keys, values, None, []
    next_low, *leftovers = results[group_size + 2 :]
    return blocks, keys, values, next_low, [*leftovers, keys, values]


def build_cache(cache, after, keys, values, first_tile, lengths, block_table, heads, heads_local):
    total_rows, width = keys.shape[1], keys.shape[0] * LANES
    page_count = total_rows // PAGE + SEGS
    blocks = block_table.shape[1]
    rows = 2 * page_count
    given = [] if cache is None else [cache]

    def body(*refs):
        refs = list(refs)
        take = lambda n: [refs.pop(0) for _ in range(n)]
        key_ref, value_ref, lens, table = take(4)
        take(len(given) + len(after))
        out, built, sem = take(3)
        row = lax.broadcasted_iota(jnp.int32, (rows, blocks), 0)
        page = lax.shift_right_logical(row, 1)
        block = lax.broadcasted_iota(jnp.int32, (rows, blocks), 1)
        first = jnp.zeros((rows, blocks), jnp.int32)
        count = jnp.zeros((rows, blocks), jnp.int32)
        start = 0
        for s in range(SEGS):
            left = lens[s] - block * PAGE
            held = (table[s : s + 1, :] == page) & (left > 0)
            first = jnp.where(held, start + block * PAGE, first)
            count = jnp.where(held, jnp.minimum(left, PAGE), count)
            start = start + lens[s]
        first = jnp.sum(first, axis=1, keepdims=True)
        count = jnp.sum(count, axis=1, keepdims=True)
        odd = jnp.bitwise_and(lax.broadcasted_iota(jnp.int32, (rows, 1), 0), 1)
        place = lax.broadcasted_iota(jnp.int32, (rows, total_rows), 1)
        every = (range(keys.shape[0]), slice(None))
        all_keys, all_values = side_by_side(key_ref, *every), side_by_side(value_ref, *every)
        picked = []
        for r in range(PAGE):
            for_keys = jnp.where((odd == 0) & (count > r), first + r, -1)
            for_values = jnp.where((odd == 1) & (count > r), first + r, -1)
            pick_keys = (place == for_keys).astype(F32).astype(BF16)
            pick_values = (place == for_values).astype(F32).astype(BF16)
            picked.append(
                jnp.dot(pick_keys, all_keys, preferred_element_type=F32)
                + jnp.dot(pick_values, all_values, preferred_element_type=F32)
            )
        copies = []
        for n, h in enumerate(heads):
            lo = h * HD - first_tile * LANES
            line = jnp.concatenate([columns[:, lo : lo + HD] for columns in picked], axis=1)
            built[n] = line.astype(BF16).reshape(page_count, 2, PAGE * HD)
            copies.append(pltpu.make_async_copy(built.at[n], out.at[h], sem.at[n]))
            copies[-1].start()
        for copy in copies:
            copy.wait()

    return pl.pallas_call(
        body,
        out_shape=jax.ShapeDtypeStruct((heads_local, page_count, 2, PAGE * HD), BF16),
        in_specs=[IN_VMEM, IN_VMEM, IN_SMEM, IN_VMEM] + [IN_HBM] * len(given) + [ANYWHERE] * len(after),
        out_specs=IN_HBM,
        scratch_shapes=[
            pltpu.VMEM((len(heads), page_count, 2, PAGE * HD), BF16),
            pltpu.SemaphoreType.DMA((len(heads),)),
        ],
        input_output_aliases={4: 0} if given else {},
        compiler_params=params(),
        cost_estimate=cost(4 * rows * PAGE * total_rows * width, 4 * total_rows * width * 2),
        name="build_cache",
    )(keys, values, lengths, block_table, *map(stay, given), *map(stay, after))


def join_heads(hidden, blocks, first_column, width, group_size):
    tok_rows, span = blocks[0].shape
    given = [] if hidden is None else [hidden]

    def body(*refs):
        sources, out, sem = refs[:group_size], refs[-2], refs[-1]
        me = lax.axis_index("seq")
        copies = []
        for bits in range(group_size):
            first = pl.multiple_of(jnp.bitwise_xor(me, bits) * width + first_column, LANES)
            copies.append(
                pltpu.make_async_copy(sources[bits], out.at[:, pl.ds(first, span)], sem.at[bits])
            )
        for copy in copies:
            copy.start()
        for copy in copies:
            copy.wait()

    return pl.pallas_call(
        body,
        out_shape=jax.ShapeDtypeStruct((tok_rows, width * group_size), BF16),
        in_specs=[ANYWHERE] * group_size + [IN_HBM] * len(given),
        out_specs=IN_HBM,
        scratch_shapes=[pltpu.SemaphoreType.DMA((group_size,))],
        input_output_aliases={group_size: 0} if given else {},
        compiler_params=params(),
        cost_estimate=cost(0, 2 * tok_rows * span * group_size * 2),
        name="join_heads",
    )(*blocks, *map(stay, given))


def per_device_tiled(inputs, adapter_down, adapter_up, shared_qkv, sink_logits, lengths, block_table):
    group_size = lax.axis_size("seq")
    partners = sends(group_size)
    width = adapter_up.shape[2]
    heads_local = width // HD
    half = heads_local // 2
    all_tiles = width // LANES
    cut = -(-half * HD // LANES)
    done_cut = half * HD // LANES
    tiles = [(0, cut), (cut, all_tiles)]
    done_tiles = [(0, done_cut), (done_cut, all_tiles)]
    heads = [tuple(range(half)), tuple(range(half, heads_local))]

    def send(parts):
        return {bits: to_partner(part, bits, group_size) for bits, part in zip(partners, parts)}

    *parts, own = make_codes(inputs, adapter_down, shared_qkv, width, tiles[0], group_size)
    arrived = [{0: own, **send(parts)}]
    *parts, own = pack_qkv(shared_qkv, own, width, tiles[1], group_size)
    arrived.append({0: own, **send(parts)})
    low_rank, carried, cache, hidden = None, [], None, None
    for n in range(2):
        blocks, keys, values, low_rank, carried = attend(
            adapter_up,
            sink_logits,
            lengths,
            low_rank,
            [arrived[n][bits] for bits in range(group_size)],
            carried,
            [] if cache is None else [cache],
            heads[n],
            tiles[n],
            done_tiles[n],
            group_size,
        )
        returned = send([blocks[bits] for bits in partners])
        returned[0] = blocks[0]
        cache = build_cache(
            cache,
            [] if hidden is None else [hidden],
            keys,
            values,
            done_tiles[n][0],
            lengths,
            block_table,
            heads[n],
            heads_local,
        )
        hidden = join_heads(
            hidden, [returned[bits] for bits in range(group_size)], done_tiles[n][0] * LANES, width, group_size
        )
    return (hidden, cache)


def per_device(inputs, adapter_down, adapter_up, shared_qkv, sink_logits, lengths, block_table):
    group_size = lax.axis_size("seq")
    width = adapter_up.shape[2]
    tiled = (
        group_size & (group_size - 1) == 0
        and width % (2 * HD) == 0
        and width % LANES == 0
        and inputs.shape[0] % LANES == 0
        and inputs.shape[0] * group_size <= 512
    )
    chosen = per_device_tiled if tiled else per_device_general
    return chosen(inputs, adapter_down, adapter_up, shared_qkv, sink_logits, lengths, block_table)


def solution(mesh):
    return jax.shard_map(
        per_device,
        mesh=mesh,
        in_specs=(
            P(("batch", "seq"), None),
            P(),
            P(None, None, "seq"),
            P(("batch", "seq"), None),
            P("seq"),
            P("batch"),
            P("batch", None),
        ),
        out_specs=(P(("batch", "seq"), None), P("seq", "batch", None, None)),
        check_vma=False,
    )
```

profile of v0, /device:TPU:0, one launch (start us, length us, event | category | flops | bytes accessed | tf_op | source)
XLA Modules:
  0.0 58.8 jit_solution(9522691333682159702)
XLA Ops:
  0.6 4.2 %make_codes.1 = (bf16[128,1920]{1,0:T(8,128)(2,1)S(1)}, bf16[128,1920]{1,0:T(8,128)(2,1)S(1)}, bf16[128,1920]{1,0:T(8,128)(2,1)S(1)}, bf16[128,1920]{1,0:T(8,128)(2,1)S(1)}) custom-call(bf16[128,7168]{1,0:T(8,128)(2,1)} %inputs_ref.1, bf16[7168,384]{1,0:T(8,128)(2,1)} %down_ref.1, bf16[128,10752]{1,0:T(8,128)(2,1)} %shared.3), custom_call_target="tpu_custom_call" | custom-call | flops 704643072 | bytes 5505024 | tf_op jit(solution)/shard_map/make_codes/pallas_call | solution.py:204
  4.9 0.0 copy-start.1
  4.9 3.0 %collective-permute-start = (bf16[128,1920]{1,0:T(8,128)(2,1)S(1)}, bf16[128,1920]{1,0:T(8,128)(2,1)S(1)}, u32[]{:S(2)}, u32[]{:S(2)}) collective-permute-start(bf16[128,1920]{1,0:T(8,128)(2,1)S(1)} %get-tuple-element.26), channel_id=1, source_target_pairs={{0,1},{1,0},{2,3},{3,2},{4,5},{5,4},{6,7},{7,6},{8,9},{9,8},{10,11... | collective-permute-start | bytes 1474568 | tf_op jit(solution)/shard_map/ppermute | solution.py:135
  7.9 1.5 %collective-permute-start.1 = (bf16[128,1920]{1,0:T(8,128)(2,1)S(1)}, bf16[128,1920]{1,0:T(8,128)(2,1)S(1)}, u32[]{:S(2)}, u32[]{:S(2)}) collective-permute-start(bf16[128,1920]{1,0:T(8,128)(2,1)S(1)} %get-tuple-element.27), channel_id=1, source_target_pairs={{0,2},{1,3},{2,0},{3,1},{4,6},{5,7},{6,4},{7,5},{8,10},{9,11},{10,... | collective-permute-start | bytes 1474568 | tf_op jit(solution)/shard_map/ppermute | solution.py:135
  9.4 0.0 collective-permute-start.2
  9.4 1.5 %pack_qkv.1 = (bf16[128,1152]{1,0:T(8,128)(2,1)S(1)}, bf16[128,1152]{1,0:T(8,128)(2,1)S(1)}, bf16[128,1152]{1,0:T(8,128)(2,1)S(1)}, bf16[128,1152]{1,0:T(8,128)(2,1)S(1)}) custom-call(bf16[128,10752]{1,0:T(8,128)(2,1)} %shared.3, bf16[128,1920]{1,0:T(8,128)(2,1)S(1)} %get-tuple-element.25.refs_3_._), custom_call_target="tpu_custom_call" | custom-call | bytes 2359296 | tf_op jit(solution)/shard_map/pack_qkv/pallas_call | solution.py:233
  10.9 2.0 %collective-permute-start.3 = (bf16[128,1152]{1,0:T(8,128)(2,1)S(1)}, bf16[128,1152]{1,0:T(8,128)(2,1)S(1)}, u32[]{:S(2)}, u32[]{:S(2)}) collective-permute-start(bf16[128,1152]{1,0:T(8,128)(2,1)S(1)} %get-tuple-element.31), channel_id=1, source_target_pairs={{0,1},{1,0},{2,3},{3,2},{4,5},{5,4},{6,7},{7,6},{8,9},{9,8},{10,11... | collective-permute-start | bytes 884744 | tf_op jit(solution)/shard_map/ppermute | solution.py:135
  12.9 1.5 %collective-permute-start.4 = (bf16[128,1152]{1,0:T(8,128)(2,1)S(1)}, bf16[128,1152]{1,0:T(8,128)(2,1)S(1)}, u32[]{:S(2)}, u32[]{:S(2)}) collective-permute-start(bf16[128,1152]{1,0:T(8,128)(2,1)S(1)} %get-tuple-element.32), channel_id=1, source_target_pairs={{0,2},{1,3},{2,0},{3,1},{4,6},{5,7},{6,4},{7,5},{8,10},{9,11},{10,... | collective-permute-start | bytes 884744 | tf_op jit(solution)/shard_map/ppermute | solution.py:135
  14.4 5.5 %collective-permute-done.refs_4_ = bf16[128,1920]{1,0:T(8,128)(2,1)S(1)} collective-permute-done((bf16[128,1920]{1,0:T(8,128)(2,1)S(1)}, bf16[128,1920]{1,0:T(8,128)(2,1)S(1)}, u32[]{:S(2)}, u32[]{:S(2)}) %collective-permute-start) | collective-permute-done | bytes 491552 | tf_op jit(solution)/shard_map/ppermute | solution.py:135
  19.9 3.0 %collective-permute-start.5 = (bf16[128,1152]{1,0:T(8,128)(2,1)S(1)}, bf16[128,1152]{1,0:T(8,128)(2,1)S(1)}, u32[]{:S(2)}, u32[]{:S(2)}) collective-permute-start(bf16[128,1152]{1,0:T(8,128)(2,1)S(1)} %get-tuple-element.33), channel_id=1, source_target_pairs={{0,3},{1,2},{2,1},{3,0},{4,7},{5,6},{6,5},{7,4},{8,11},{9,10},{10,... | collective-permute-start | bytes 884744 | tf_op jit(solution)/shard_map/ppermute | solution.py:135
  22.9 9.6 %collective-permute-done.1.refs_5_ = bf16[128,1920]{1,0:T(8,128)(2,1)S(1)} collective-permute-done((bf16[128,1920]{1,0:T(8,128)(2,1)S(1)}, bf16[128,1920]{1,0:T(8,128)(2,1)S(1)}, u32[]{:S(2)}, u32[]{:S(2)}) %collective-permute-start.1) | collective-permute-done | bytes 491552 | tf_op jit(solution)/shard_map/ppermute | solution.py:135
  32.6 2.7 %attend.2 = (bf16[128,384]{1,0:T(8,128)(2,1)S(1)}, bf16[128,384]{1,0:T(8,128)(2,1)S(1)}, bf16[128,384]{1,0:T(8,128)(2,1)S(1)}, bf16[128,384]{1,0:T(8,128)(2,1)S(...) custom-call(bf16[3,128,896]{2,1,0:T(8,128)(2,1)S(1)} %copy-done, ...), custom_call_target="tpu_custom_call" | custom-call | flops 536870912 | bytes 4194304 | tf_op jit(solution)/shard_map/attend/pallas_call | solution.py:370
  35.3 1.0 %collective-permute-start.9 = (bf16[128,384]{1,0:T(8,128)(2,1)S(1)}, bf16[128,384]{1,0:T(8,128)(2,1)S(1)}, u32[]{:S(2)}, u32[]{:S(2)}) collective-permute-start(bf16[128,384]{1,0:T(8,128)(2,1)S(1)} %get-tuple-element.43), channel_id=1, source_target_pairs={{0,1},{1,0},{2,3},{3,2},{4,5},{5,4},{6,7},{7,6},{8,9},{9,8},{10,11... | collective-permute-start | bytes 294920 | tf_op jit(solution)/shard_map/ppermute | solution.py:135
  36.3 1.1 %collective-permute-start.10 = (bf16[128,384]{1,0:T(8,128)(2,1)S(1)}, bf16[128,384]{1,0:T(8,128)(2,1)S(1)}, u32[]{:S(2)}, u32[]{:S(2)}) collective-permute-start(bf16[128,384]{1,0:T(8,128)(2,1)S(1)} %get-tuple-element.44), channel_id=1, source_target_pairs={{0,2},{1,3},{2,0},{3,1},{4,6},{5,7},{6,4},{7,5},{8,10},{9,11},{10,... | collective-permute-start | bytes 294920 | tf_op jit(solution)/shard_map/ppermute | solution.py:135
  37.4 2.5 %collective-permute-start.11 = (bf16[128,384]{1,0:T(8,128)(2,1)S(1)}, bf16[128,384]{1,0:T(8,128)(2,1)S(1)}, u32[]{:S(2)}, u32[]{:S(2)}) collective-permute-start(bf16[128,384]{1,0:T(8,128)(2,1)S(1)} %get-tuple-element.45), channel_id=1, source_target_pairs={{0,3},{1,2},{2,1},{3,0},{4,7},{5,6},{6,5},{7,4},{8,11},{9,10},{10,... | collective-permute-start | bytes 294920 | tf_op jit(solution)/shard_map/ppermute | solution.py:135
  39.8 5.2 %build_cache.2.refs_12_.refs_4_ = bf16[4,40,2,3584]{3,2,1,0:T(2,128)(2,1)} custom-call(bf16[4,512,128]{2,1,0:T(8,128)(2,1)S(1)} %get-tuple-element.36.refs_0_.refs_10_, bf16[4,512,128]{2,1,0:T(8,128)(2,1)S(1)} %get-tuple-element.37.refs_1_.refs_11_, s32[8]{0:T(128)S(1)} %copy-done.1, s32[8,24]{1,0:T(8,128)S(1)} %copy-done.2), custom_call_target="tpu_custom_call" | custom-call | flops 1342177280 | bytes 2097152 | tf_op jit(solution)/shard_map/build_cache/pallas_call | solution.py:440
  45.0 1.0 %collective-permute-done.4.refs_6_ = bf16[128,1152]{1,0:T(8,128)(2,1)S(1)} collective-permute-done((bf16[128,1152]{1,0:T(8,128)(2,1)S(1)}, bf16[128,1152]{1,0:T(8,128)(2,1)S(1)}, u32[]{:S(2)}, u32[]{:S(2)}) %collective-permute-start.4) | collective-permute-done | bytes 294944 | tf_op jit(solution)/shard_map/ppermute | solution.py:135
  46.0 2.1 %attend.3 = (bf16[128,512]{1,0:T(8,128)(2,1)S(1)}, bf16[128,512]{1,0:T(8,128)(2,1)S(1)}, bf16[128,512]{1,0:T(8,128)(2,1)S(1)}, bf16[128,512]{1,0:T(8,128)(2,1)S(...) custom-call(bf16[3,128,896]{2,1,0:T(8,128)(2,1)S(1)} %copy-done, f32[4]{0:T(128)S(1)} %copy-done.3, ...), custom_call_target="tpu_custom_call" | custom-call | flops 402653184 | bytes 3145728 | tf_op jit(solution)/shard_map/attend/pallas_call | solution.py:370
  48.0 0.3 collective-permute-start.6
  48.4 2.3 %collective-permute-start.7 = (bf16[128,512]{1,0:T(8,128)(2,1)S(1)}, bf16[128,512]{1,0:T(8,128)(2,1)S(1)}, u32[]{:S(2)}, u32[]{:S(2)}) collective-permute-start(bf16[128,512]{1,0:T(8,128)(2,1)S(1)} %get-tuple-element.40), channel_id=1, source_target_pairs={{0,2},{1,3},{2,0},{3,1},{4,6},{5,7},{6,4},{7,5},{8,10},{9,11},{10,... | collective-permute-start | bytes 393224 | tf_op jit(solution)/shard_map/ppermute | solution.py:135
  50.6 1.4 %collective-permute-start.8 = (bf16[128,512]{1,0:T(8,128)(2,1)S(1)}, bf16[128,512]{1,0:T(8,128)(2,1)S(1)}, u32[]{:S(2)}, u32[]{:S(2)}) collective-permute-start(bf16[128,512]{1,0:T(8,128)(2,1)S(1)} %get-tuple-element.41), channel_id=1, source_target_pairs={{0,3},{1,2},{2,1},{3,0},{4,7},{5,6},{6,5},{7,4},{8,11},{9,10},{10,... | collective-permute-start | bytes 393224 | tf_op jit(solution)/shard_map/ppermute | solution.py:135
  52.0 0.8 %join_heads.2.refs_4_.refs_5_ = bf16[128,3584]{1,0:T(8,128)(2,1)} custom-call(bf16[128,384]{1,0:T(8,128)(2,1)S(1)} %get-tuple-element.42.refs_0_, bf16[128,384]{1,0:T(8,128)(2,1)S(1)} %collective-permute-done.9.refs_1_, bf16[128,384]{1,0:T(8,128)(2,1)S(1)} %collective-permute-done.10.refs_2_, bf16[128,384]{1,0:T(8,128)(2,1)S(1)} %collective-permute-done.11.refs_3_), custom_call_target="tpu_custom_call" | custom-call | bytes 786432 | tf_op jit(solution)/shard_map/join_heads/pallas_call | solution.py:474
  52.8 5.1 %build_cache.3 = bf16[4,40,2,3584]{3,2,1,0:T(2,128)(2,1)} custom-call(bf16[4,512,128]{2,1,0:T(8,128)(2,1)S(1)} %get-tuple-element.46.refs_0_, bf16[4,512,128]{2,1,0:T(8,128)(2,1)S(1)} %get-tuple-element.47.refs_1_, s32[8]{0:T(128)S(1)} %copy-done.1, s32[8,24]{1,0:T(8,128)S(1)} %copy-done.2, ...), custom_call_target="tpu_custom_call", output_to_operand_aliasing={{}: (4, {})} | custom-call | flops 1342177280 | bytes 2097152 | tf_op jit(solution)/shard_map/build_cache/pallas_call | solution.py:440
  58.0 0.8 %join_heads.3 = bf16[128,3584]{1,0:T(8,128)(2,1)} custom-call(bf16[128,512]{1,0:T(8,128)(2,1)S(1)} %get-tuple-element.38.refs_0_, bf16[128,512]{1,0:T(8,128)(2,1)S(1)} %collective-permute-done.6.refs_1_, bf16[128,512]{1,0:T(8,128)(2,1)S(1)} %collective-permute-done.7.refs_2_, ...), custom_call_target="tpu_custom_call", output_to_operand_aliasing={{}: (4, {})} | custom-call | bytes 1048576 | tf_op jit(solution)/shard_map/join_heads/pallas_call | solution.py:474
  (16 shorter events, 0.0 us)
Async XLA Ops:
  4.8 27.7 %copy-start = (bf16[3,128,896]{2,1,0:T(8,128)(2,1)S(1)}, bf16[3,128,896]{2,1,0:T(8,128)(2,1)}, u32[]{:S(2)}) copy-start(bf16[3,128,896]{2,1,0:T(8,128)(2,1)} %refs_0_.3) | copy-start | bytes 2064388
  4.9 27.7 %copy-start.1 = (s32[8]{0:T(128)S(1)}, s32[8]{0:T(128)}, u32[]{:S(2)}) copy-start(s32[8]{0:T(128)} %refs_2_.7) | copy-start | bytes 100
  4.9 27.7 %copy-start.3 = (f32[4]{0:T(128)S(1)}, f32[4]{0:T(128)}, u32[]{:S(2)}) copy-start(f32[4]{0:T(128)} %refs_1_.3) | copy-start | bytes 52
  4.9 15.1 %collective-permute-start = (bf16[128,1920]{1,0:T(8,128)(2,1)S(1)}, bf16[128,1920]{1,0:T(8,128)(2,1)S(1)}, u32[]{:S(2)}, u32[]{:S(2)}) collective-permute-start(bf16[128,1920]{1,0:T(8,128)(2,1)S(1)} %get-tuple-element.26), channel_id=1, source_target_pairs={{0,1},{1,0},{2,3},{3,2},{4,5},{5,4},{6,7},{7,6},{8,9},{9,8},{10,11... | collective-permute-start | bytes 1474568 | tf_op jit(solution)/shard_map/ppermute | solution.py:135
  7.9 24.7 %collective-permute-start.1 = (bf16[128,1920]{1,0:T(8,128)(2,1)S(1)}, bf16[128,1920]{1,0:T(8,128)(2,1)S(1)}, u32[]{:S(2)}, u32[]{:S(2)}) collective-permute-start(bf16[128,1920]{1,0:T(8,128)(2,1)S(1)} %get-tuple-element.27), channel_id=1, source_target_pairs={{0,2},{1,3},{2,0},{3,1},{4,6},{5,7},{6,4},{7,5},{8,10},{9,11},{10,... | collective-permute-start | bytes 1474568 | tf_op jit(solution)/shard_map/ppermute | solution.py:135
  9.4 23.2 %collective-permute-start.2 = (bf16[128,1920]{1,0:T(8,128)(2,1)S(1)}, bf16[128,1920]{1,0:T(8,128)(2,1)S(1)}, u32[]{:S(2)}, u32[]{:S(2)}) collective-permute-start(bf16[128,1920]{1,0:T(8,128)(2,1)S(1)} %get-tuple-element.28), channel_id=1, source_target_pairs={{0,3},{1,2},{2,1},{3,0},{4,7},{5,6},{6,5},{7,4},{8,11},{9,10},{10,... | collective-permute-start | bytes 1474568 | tf_op jit(solution)/shard_map/ppermute | solution.py:135
  9.4 30.4 %copy-start.2 = (s32[8,24]{1,0:T(8,128)S(1)}, s32[8,24]{1,0:T(8,128)}, u32[]{:S(2)}) copy-start(s32[8,24]{1,0:T(8,128)} %refs_3_.3) | copy-start | bytes 2308
  10.9 26.5 %collective-permute-start.3 = (bf16[128,1152]{1,0:T(8,128)(2,1)S(1)}, bf16[128,1152]{1,0:T(8,128)(2,1)S(1)}, u32[]{:S(2)}, u32[]{:S(2)}) collective-permute-start(bf16[128,1152]{1,0:T(8,128)(2,1)S(1)} %get-tuple-element.31), channel_id=1, source_target_pairs={{0,1},{1,0},{2,3},{3,2},{4,5},{5,4},{6,7},{7,6},{8,9},{9,8},{10,11... | collective-permute-start | bytes 884744 | tf_op jit(solution)/shard_map/ppermute | solution.py:135
  12.9 33.1 %collective-permute-start.4 = (bf16[128,1152]{1,0:T(8,128)(2,1)S(1)}, bf16[128,1152]{1,0:T(8,128)(2,1)S(1)}, u32[]{:S(2)}, u32[]{:S(2)}) collective-permute-start(bf16[128,1152]{1,0:T(8,128)(2,1)S(1)} %get-tuple-element.32), channel_id=1, source_target_pairs={{0,2},{1,3},{2,0},{3,1},{4,6},{5,7},{6,4},{7,5},{8,10},{9,11},{10,... | collective-permute-start | bytes 884744 | tf_op jit(solution)/shard_map/ppermute | solution.py:135
  19.9 26.0 %collective-permute-start.5 = (bf16[128,1152]{1,0:T(8,128)(2,1)S(1)}, bf16[128,1152]{1,0:T(8,128)(2,1)S(1)}, u32[]{:S(2)}, u32[]{:S(2)}) collective-permute-start(bf16[128,1152]{1,0:T(8,128)(2,1)S(1)} %get-tuple-element.33), channel_id=1, source_target_pairs={{0,3},{1,2},{2,1},{3,0},{4,7},{5,6},{6,5},{7,4},{8,11},{9,10},{10,... | collective-permute-start | bytes 884744 | tf_op jit(solution)/shard_map/ppermute | solution.py:135
  35.3 15.4 %collective-permute-start.9 = (bf16[128,384]{1,0:T(8,128)(2,1)S(1)}, bf16[128,384]{1,0:T(8,128)(2,1)S(1)}, u32[]{:S(2)}, u32[]{:S(2)}) collective-permute-start(bf16[128,384]{1,0:T(8,128)(2,1)S(1)} %get-tuple-element.43), channel_id=1, source_target_pairs={{0,1},{1,0},{2,3},{3,2},{4,5},{5,4},{6,7},{7,6},{8,9},{9,8},{10,11... | collective-permute-start | bytes 294920 | tf_op jit(solution)/shard_map/ppermute | solution.py:135
  36.3 15.8 %collective-permute-start.10 = (bf16[128,384]{1,0:T(8,128)(2,1)S(1)}, bf16[128,384]{1,0:T(8,128)(2,1)S(1)}, u32[]{:S(2)}, u32[]{:S(2)}) collective-permute-start(bf16[128,384]{1,0:T(8,128)(2,1)S(1)} %get-tuple-element.44), channel_id=1, source_target_pairs={{0,2},{1,3},{2,0},{3,1},{4,6},{5,7},{6,4},{7,5},{8,10},{9,11},{10,... | collective-permute-start | bytes 294920 | tf_op jit(solution)/shard_map/ppermute | solution.py:135
  37.4 14.6 %collective-permute-start.11 = (bf16[128,384]{1,0:T(8,128)(2,1)S(1)}, bf16[128,384]{1,0:T(8,128)(2,1)S(1)}, u32[]{:S(2)}, u32[]{:S(2)}) collective-permute-start(bf16[128,384]{1,0:T(8,128)(2,1)S(1)} %get-tuple-element.45), channel_id=1, source_target_pairs={{0,3},{1,2},{2,1},{3,0},{4,7},{5,6},{6,5},{7,4},{8,11},{9,10},{10,... | collective-permute-start | bytes 294920 | tf_op jit(solution)/shard_map/ppermute | solution.py:135
  48.0 9.9 %collective-permute-start.6 = (bf16[128,512]{1,0:T(8,128)(2,1)S(1)}, bf16[128,512]{1,0:T(8,128)(2,1)S(1)}, u32[]{:S(2)}, u32[]{:S(2)}) collective-permute-start(bf16[128,512]{1,0:T(8,128)(2,1)S(1)} %get-tuple-element.39), channel_id=1, source_target_pairs={{0,1},{1,0},{2,3},{3,2},{4,5},{5,4},{6,7},{7,6},{8,9},{9,8},{10,11... | collective-permute-start | bytes 393224 | tf_op jit(solution)/shard_map/ppermute | solution.py:135
  48.4 9.6 %collective-permute-start.7 = (bf16[128,512]{1,0:T(8,128)(2,1)S(1)}, bf16[128,512]{1,0:T(8,128)(2,1)S(1)}, u32[]{:S(2)}, u32[]{:S(2)}) collective-permute-start(bf16[128,512]{1,0:T(8,128)(2,1)S(1)} %get-tuple-element.40), channel_id=1, source_target_pairs={{0,2},{1,3},{2,0},{3,1},{4,6},{5,7},{6,4},{7,5},{8,10},{9,11},{10,... | collective-permute-start | bytes 393224 | tf_op jit(solution)/shard_map/ppermute | solution.py:135
  50.6 7.3 %collective-permute-start.8 = (bf16[128,512]{1,0:T(8,128)(2,1)S(1)}, bf16[128,512]{1,0:T(8,128)(2,1)S(1)}, u32[]{:S(2)}, u32[]{:S(2)}) collective-permute-start(bf16[128,512]{1,0:T(8,128)(2,1)S(1)} %get-tuple-element.41), channel_id=1, source_target_pairs={{0,3},{1,2},{2,1},{3,0},{4,7},{5,6},{6,5},{7,4},{8,11},{9,10},{10,... | collective-permute-start | bytes 393224 | tf_op jit(solution)/shard_map/ppermute | solution.py:135
where the time goes:
time: 59 us; the launch traced here: 58.8 us
  Pallas kernels  22.3 us (38%)
  starting transfers between devices  19.6 us (33%)
  waiting for transfers between devices  16.1 us (27%)
  between operations  0.76 us (1%)
    ppermute x12, starting transfers between devices, to_partner(): lax.ppermute(values, 'seq', [(i, i ^ bits) for i in range(group_size)])  19.6 us
    ppermute x12, waiting for transfers between devices, to_partner(): lax.ppermute(values, 'seq', [(i, i ^ bits) for i in range(group_size)])  16.1 us
    pallas_call x2, Pallas kernels, build_cache(): pl.pallas_call(body, out_shape=jax.ShapeDtypeStruct((heads_local, page_co...  10.3 us
    pallas_call x2, Pallas kernels, attend(): pl.pallas_call(body, out_shape=out_shape, in_specs=[IN_VMEM, IN_SMEM, IN_...  4.73 us
    pallas_call x1, Pallas kernels, make_codes(): pl.pallas_call(body, out_shape=[jax.ShapeDtypeStruct((tok_rows, span + co...  4.21 us
    pallas_call x2, Pallas kernels, join_heads(): pl.pallas_call(body, out_shape=jax.ShapeDtypeStruct((tok_rows, width * gr...  1.6 us
    pallas_call x1, Pallas kernels, pack_qkv(): pl.pallas_call(body, out_shape=[jax.ShapeDtypeStruct((tok_rows, span), BF...  1.45 us
  transfers between devices with their start and end apart: 12, of which 3 were waited for; matrix products, arithmetic and copies ran while one was open for 0% of the time, Pallas kernels for 29%

commit v1 on v0

--- a/solution.py
+++ b/solution.py
@@ -135,6 +135,11 @@
     return lax.ppermute(values, "seq", [(i, i ^ bits) for i in range(group_size)])
 
 
+def map_partners(partners, parts, group_size):
+    sent = [to_partner(part, bits, group_size) for bits, part in zip(partners, parts)]
+    return sent + list(parts[len(partners) :])
+
+
 def params(mebibytes=40):
     return pltpu.CompilerParams(vmem_limit_bytes=mebibytes * 1024 * 1024)
 
@@ -147,32 +152,34 @@
     return pl.CostEstimate(flops=flops, bytes_accessed=moved, transcendentals=0)
 
 
-def column_copies(shared, outs, sem, width, tiles, group_size):
+def start_columns(shared, outs, sem, width, tiles, wanted):
     me = lax.axis_index("seq")
     span = (tiles[1] - tiles[0]) * LANES
     copies = []
-    for n, bits in enumerate(sends(group_size) + [0]):
+    for n, (bits, kinds) in enumerate(wanted):
         owner = jnp.bitwise_xor(me, bits)
-        for c in range(3):
+        for m, c in enumerate(kinds):
             first = pl.multiple_of(c * HEADS * HD + owner * width + tiles[0] * LANES, LANES)
             copies.append(
                 pltpu.make_async_copy(
                     shared.at[:, pl.ds(first, span)],
-                    outs[n].at[:, pl.ds(c * span, span)],
-                    sem.at[n, c],
+                    outs[n].at[:, pl.ds(m * span, span)],
+                    sem.at[n, m],
                 )
             )
+    for copy in copies:
+        copy.start()
     return copies
 
 
-def make_codes(inputs, adapter_down, shared_qkv, width, tiles, group_size):
+def make_codes(inputs, adapter_down, shared_qkv, after, width, tiles, wanted):
     tok_rows, depth = inputs.shape
     code_width = adapter_down.shape[1]
     steps = 8
     chunk = depth // steps
-    span = 3 * (tiles[1] - tiles[0]) * LANES
-
-    def body(inputs_ref, down_ref, shared, *refs):
+    spans = [len(kinds) * (tiles[1] - tiles[0]) * LANES for _, kinds in wanted]
+
+    def body(inputs_ref, down_ref, shared, _, *refs):
         outs, (held, down, in_sem, down_sem, sem) = refs[:-5], refs[-5:]
         loads = []
         for step in range(steps):
@@ -185,9 +192,7 @@
             )
             for load in loads[-1]:
                 load.start()
-        copies = column_copies(shared, outs, sem, width, tiles, group_size)
-        for copy in copies:
-            copy.start()
+        copies = start_columns(shared, outs, sem, width, tiles, wanted)
         total = None
         for step in range(steps):
             for load in loads[step]:
@@ -196,50 +201,48 @@
             term = jnp.dot(held[:, at], down[at, :], preferred_element_type=F32)
             total = term if total is None else total + term
         own_codes = total.astype(BF16)
-        for out in outs:
+        for out, span in zip(outs, spans):
             out[:, span:] = own_codes
         for copy in copies:
             copy.wait()
 
     return pl.pallas_call(
         body,
-        out_shape=[jax.ShapeDtypeStruct((tok_rows, span + code_width), BF16)] * group_size,
-        in_specs=[IN_HBM, IN_HBM, IN_HBM],
-        out_specs=[IN_VMEM] * group_size,
+        out_shape=[jax.ShapeDtypeStruct((tok_rows, span + code_width), BF16) for span in spans],
+        in_specs=[IN_HBM, IN_HBM, IN_HBM, ANYWHERE],
+        out_specs=[IN_VMEM] * len(wanted),
         scratch_shapes=[
             pltpu.VMEM((tok_rows, depth), BF16),
             pltpu.VMEM((depth, code_width), BF16),
             pltpu.SemaphoreType.DMA((steps,)),
             pltpu.SemaphoreType.DMA((steps,)),
-            pltpu.SemaphoreType.DMA((group_size, 3)),
+            pltpu.SemaphoreType.DMA((len(wanted), 3)),
         ],
         compiler_params=params(20),
         cost_estimate=cost(2 * tok_rows * depth * code_width, depth * code_width * 2),
         name="make_codes",
-    )(stay(inputs), stay(adapter_down), stay(shared_qkv))
-
-
-def pack_qkv(shared_qkv, after, width, tiles, group_size):
+    )(stay(inputs), stay(adapter_down), stay(shared_qkv), after)
+
+
+def pack_qkv(shared_qkv, after, width, tiles, wanted):
     tok_rows = shared_qkv.shape[0]
-    span = 3 * (tiles[1] - tiles[0]) * LANES
-
-    def body(shared, _, *refs):
-        copies = column_copies(shared, refs[:-1], refs[-1], width, tiles, group_size)
-        for copy in copies:
-            copy.start()
-        for copy in copies:
+    spans = [len(kinds) * (tiles[1] - tiles[0]) * LANES for _, kinds in wanted]
+
+    def body(shared, *refs):
+        outs, sem = refs[len(after) : -1], refs[-1]
+        for copy in start_columns(shared, outs, sem, width, tiles, wanted):
             copy.wait()
 
     return pl.pallas_call(
         body,
-        out_shape=[jax.ShapeDtypeStruct((tok_rows, span), BF16)] * group_size,
-        in_specs=[IN_HBM, ANYWHERE],
-        out_specs=[IN_VMEM] * group_size,
-        scratch_shapes=[pltpu.SemaphoreType.DMA((group_size, 3))],
+        out_shape=[jax.ShapeDtypeStruct((tok_rows, span), BF16) for span in spans],
+        in_specs=[IN_HBM] + [ANYWHERE] * len(after),
+        out_specs=[IN_VMEM] * len(wanted),
+        scratch_shapes=[pltpu.SemaphoreType.DMA((len(wanted), 3))],
         compiler_params=params(20),
-        cost_estimate=cost(0, 2 * group_size * tok_rows * span * 2),
+        cost_estimate=cost(0, 2 * tok_rows * sum(spans) * 2),
         name="pack_qkv",
-    )(stay(shared_qkv), after)
+    )(stay(shared_qkv), *after)
 
 
 def head_tiles(h):
@@ -250,7 +253,8 @@
     return jnp.concatenate([ref[tile, rows, :] for tile in window], axis=1)
 
 
-def attend(up, sink_logits, lengths, low_rank, arrived, carried, after, heads, tiles, done_tiles, group_size):
+def attend(up, sink_logits, lengths, low_rank, arrived, places, carried, after, heads, tiles, done_tiles):
+    group_size = len(places)
     tok_rows = arrived[0].shape[0]
     total_rows = tok_rows * group_size
     window_span = total_rows // 2
@@ -270,7 +274,7 @@
         take = lambda n: [refs.pop(0) for _ in range(n)]
         up_ref, sinks, lens = take(3)
         low_refs = take(len(given_low))
-        arrived_refs = take(group_size)
+        arrived_refs = take(len(arrived))
         before = take(len(carried))
         take(len(after))
         outs = take(group_size)
@@ -283,19 +287,19 @@
             for target, source in zip((queries, merged, keys, values), before):
                 target[:kept_tiles] = source[source.shape[0] - kept_tiles :]
         for bits in range(group_size):
-            source = arrived_refs[bits]
             place = pl.ds(pl.multiple_of(jnp.bitwise_xor(me, bits) * tok_rows, tok_rows), tok_rows)
             for c, target in enumerate((queries, keys, values)):
                 if first_call:
-                    at = 3 * span + c * RANK
-                    codes = source[:, at : at + RANK]
+                    which, at = places[bits][3]
+                    codes = arrived_refs[which][:, at + c * RANK : at + (c + 1) * RANK]
                     low = jnp.dot(codes, up_ref[c, :, :span], preferred_element_type=F32)
                     carried_out[0][bits, :, c * rest : (c + 1) * rest] = jnp.dot(
                         codes, up_ref[c, :, span:], preferred_element_type=F32
                     )
                 else:
                     low = low_refs[0][bits, :, c * span : (c + 1) * span]
-                base = source[:, c * span : (c + 1) * span].astype(F32)
+                which, at = places[bits][c]
+                base = arrived_refs[which][:, at : at + span].astype(F32)
                 new = (base + low).astype(BF16)
                 for n in range(tiles[1] - tiles[0]):
                     target[kept_tiles + n, place, :] = new[:, n * LANES : (n + 1) * LANES]
@@ -371,7 +375,7 @@
         body,
         out_shape=out_shape,
         in_specs=[IN_VMEM, IN_SMEM, IN_SMEM]
-        + [IN_VMEM] * (len(given_low) + group_size + len(carried))
+        + [IN_VMEM] * (len(given_low) + len(arrived) + len(carried))
         + [ANYWHERE] * len(after),
         out_specs=[IN_VMEM] * len(out_shape),
         scratch_shapes=[pltpu.VMEM((all_tiles, total_rows, LANES), BF16)] * 2,
@@ -414,26 +418,33 @@
         first = jnp.sum(first, axis=1, keepdims=True)
         count = jnp.sum(count, axis=1, keepdims=True)
         odd = jnp.bitwise_and(lax.broadcasted_iota(jnp.int32, (rows, 1), 0), 1)
-        place = lax.broadcasted_iota(jnp.int32, (rows, total_rows), 1)
+        place = lax.broadcasted_iota(jnp.int32, (4 * rows, total_rows), 1)
         every = (range(keys.shape[0]), slice(None))
         all_keys, all_values = side_by_side(key_ref, *every), side_by_side(value_ref, *every)
-        picked = []
-        for r in range(PAGE):
-            for_keys = jnp.where((odd == 0) & (count > r), first + r, -1)
-            for_values = jnp.where((odd == 1) & (count > r), first + r, -1)
+        copies = []
+        group = 4
+        for r in range(0, PAGE, group):
+            wanted = [jnp.where(count > r + n, first + r + n, -1) for n in range(group)]
+            for_keys = jnp.concatenate([jnp.where(odd == 0, want, -1) for want in wanted], axis=0)
+            for_values = jnp.concatenate([jnp.where(odd == 1, want, -1) for want in wanted], axis=0)
             pick_keys = (place == for_keys).astype(F32).astype(BF16)
             pick_values = (place == for_values).astype(F32).astype(BF16)
-            picked.append(
-                jnp.dot(pick_keys, all_keys, preferred_element_type=F32)
-                + jnp.dot(pick_values, all_values, preferred_element_type=F32)
+            picked = jnp.dot(pick_keys, all_keys, preferred_element_type=F32) + jnp.dot(
+                pick_values, all_values, preferred_element_type=F32
             )
-        copies = []
-        for n, h in enumerate(heads):
-            lo = h * HD - first_tile * LANES
-            line = jnp.concatenate([columns[:, lo : lo + HD] for columns in picked], axis=1)
-            built[n] = line.astype(BF16).reshape(page_count, 2, PAGE * HD)
-            copies.append(pltpu.make_async_copy(built.at[n], out.at[h], sem.at[n]))
-            copies[-1].start()
+            lanes = slice(r * HD, (r + group) * HD)
+            for n, h in enumerate(heads):
+                lo = h * HD - first_tile * LANES
+                line = jnp.concatenate(
+                    [picked[m * rows : (m + 1) * rows, lo : lo + HD] for m in range(group)], axis=1
+                )
+                built[n, :, :, lanes] = line.astype(BF16).reshape(page_count, 2, group * HD)
+                copies.append(
+                    pltpu.make_async_copy(
+                        built.at[n, :, :, lanes], out.at[h, :, :, lanes], sem.at[n, r // group]
+                    )
+                )
+                copies[-1].start()
         for copy in copies:
             copy.wait()
 
@@ -444,7 +455,7 @@
         out_specs=IN_HBM,
         scratch_shapes=[
             pltpu.VMEM((len(heads), page_count, 2, PAGE * HD), BF16),
-            pltpu.SemaphoreType.DMA((len(heads),)),
+            pltpu.SemaphoreType.DMA((len(heads), 4)),
         ],
         input_output_aliases={4: 0} if given else {},
         compiler_params=params(),
@@ -500,10 +511,22 @@
     def send(parts):
         return {bits: to_partner(part, bits, group_size) for bits, part in zip(partners, parts)}
 
-    *parts, own = make_codes(inputs, adapter_down, shared_qkv, width, tiles[0], group_size)
-    arrived = [{0: own, **send(parts)}]
-    *parts, own = pack_qkv(shared_qkv, own, width, tiles[1], group_size)
-    arrived.append({0: own, **send(parts)})
+    every = (0, 1, 2)
+    first, others = partners[0], partners[1:]
+    (early,) = pack_qkv(shared_qkv, [], width, tiles[0], [(first, (0, 1))])
+    wanted = [(bits, every) for bits in others + [0]]
+    parts = make_codes(inputs, adapter_down, shared_qkv, early, width, tiles[0], [(first, (2,))] + wanted)
+    early = to_partner(early, first, group_size)
+    arrived = [[early, *map_partners(partners, parts, group_size)]]
+    parts = pack_qkv(shared_qkv, [parts[-1], early], width, tiles[1], [(first, every)] + wanted)
+    arrived.append(map_partners(partners, parts, group_size))
+    places = []
+    for n in range(2):
+        span = (tiles[n][1] - tiles[n][0]) * LANES
+        columns = (0, span, 2 * span, 3 * span)
+        at = {bits: [(m + 2 - n, column) for column in columns] for m, bits in enumerate(others + [0])}
+        at[first] = [(0, 0), (0, span), (1, 0), (1, span)] if n == 0 else [(0, column) for column in columns]
+        places.append([at[bits] for bits in range(group_size)])
     low_rank, carried, cache, hidden = None, [], None, None
     for n in range(2):
         blocks, keys, values, low_rank, carried = attend(
@@ -511,13 +534,13 @@
             sink_logits,
             lengths,
             low_rank,
-            [arrived[n][bits] for bits in range(group_size)],
+            arrived[n],
+            places[n],
             carried,
             [] if cache is None else [cache],
             heads[n],
             tiles[n],
             done_tiles[n],
-            group_size,
         )
         returned = send([blocks[bits] for bits in partners])
         returned[0] = blocks[0]

time: 59 us -> 55.4 us (0.939)
  Pallas kernels: 22.3 us -> 19.4 us
  waiting for transfers between devices: 16.1 us -> 15.3 us
    pallas_call x2, Pallas kernels: 10.3 us -> 6.54 us  [build_cache(): pl.pallas_call(body, out_shape=jax.ShapeDtypeStruct((heads_local, page_co...]
    pallas_call x1 -> x2, Pallas kernels: 1.45 us -> 2.46 us  [pack_qkv(): pl.pallas_call(body, out_shape=[jax.ShapeDtypeStruct((tok_rows, span), BF...]
    ppermute x12 -> x13, waiting for transfers between devices: 16.1 us -> 15.3 us  [to_partner(): lax.ppermute(values, 'seq', [(i, i ^ bits) for i in range(group_size)])]
    ppermute x12 -> x13, starting transfers between devices: 19.6 us -> 19.8 us  [to_partner(): lax.ppermute(values, 'seq', [(i, i ^ bits) for i in range(group_size)])]
  transfers between devices with their start and end apart: 12 -> 13, of which waited for: 3 -> 3; matrix products, arithmetic and copies ran while one was open for 0% -> 0% of each run, Pallas kernels for 29% -> 32%
where the time goes in v1:
time: 55.4 us; the launch traced here: 55.3 us
  starting transfers between devices  19.8 us (36%)
  Pallas kernels  19.4 us (35%)
  waiting for transfers between devices  15.3 us (28%)
  between operations  0.76 us (1%)
    ppermute x13, starting transfers between devices, to_partner(): lax.ppermute(values, 'seq', [(i, i ^ bits) for i in range(group_size)])  19.8 us
    ppermute x13, waiting for transfers between devices, to_partner(): lax.ppermute(values, 'seq', [(i, i ^ bits) for i in range(group_size)])  15.3 us
    pallas_call x2, Pallas kernels, build_cache(): pl.pallas_call(body, out_shape=jax.ShapeDtypeStruct((heads_local, page_co...  6.54 us
    pallas_call x2, Pallas kernels, attend(): pl.pallas_call(body, out_shape=out_shape, in_specs=[IN_VMEM, IN_SMEM, IN_...  4.73 us
    pallas_call x1, Pallas kernels, make_codes(): pl.pallas_call(body, out_shape=[jax.ShapeDtypeStruct((tok_rows, span + co...  4.11 us
    pallas_call x2, Pallas kernels, pack_qkv(): pl.pallas_call(body, out_shape=[jax.ShapeDtypeStruct((tok_rows, span), BF...  2.46 us
    pallas_call x2, Pallas kernels, join_heads(): pl.pallas_call(body, out_shape=jax.ShapeDtypeStruct((tok_rows, width * gr...  1.59 us
  transfers between devices with their start and end apart: 13, of which 3 were waited for; matrix products, arithmetic and copies ran while one was open for 0% of the time, Pallas kernels for 32%

profile of v1, /device:TPU:0, one launch (start us, length us, event | category | flops | bytes accessed | tf_op | source)
XLA Modules:
  0.0 55.3 jit_solution(8173143209078905546)
XLA Ops:
  0.6 1.0 %pack_qkv.2._ = bf16[128,1024]{1,0:T(8,128)(2,1)S(1)} custom-call(bf16[128,10752]{1,0:T(8,128)(2,1)} %shared.5), custom_call_target="tpu_custom_call" | custom-call | bytes 524288 | tf_op jit(solution)/shard_map/pack_qkv/pallas_call | solution.py:236
  1.6 4.0 %collective-permute-start = (bf16[128,1024]{1,0:T(8,128)(2,1)S(1)}, bf16[128,1024]{1,0:T(8,128)(2,1)S(1)}, u32[]{:S(2)}, u32[]{:S(2)}) collective-permute-start(bf16[128,1024]{1,0:T(8,128)(2,1)S(1)} %pack_qkv.2._), channel_id=1, source_target_pairs={{0,3},{1,2},{2,1},{3,0},{4,7},{5,6},{6,5},{7,4},{8,11},{9,10},{10,... | collective-permute-start | bytes 786440 | tf_op jit(solution)/shard_map/ppermute | solution.py:135
  5.6 4.1 %make_codes.1 = (bf16[128,896]{1,0:T(8,128)(2,1)S(1)}, bf16[128,1920]{1,0:T(8,128)(2,1)S(1)}, bf16[128,1920]{1,0:T(8,128)(2,1)S(1)}, bf16[128,1920]{1,0:T(8,128)(2,1)S(1)}) custom-call(bf16[128,7168]{1,0:T(8,128)(2,1)} %inputs_ref.1, bf16[7168,384]{1,0:T(8,128)(2,1)} %down_ref.1, bf16[128,10752]{1,0:T(8,128)(2,1)} %shared.5, bf16[128,1024]{1,0:T(8,128)(2,1)S(1)} %pack_qkv.2._), custom_call_target="tpu_custom_call" | custom-call | flops 704643072 | bytes 5505024 | tf_op jit(solution)/shard_map/make_codes/pallas_call | solution.py:209
  9.7 0.0 copy-start.3
  9.8 0.6 %collective-permute-start.2 = (bf16[128,1920]{1,0:T(8,128)(2,1)S(1)}, bf16[128,1920]{1,0:T(8,128)(2,1)S(1)}, u32[]{:S(2)}, u32[]{:S(2)}) collective-permute-start(bf16[128,1920]{1,0:T(8,128)(2,1)S(1)} %get-tuple-element.26), channel_id=1, source_target_pairs={{0,1},{1,0},{2,3},{3,2},{4,5},{5,4},{6,7},{7,6},{8,9},{9,8},{10,11... | collective-permute-start | bytes 1474568 | tf_op jit(solution)/shard_map/ppermute | solution.py:135
  10.4 0.1 collective-permute-start.3
  10.4 2.9 %collective-permute-start.1 = (bf16[128,896]{1,0:T(8,128)(2,1)S(1)}, bf16[128,896]{1,0:T(8,128)(2,1)S(1)}, u32[]{:S(2)}, u32[]{:S(2)}) collective-permute-start(bf16[128,896]{1,0:T(8,128)(2,1)S(1)} %get-tuple-element.25), channel_id=1, source_target_pairs={{0,3},{1,2},{2,1},{3,0},{4,7},{5,6},{6,5},{7,4},{8,11},{9,10},{10,... | collective-permute-start | bytes 688136 | tf_op jit(solution)/shard_map/ppermute | solution.py:135
  13.3 1.5 %pack_qkv.3 = (bf16[128,1152]{1,0:T(8,128)(2,1)S(1)}, bf16[128,1152]{1,0:T(8,128)(2,1)S(1)}, bf16[128,1152]{1,0:T(8,128)(2,1)S(1)}, bf16[128,1152]{1,0:T(8,128)(2,1)S(1)}) custom-call(bf16[128,10752]{1,0:T(8,128)(2,1)} %shared.5, bf16[128,1920]{1,0:T(8,128)(2,1)S(1)} %get-tuple-element.28.refs_7_.refs_0_, ...), custom_call_target="tpu_custom_call" | custom-call | bytes 2359296 | tf_op jit(solution)/shard_map/pack_qkv/pallas_call | solution.py:236
  14.8 2.4 %collective-permute-start.4 = (bf16[128,1152]{1,0:T(8,128)(2,1)S(1)}, bf16[128,1152]{1,0:T(8,128)(2,1)S(1)}, u32[]{:S(2)}, u32[]{:S(2)}) collective-permute-start(bf16[128,1152]{1,0:T(8,128)(2,1)S(1)} %get-tuple-element.30), channel_id=1, source_target_pairs={{0,3},{1,2},{2,1},{3,0},{4,7},{5,6},{6,5},{7,4},{8,11},{9,10},{10,... | collective-permute-start | bytes 884744 | tf_op jit(solution)/shard_map/ppermute | solution.py:135
  17.2 11.8 %collective-permute-done.1.refs_4_ = bf16[128,896]{1,0:T(8,128)(2,1)S(1)} collective-permute-done((bf16[128,896]{1,0:T(8,128)(2,1)S(1)}, bf16[128,896]{1,0:T(8,128)(2,1)S(1)}, u32[]{:S(2)}, u32[]{:S(2)}) %collective-permute-start.1) | collective-permute-done | bytes 229408 | tf_op jit(solution)/shard_map/ppermute | solution.py:135
  28.9 1.4 %collective-permute-start.6 = (bf16[128,1152]{1,0:T(8,128)(2,1)S(1)}, bf16[128,1152]{1,0:T(8,128)(2,1)S(1)}, u32[]{:S(2)}, u32[]{:S(2)}) collective-permute-start(bf16[128,1152]{1,0:T(8,128)(2,1)S(1)} %get-tuple-element.32), channel_id=1, source_target_pairs={{0,2},{1,3},{2,0},{3,1},{4,6},{5,7},{6,4},{7,5},{8,10},{9,11},{10,... | collective-permute-start | bytes 884744 | tf_op jit(solution)/shard_map/ppermute | solution.py:135
  30.3 2.7 %collective-permute-done.3.refs_6_ = bf16[128,1920]{1,0:T(8,128)(2,1)S(1)} collective-permute-done((bf16[128,1920]{1,0:T(8,128)(2,1)S(1)}, bf16[128,1920]{1,0:T(8,128)(2,1)S(1)}, u32[]{:S(2)}, u32[]{:S(2)}) %collective-permute-start.3) | collective-permute-done | bytes 491552 | tf_op jit(solution)/shard_map/ppermute | solution.py:135
  33.1 2.7 %attend.2 = (bf16[128,384]{1,0:T(8,128)(2,1)S(1)}, bf16[128,384]{1,0:T(8,128)(2,1)S(1)}, bf16[128,384]{1,0:T(8,128)(2,1)S(1)}, bf16[128,384]{1,0:T(8,128)(2,1)S(...) custom-call(bf16[3,128,896]{2,1,0:T(8,128)(2,1)S(1)} %copy-done, ...), custom_call_target="tpu_custom_call" | custom-call | flops 536870912 | bytes 4194304 | tf_op jit(solution)/shard_map/attend/pallas_call | solution.py:374
  35.8 3.4 %collective-permute-start.10 = (bf16[128,384]{1,0:T(8,128)(2,1)S(1)}, bf16[128,384]{1,0:T(8,128)(2,1)S(1)}, u32[]{:S(2)}, u32[]{:S(2)}) collective-permute-start(bf16[128,384]{1,0:T(8,128)(2,1)S(1)} %get-tuple-element.43), channel_id=1, source_target_pairs={{0,1},{1,0},{2,3},{3,2},{4,5},{5,4},{6,7},{7,6},{8,9},{9,8},{10,11... | collective-permute-start | bytes 294920 | tf_op jit(solution)/shard_map/ppermute | solution.py:135
  39.1 1.5 %collective-permute-start.12 = (bf16[128,384]{1,0:T(8,128)(2,1)S(1)}, bf16[128,384]{1,0:T(8,128)(2,1)S(1)}, u32[]{:S(2)}, u32[]{:S(2)}) collective-permute-start(bf16[128,384]{1,0:T(8,128)(2,1)S(1)} %get-tuple-element.45), channel_id=1, source_target_pairs={{0,3},{1,2},{2,1},{3,0},{4,7},{5,6},{6,5},{7,4},{8,11},{9,10},{10,... | collective-permute-start | bytes 294920 | tf_op jit(solution)/shard_map/ppermute | solution.py:135
  40.7 3.3 %build_cache.2.refs_12_.refs_4_ = bf16[4,40,2,3584]{3,2,1,0:T(2,128)(2,1)} custom-call(bf16[4,512,128]{2,1,0:T(8,128)(2,1)S(1)} %get-tuple-element.36.refs_0_.refs_10_, bf16[4,512,128]{2,1,0:T(8,128)(2,1)S(1)} %get-tuple-element.37.refs_1_.refs_11_, s32[8]{0:T(128)S(1)} %copy-done.1, s32[8,24]{1,0:T(8,128)S(1)} %copy-done.2), custom_call_target="tpu_custom_call" | custom-call | flops 1342177280 | bytes 2097152 | tf_op jit(solution)/shard_map/build_cache/pallas_call | solution.py:451
  44.0 2.1 %attend.3 = (bf16[128,512]{1,0:T(8,128)(2,1)S(1)}, bf16[128,512]{1,0:T(8,128)(2,1)S(1)}, bf16[128,512]{1,0:T(8,128)(2,1)S(1)}, bf16[128,512]{1,0:T(8,128)(2,1)S(...) custom-call(bf16[3,128,896]{2,1,0:T(8,128)(2,1)S(1)} %copy-done, f32[4]{0:T(128)S(1)} %copy-done.3, ...), custom_call_target="tpu_custom_call" | custom-call | flops 402653184 | bytes 3145728 | tf_op jit(solution)/shard_map/attend/pallas_call | solution.py:374
  46.0 2.0 %collective-permute-start.7 = (bf16[128,512]{1,0:T(8,128)(2,1)S(1)}, bf16[128,512]{1,0:T(8,128)(2,1)S(1)}, u32[]{:S(2)}, u32[]{:S(2)}) collective-permute-start(bf16[128,512]{1,0:T(8,128)(2,1)S(1)} %get-tuple-element.39), channel_id=1, source_target_pairs={{0,1},{1,0},{2,3},{3,2},{4,5},{5,4},{6,7},{7,6},{8,9},{9,8},{10,11... | collective-permute-start | bytes 393224 | tf_op jit(solution)/shard_map/ppermute | solution.py:135
  48.1 0.0 collective-permute-start.8
  48.1 1.5 %collective-permute-start.9 = (bf16[128,512]{1,0:T(8,128)(2,1)S(1)}, bf16[128,512]{1,0:T(8,128)(2,1)S(1)}, u32[]{:S(2)}, u32[]{:S(2)}) collective-permute-start(bf16[128,512]{1,0:T(8,128)(2,1)S(1)} %get-tuple-element.41), channel_id=1, source_target_pairs={{0,3},{1,2},{2,1},{3,0},{4,7},{5,6},{6,5},{7,4},{8,11},{9,10},{10,... | collective-permute-start | bytes 393224 | tf_op jit(solution)/shard_map/ppermute | solution.py:135
  49.6 0.8 %join_heads.2.refs_4_.refs_5_ = bf16[128,3584]{1,0:T(8,128)(2,1)} custom-call(bf16[128,384]{1,0:T(8,128)(2,1)S(1)} %get-tuple-element.42.refs_0_, bf16[128,384]{1,0:T(8,128)(2,1)S(1)} %collective-permute-done.10.refs_1_, bf16[128,384]{1,0:T(8,128)(2,1)S(1)} %collective-permute-done.11.refs_2_, bf16[128,384]{1,0:T(8,128)(2,1)S(1)} %collective-permute-done.12.refs_3_), custom_call_target="tpu_custom_call" | custom-call | bytes 786432 | tf_op jit(solution)/shard_map/join_heads/pallas_call | solution.py:485
  50.4 3.3 %build_cache.3 = bf16[4,40,2,3584]{3,2,1,0:T(2,128)(2,1)} custom-call(bf16[4,512,128]{2,1,0:T(8,128)(2,1)S(1)} %get-tuple-element.46.refs_0_, bf16[4,512,128]{2,1,0:T(8,128)(2,1)S(1)} %get-tuple-element.47.refs_1_, s32[8]{0:T(128)S(1)} %copy-done.1, s32[8,24]{1,0:T(8,128)S(1)} %copy-done.2, ...), custom_call_target="tpu_custom_call", output_to_operand_aliasing={{}: (4, {})} | custom-call | flops 1342177280 | bytes 2097152 | tf_op jit(solution)/shard_map/build_cache/pallas_call | solution.py:451
  53.7 0.7 %collective-permute-done.8.refs_2_ = bf16[128,512]{1,0:T(8,128)(2,1)S(1)} collective-permute-done((bf16[128,512]{1,0:T(8,128)(2,1)S(1)}, bf16[128,512]{1,0:T(8,128)(2,1)S(1)}, u32[]{:S(2)}, u32[]{:S(2)}) %collective-permute-start.8) | collective-permute-done | bytes 131104 | tf_op jit(solution)/shard_map/ppermute | solution.py:135
  54.4 0.8 %join_heads.3 = bf16[128,3584]{1,0:T(8,128)(2,1)} custom-call(bf16[128,512]{1,0:T(8,128)(2,1)S(1)} %get-tuple-element.38.refs_0_, bf16[128,512]{1,0:T(8,128)(2,1)S(1)} %collective-permute-done.7.refs_1_, bf16[128,512]{1,0:T(8,128)(2,1)S(1)} %collective-permute-done.8.refs_2_, ...), custom_call_target="tpu_custom_call", output_to_operand_aliasing={{}: (4, {})} | custom-call | bytes 1048576 | tf_op jit(solution)/shard_map/join_heads/pallas_call | solution.py:485
  (19 shorter events, 0.1 us)
Async XLA Ops:
  1.6 11.7 %collective-permute-start = (bf16[128,1024]{1,0:T(8,128)(2,1)S(1)}, bf16[128,1024]{1,0:T(8,128)(2,1)S(1)}, u32[]{:S(2)}, u32[]{:S(2)}) collective-permute-start(bf16[128,1024]{1,0:T(8,128)(2,1)S(1)} %pack_qkv.2._), channel_id=1, source_target_pairs={{0,3},{1,2},{2,1},{3,0},{4,7},{5,6},{6,5},{7,4},{8,11},{9,10},{10,... | collective-permute-start | bytes 786440 | tf_op jit(solution)/shard_map/ppermute | solution.py:135
  9.7 23.4 %copy-start = (bf16[3,128,896]{2,1,0:T(8,128)(2,1)S(1)}, bf16[3,128,896]{2,1,0:T(8,128)(2,1)}, u32[]{:S(2)}) copy-start(bf16[3,128,896]{2,1,0:T(8,128)(2,1)} %refs_0_.3) | copy-start | bytes 2064388
  9.7 23.4 %copy-start.1 = (s32[8]{0:T(128)S(1)}, s32[8]{0:T(128)}, u32[]{:S(2)}) copy-start(s32[8]{0:T(128)} %refs_2_.7) | copy-start | bytes 100
  9.7 23.4 %copy-start.3 = (f32[4]{0:T(128)S(1)}, f32[4]{0:T(128)}, u32[]{:S(2)}) copy-start(f32[4]{0:T(128)} %refs_1_.3) | copy-start | bytes 52
  9.8 20.6 %collective-permute-start.2 = (bf16[128,1920]{1,0:T(8,128)(2,1)S(1)}, bf16[128,1920]{1,0:T(8,128)(2,1)S(1)}, u32[]{:S(2)}, u32[]{:S(2)}) collective-permute-start(bf16[128,1920]{1,0:T(8,128)(2,1)S(1)} %get-tuple-element.26), channel_id=1, source_target_pairs={{0,1},{1,0},{2,3},{3,2},{4,5},{5,4},{6,7},{7,6},{8,9},{9,8},{10,11... | collective-permute-start | bytes 1474568 | tf_op jit(solution)/shard_map/ppermute | solution.py:135
  10.4 22.7 %collective-permute-start.3 = (bf16[128,1920]{1,0:T(8,128)(2,1)S(1)}, bf16[128,1920]{1,0:T(8,128)(2,1)S(1)}, u32[]{:S(2)}, u32[]{:S(2)}) collective-permute-start(bf16[128,1920]{1,0:T(8,128)(2,1)S(1)} %get-tuple-element.27), channel_id=1, source_target_pairs={{0,2},{1,3},{2,0},{3,1},{4,6},{5,7},{6,4},{7,5},{8,10},{9,11},{10,... | collective-permute-start | bytes 1474568 | tf_op jit(solution)/shard_map/ppermute | solution.py:135
  10.4 18.5 %collective-permute-start.1 = (bf16[128,896]{1,0:T(8,128)(2,1)S(1)}, bf16[128,896]{1,0:T(8,128)(2,1)S(1)}, u32[]{:S(2)}, u32[]{:S(2)}) collective-permute-start(bf16[128,896]{1,0:T(8,128)(2,1)S(1)} %get-tuple-element.25), channel_id=1, source_target_pairs={{0,3},{1,2},{2,1},{3,0},{4,7},{5,6},{6,5},{7,4},{8,11},{9,10},{10,... | collective-permute-start | bytes 688136 | tf_op jit(solution)/shard_map/ppermute | solution.py:135
  13.3 27.4 %copy-start.2 = (s32[8,24]{1,0:T(8,128)S(1)}, s32[8,24]{1,0:T(8,128)}, u32[]{:S(2)}) copy-start(s32[8,24]{1,0:T(8,128)} %refs_3_.3) | copy-start | bytes 2308
  14.8 24.4 %collective-permute-start.4 = (bf16[128,1152]{1,0:T(8,128)(2,1)S(1)}, bf16[128,1152]{1,0:T(8,128)(2,1)S(1)}, u32[]{:S(2)}, u32[]{:S(2)}) collective-permute-start(bf16[128,1152]{1,0:T(8,128)(2,1)S(1)} %get-tuple-element.30), channel_id=1, source_target_pairs={{0,3},{1,2},{2,1},{3,0},{4,7},{5,6},{6,5},{7,4},{8,11},{9,10},{10,... | collective-permute-start | bytes 884744 | tf_op jit(solution)/shard_map/ppermute | solution.py:135
  17.2 26.8 %collective-permute-start.5 = (bf16[128,1152]{1,0:T(8,128)(2,1)S(1)}, bf16[128,1152]{1,0:T(8,128)(2,1)S(1)}, u32[]{:S(2)}, u32[]{:S(2)}) collective-permute-start(bf16[128,1152]{1,0:T(8,128)(2,1)S(1)} %get-tuple-element.31), channel_id=1, source_target_pairs={{0,1},{1,0},{2,3},{3,2},{4,5},{5,4},{6,7},{7,6},{8,9},{9,8},{10,11... | collective-permute-start | bytes 884744 | tf_op jit(solution)/shard_map/ppermute | solution.py:135
  28.9 15.0 %collective-permute-start.6 = (bf16[128,1152]{1,0:T(8,128)(2,1)S(1)}, bf16[128,1152]{1,0:T(8,128)(2,1)S(1)}, u32[]{:S(2)}, u32[]{:S(2)}) collective-permute-start(bf16[128,1152]{1,0:T(8,128)(2,1)S(1)} %get-tuple-element.32), channel_id=1, source_target_pairs={{0,2},{1,3},{2,0},{3,1},{4,6},{5,7},{6,4},{7,5},{8,10},{9,11},{10,... | collective-permute-start | bytes 884744 | tf_op jit(solution)/shard_map/ppermute | solution.py:135
  35.8 12.3 %collective-permute-start.10 = (bf16[128,384]{1,0:T(8,128)(2,1)S(1)}, bf16[128,384]{1,0:T(8,128)(2,1)S(1)}, u32[]{:S(2)}, u32[]{:S(2)}) collective-permute-start(bf16[128,384]{1,0:T(8,128)(2,1)S(1)} %get-tuple-element.43), channel_id=1, source_target_pairs={{0,1},{1,0},{2,3},{3,2},{4,5},{5,4},{6,7},{7,6},{8,9},{9,8},{10,11... | collective-permute-start | bytes 294920 | tf_op jit(solution)/shard_map/ppermute | solution.py:135
  39.1 10.5 %collective-permute-start.11 = (bf16[128,384]{1,0:T(8,128)(2,1)S(1)}, bf16[128,384]{1,0:T(8,128)(2,1)S(1)}, u32[]{:S(2)}, u32[]{:S(2)}) collective-permute-start(bf16[128,384]{1,0:T(8,128)(2,1)S(1)} %get-tuple-element.44), channel_id=1, source_target_pairs={{0,2},{1,3},{2,0},{3,1},{4,6},{5,7},{6,4},{7,5},{8,10},{9,11},{10,... | collective-permute-start | bytes 294920 | tf_op jit(solution)/shard_map/ppermute | solution.py:135
  39.1 10.5 %collective-permute-start.12 = (bf16[128,384]{1,0:T(8,128)(2,1)S(1)}, bf16[128,384]{1,0:T(8,128)(2,1)S(1)}, u32[]{:S(2)}, u32[]{:S(2)}) collective-permute-start(bf16[128,384]{1,0:T(8,128)(2,1)S(1)} %get-tuple-element.45), channel_id=1, source_target_pairs={{0,3},{1,2},{2,1},{3,0},{4,7},{5,6},{6,5},{7,4},{8,11},{9,10},{10,... | collective-permute-start | bytes 294920 | tf_op jit(solution)/shard_map/ppermute | solution.py:135
  46.0 7.6 %collective-permute-start.7 = (bf16[128,512]{1,0:T(8,128)(2,1)S(1)}, bf16[128,512]{1,0:T(8,128)(2,1)S(1)}, u32[]{:S(2)}, u32[]{:S(2)}) collective-permute-start(bf16[128,512]{1,0:T(8,128)(2,1)S(1)} %get-tuple-element.39), channel_id=1, source_target_pairs={{0,1},{1,0},{2,3},{3,2},{4,5},{5,4},{6,7},{7,6},{8,9},{9,8},{10,11... | collective-permute-start | bytes 393224 | tf_op jit(solution)/shard_map/ppermute | solution.py:135
  48.1 6.4 %collective-permute-start.8 = (bf16[128,512]{1,0:T(8,128)(2,1)S(1)}, bf16[128,512]{1,0:T(8,128)(2,1)S(1)}, u32[]{:S(2)}, u32[]{:S(2)}) collective-permute-start(bf16[128,512]{1,0:T(8,128)(2,1)S(1)} %get-tuple-element.40), channel_id=1, source_target_pairs={{0,2},{1,3},{2,0},{3,1},{4,6},{5,7},{6,4},{7,5},{8,10},{9,11},{10,... | collective-permute-start | bytes 393224 | tf_op jit(solution)/shard_map/ppermute | solution.py:135
  48.1 6.3 %collective-permute-start.9 = (bf16[128,512]{1,0:T(8,128)(2,1)S(1)}, bf16[128,512]{1,0:T(8,128)(2,1)S(1)}, u32[]{:S(2)}, u32[]{:S(2)}) collective-permute-start(bf16[128,512]{1,0:T(8,128)(2,1)S(1)} %get-tuple-element.41), channel_id=1, source_target_pairs={{0,3},{1,2},{2,1},{3,0},{4,7},{5,6},{6,5},{7,4},{8,11},{9,10},{10,... | collective-permute-start | bytes 393224 | tf_op jit(solution)/shard_map/ppermute | solution.py:135

commit v2 on v1

--- a/solution.py
+++ b/solution.py
@@ -152,11 +152,11 @@
     return pl.CostEstimate(flops=flops, bytes_accessed=moved, transcendentals=0)
 
 
-def start_columns(shared, outs, sem, width, tiles, wanted):
+def start_columns(shared, outs, sem, width, wanted):
     me = lax.axis_index("seq")
-    span = (tiles[1] - tiles[0]) * LANES
     copies = []
-    for n, (bits, kinds) in enumerate(wanted):
+    for n, (bits, kinds, tiles) in enumerate(wanted):
+        span = (tiles[1] - tiles[0]) * LANES
         owner = jnp.bitwise_xor(me, bits)
         for m, c in enumerate(kinds):
             first = pl.multiple_of(c * HEADS * HD + owner * width + tiles[0] * LANES, LANES)
@@ -172,12 +172,12 @@
     return copies
 
 
-def make_codes(inputs, adapter_down, shared_qkv, after, width, tiles, wanted):
+def make_codes(inputs, adapter_down, shared_qkv, after, width, wanted):
     tok_rows, depth = inputs.shape
     code_width = adapter_down.shape[1]
     steps = 8
     chunk = depth // steps
-    spans = [len(kinds) * (tiles[1] - tiles[0]) * LANES for _, kinds in wanted]
+    spans = [len(kinds) * (tiles[1] - tiles[0]) * LANES for _, kinds, tiles in wanted]
 
     def body(inputs_ref, down_ref, shared, _, *refs):
         outs, (held, down, in_sem, down_sem, sem) = refs[:-5], refs[-5:]
@@ -192,7 +192,7 @@
             )
             for load in loads[-1]:
                 load.start()
-        copies = start_columns(shared, outs, sem, width, tiles, wanted)
+        copies = start_columns(shared, outs, sem, width, wanted)
         total = None
         for step in range(steps):
             for load in loads[step]:
@@ -224,13 +224,13 @@
     )(stay(inputs), stay(adapter_down), stay(shared_qkv), after)
 
 
-def pack_qkv(shared_qkv, after, width, tiles, wanted):
+def pack_qkv(shared_qkv, after, width, wanted):
     tok_rows = shared_qkv.shape[0]
-    spans = [len(kinds) * (tiles[1] - tiles[0]) * LANES for _, kinds in wanted]
+    spans = [len(kinds) * (tiles[1] - tiles[0]) * LANES for _, kinds, tiles in wanted]
 
     def body(shared, *refs):
         outs, sem = refs[len(after) : -1], refs[-1]
-        for copy in start_columns(shared, outs, sem, width, tiles, wanted):
+        for copy in start_columns(shared, outs, sem, width, wanted):
             copy.wait()
 
     return pl.pallas_call(
@@ -253,7 +253,7 @@
     return jnp.concatenate([ref[tile, rows, :] for tile in window], axis=1)
 
 
-def attend(up, sink_logits, lengths, low_rank, arrived, places, carried, after, heads, tiles, done_tiles):
+def attend(up, sink_logits, lengths, low_rank, arrived, places, carried, heads, tiles, done_tiles):
     group_size = len(places)
     tok_rows = arrived[0].shape[0]
     total_rows = tok_rows * group_size
@@ -276,7 +276,6 @@
         low_refs = take(len(given_low))
         arrived_refs = take(len(arrived))
         before = take(len(carried))
-        take(len(after))
         outs = take(group_size)
         keys, values = take(2)
         carried_out = take(0 if last else 3)
@@ -375,14 +374,13 @@
         body,
         out_shape=out_shape,
         in_specs=[IN_VMEM, IN_SMEM, IN_SMEM]
-        + [IN_VMEM] * (len(given_low) + len(arrived) + len(carried))
-        + [ANYWHERE] * len(after),
+        + [IN_VMEM] * (len(given_low) + len(arrived) + len(carried)),
         out_specs=[IN_VMEM] * len(out_shape),
         scratch_shapes=[pltpu.VMEM((all_tiles, total_rows, LANES), BF16)] * 2,
         compiler_params=params(),
         cost_estimate=cost(4 * total_rows * total_rows * span, 8 * total_rows * span * 2),
         name="attend",
-    )(up, sink_logits, lengths, *given_low, *arrived, *carried, *map(stay, after))
+    )(up, sink_logits, lengths, *given_low, *arrived, *carried)
     blocks, (keys, values) = results[:group_size], results[group_size : group_size + 2]
     if last:
         return blocks, keys, values, None, []
@@ -390,19 +388,19 @@
     return blocks, keys, values, next_low, [*leftovers, keys, values]
 
 
-def build_cache(cache, after, keys, values, first_tile, lengths, block_table, heads, heads_local):
-    total_rows, width = keys.shape[1], keys.shape[0] * LANES
+def build_cache(keys, values, starts, lengths, block_table):
+    total_rows = keys[0].shape[1]
+    parts = len(keys)
+    width = sum(part.shape[0] - start for part, start in zip(keys, starts)) * LANES
+    heads_local = width // HD
     page_count = total_rows // PAGE + SEGS
     blocks = block_table.shape[1]
     rows = 2 * page_count
-    given = [] if cache is None else [cache]
+    group = 4
 
     def body(*refs):
-        refs = list(refs)
-        take = lambda n: [refs.pop(0) for _ in range(n)]
-        key_ref, value_ref, lens, table = take(4)
-        take(len(given) + len(after))
-        out, built, sem = take(3)
+        key_refs, value_refs = refs[:parts], refs[parts : 2 * parts]
+        lens, table, out, built, sem = refs[2 * parts :]
         row = lax.broadcasted_iota(jnp.int32, (rows, blocks), 0)
         page = lax.shift_right_logical(row, 1)
         block = lax.broadcasted_iota(jnp.int32, (rows, blocks), 1)
@@ -418,11 +416,14 @@
         first = jnp.sum(first, axis=1, keepdims=True)
         count = jnp.sum(count, axis=1, keepdims=True)
         odd = jnp.bitwise_and(lax.broadcasted_iota(jnp.int32, (rows, 1), 0), 1)
-        place = lax.broadcasted_iota(jnp.int32, (4 * rows, total_rows), 1)
-        every = (range(keys.shape[0]), slice(None))
-        all_keys, all_values = side_by_side(key_ref, *every), side_by_side(value_ref, *every)
+        place = lax.broadcasted_iota(jnp.int32, (group * rows, total_rows), 1)
+
+        def columns(part_refs):
+            every = [(ref, tile) for ref, low in zip(part_refs, starts) for tile in range(low, ref.shape[0])]
+            return jnp.concatenate([ref[tile] for ref, tile in every], axis=1)
+
+        all_keys, all_values = columns(key_refs), columns(value_refs)
         copies = []
-        group = 4
         for r in range(0, PAGE, group):
             wanted = [jnp.where(count > r + n, first + r + n, -1) for n in range(group)]
             for_keys = jnp.concatenate([jnp.where(odd == 0, want, -1) for want in wanted], axis=0)
@@ -433,50 +434,53 @@
                 pick_values, all_values, preferred_element_type=F32
             )
             lanes = slice(r * HD, (r + group) * HD)
-            for n, h in enumerate(heads):
-                lo = h * HD - first_tile * LANES
+            for h in range(heads_local):
                 line = jnp.concatenate(
-                    [picked[m * rows : (m + 1) * rows, lo : lo + HD] for m in range(group)], axis=1
-                )
-                built[n, :, :, lanes] = line.astype(BF16).reshape(page_count, 2, group * HD)
+                    [picked[m * rows : (m + 1) * rows, h * HD : (h + 1) * HD] for m in range(group)], axis=1
+                )
+                built[h, :, :, lanes] = line.astype(BF16).reshape(page_count, 2, group * HD)
                 copies.append(
                     pltpu.make_async_copy(
-                        built.at[n, :, :, lanes], out.at[h, :, :, lanes], sem.at[n, r // group]
+                        built.at[h, :, :, lanes], out.at[h, :, :, lanes], sem.at[h, r // group]
                     )
                 )
                 copies[-1].start()
         for copy in copies:
             copy.wait()
 
+    cache = (heads_local, page_count, 2, PAGE * HD)
     return pl.pallas_call(
         body,
-        out_shape=jax.ShapeDtypeStruct((heads_local, page_count, 2, PAGE * HD), BF16),
-        in_specs=[IN_VMEM, IN_VMEM, IN_SMEM, IN_VMEM] + [IN_HBM] * len(given) + [ANYWHERE] * len(after),
+        out_shape=jax.ShapeDtypeStruct(cache, BF16),
+        in_specs=[IN_VMEM] * (2 * parts) + [IN_SMEM, IN_VMEM],
         out_specs=IN_HBM,
-        scratch_shapes=[
-            pltpu.VMEM((len(heads), page_count, 2, PAGE * HD), BF16),
-            pltpu.SemaphoreType.DMA((len(heads), 4)),
-        ],
-        input_output_aliases={4: 0} if given else {},
+        scratch_shapes=[pltpu.VMEM(cache, BF16), pltpu.SemaphoreType.DMA((heads_local, PAGE // group))],
         compiler_params=params(),
         cost_estimate=cost(4 * rows * PAGE * total_rows * width, 4 * total_rows * width * 2),
         name="build_cache",
-    )(keys, values, lengths, block_table, *map(stay, given), *map(stay, after))
-
-
-def join_heads(hidden, blocks, first_column, width, group_size):
-    tok_rows, span = blocks[0].shape
-    given = [] if hidden is None else [hidden]
+    )(*keys, *values, lengths, block_table)
+
+
+def join_heads(parts, group_size):
+    tok_rows = parts[0][0].shape[0]
+    width = sum(blocks[0].shape[1] for blocks in parts)
+    sources = [block for blocks in parts for block in blocks]
 
     def body(*refs):
-        sources, out, sem = refs[:group_size], refs[-2], refs[-1]
+        out, sem = refs[-2:]
         me = lax.axis_index("seq")
         copies = []
-        for bits in range(group_size):
-            first = pl.multiple_of(jnp.bitwise_xor(me, bits) * width + first_column, LANES)
-            copies.append(
-                pltpu.make_async_copy(sources[bits], out.at[:, pl.ds(first, span)], sem.at[bits])
-            )
+        begin = 0
+        for n, blocks in enumerate(parts):
+            span = blocks[0].shape[1]
+            for bits in range(group_size):
+                first = pl.multiple_of(jnp.bitwise_xor(me, bits) * width + begin, LANES)
+                copies.append(
+                    pltpu.make_async_copy(
+                        refs[n * group_size + bits], out.at[:, pl.ds(first, span)], sem.at[n, bits]
+                    )
+                )
+            begin += span
         for copy in copies:
             copy.start()
         for copy in copies:
@@ -485,14 +489,13 @@
     return pl.pallas_call(
         body,
         out_shape=jax.ShapeDtypeStruct((tok_rows, width * group_size), BF16),
-        in_specs=[ANYWHERE] * group_size + [IN_HBM] * len(given),
+        in_specs=[ANYWHERE] * len(sources),
         out_specs=IN_HBM,
-        scratch_shapes=[pltpu.SemaphoreType.DMA((group_size,))],
-        input_output_aliases={group_size: 0} if given else {},
+        scratch_shapes=[pltpu.SemaphoreType.DMA((len(parts), group_size))],
         compiler_params=params(),
-        cost_estimate=cost(0, 2 * tok_rows * span * group_size * 2),
+        cost_estimate=cost(0, 2 * tok_rows * width * group_size * 2),
         name="join_heads",
-    )(*blocks, *map(stay, given))
+    )(*sources)
 
 
 def per_device_tiled(inputs, adapter_down, adapter_up, shared_qkv, sink_logits, lengths, block_table):
@@ -508,28 +511,28 @@
     done_tiles = [(0, done_cut), (done_cut, all_tiles)]
     heads = [tuple(range(half)), tuple(range(half, heads_local))]
 
-    def send(parts):
-        return {bits: to_partner(part, bits, group_size) for bits, part in zip(partners, parts)}
-
     every = (0, 1, 2)
     first, others = partners[0], partners[1:]
-    (early,) = pack_qkv(shared_qkv, [], width, tiles[0], [(first, (0, 1))])
-    wanted = [(bits, every) for bits in others + [0]]
-    parts = make_codes(inputs, adapter_down, shared_qkv, early, width, tiles[0], [(first, (2,))] + wanted)
+    whole = (0, all_tiles)
+    (early,) = pack_qkv(shared_qkv, [], width, [(first, (0, 1), whole)])
+    wanted = [(bits, every, tiles[0]) for bits in others + [0]]
+    parts = make_codes(inputs, adapter_down, shared_qkv, early, width, [(first, (2,), whole)] + wanted)
     early = to_partner(early, first, group_size)
-    arrived = [[early, *map_partners(partners, parts, group_size)]]
-    parts = pack_qkv(shared_qkv, [parts[-1], early], width, tiles[1], [(first, every)] + wanted)
-    arrived.append(map_partners(partners, parts, group_size))
+    parts = map_partners(partners, parts, group_size)
+    arrived = [[early, *parts]]
+    wanted = [(bits, every, tiles[1]) for bits in others + [0]]
+    later = pack_qkv(shared_qkv, [parts[-1], early], width, wanted)
+    arrived.append([early, parts[0], *map_partners(others, later, group_size)])
     places = []
     for n in range(2):
         span = (tiles[n][1] - tiles[n][0]) * LANES
-        columns = (0, span, 2 * span, 3 * span)
-        at = {bits: [(m + 2 - n, column) for column in columns] for m, bits in enumerate(others + [0])}
-        at[first] = [(0, 0), (0, span), (1, 0), (1, span)] if n == 0 else [(0, column) for column in columns]
+        at = {bits: [(m + 2, c * span) for c in range(4)] for m, bits in enumerate(others + [0])}
+        begin = tiles[n][0] * LANES
+        at[first] = [(0, begin), (0, width + begin), (1, begin), (1, width)]
         places.append([at[bits] for bits in range(group_size)])
-    low_rank, carried, cache, hidden = None, [], None, None
+    low_rank, carried, hidden, keys, values = None, [], [], [], []
     for n in range(2):
-        blocks, keys, values, low_rank, carried = attend(
+        blocks, new_keys, new_values, low_rank, carried = attend(
             adapter_up,
             sink_logits,
             lengths,
@@ -537,28 +540,16 @@
             arrived[n],
             places[n],
             carried,
-            [] if cache is None else [cache],
             heads[n],
             tiles[n],
             done_tiles[n],
         )
-        returned = send([blocks[bits] for bits in partners])
-        returned[0] = blocks[0]
-        cache = build_cache(
-            cache,
-            [] if hidden is None else [hidden],
-            keys,
-            values,
-            done_tiles[n][0],
-            lengths,
-            block_table,
-            heads[n],
-            heads_local,
-        )
-        hidden = join_heads(
-            hidden, [returned[bits] for bits in range(group_size)], done_tiles[n][0] * LANES, width, group_size
-        )
-    return (hidden, cache)
+        returned = {bits: to_partner(blocks[bits], bits, group_size) for bits in partners}
+        hidden.append([blocks[0]] + [returned[bits] for bits in range(1, group_size)])
+        keys, values = keys + [new_keys], values + [new_values]
+    starts = [0, cut - done_cut]
+    cache = build_cache(keys, values, starts, lengths, block_table)
+    return (join_heads(hidden, group_size), cache)
 
 
 def per_device(inputs, adapter_down, adapter_up, shared_qkv, sink_logits, lengths, block_table):

time: 55.4 us -> 53.9 us (0.973)
  waiting for transfers between devices: 15.3 us -> 17.6 us
  Pallas kernels: 19.4 us -> 17.1 us
  starting transfers between devices: 19.8 us -> 18.3 us
    ppermute x13 -> x12, waiting for transfers between devices: 15.3 us -> 17.6 us  [to_partner(): lax.ppermute(values, 'seq', [(i, i ^ bits) for i in range(group_size)])]
    pallas_call x2 -> x1, Pallas kernels: 6.54 us -> 4.84 us  [build_cache(): pl.pallas_call(body, out_shape=jax.ShapeDtypeStruct(cache, BF16), in_spec...]
    ppermute x13 -> x12, starting transfers between devices: 19.8 us -> 18.3 us  [to_partner(): lax.ppermute(values, 'seq', [(i, i ^ bits) for i in range(group_size)])]
    pallas_call x2 -> x1, Pallas kernels: 1.59 us -> 0.98 us  [join_heads(): pl.pallas_call(body, out_shape=jax.ShapeDtypeStruct((tok_rows, width * gr...]
  transfers between devices with their start and end apart: 13 -> 12, of which waited for: 3 -> 4; matrix products, arithmetic and copies ran while one was open for 0% -> 0% of each run, Pallas kernels for 32% -> 28%
where the time goes in v2:
time: 53.9 us; the launch traced here: 53.8 us
  starting transfers between devices  18.3 us (34%)
  waiting for transfers between devices  17.6 us (33%)
  Pallas kernels  17.1 us (32%)
  between operations  0.76 us (1%)
    ppermute x12, starting transfers between devices, to_partner(): lax.ppermute(values, 'seq', [(i, i ^ bits) for i in range(group_size)])  18.3 us
    ppermute x12, waiting for transfers between devices, to_partner(): lax.ppermute(values, 'seq', [(i, i ^ bits) for i in range(group_size)])  17.6 us
    pallas_call x1, Pallas kernels, build_cache(): pl.pallas_call(body, out_shape=jax.ShapeDtypeStruct(cache, BF16), in_spec...  4.84 us
    pallas_call x2, Pallas kernels, attend(): pl.pallas_call(body, out_shape=out_shape, in_specs=[IN_VMEM, IN_SMEM, IN_...  4.72 us
    pallas_call x1, Pallas kernels, make_codes(): pl.pallas_call(body, out_shape=[jax.ShapeDtypeStruct((tok_rows, span + co...  4.15 us
    pallas_call x2, Pallas kernels, pack_qkv(): pl.pallas_call(body, out_shape=[jax.ShapeDtypeStruct((tok_rows, span), BF...  2.41 us
  transfers between devices with their start and end apart: 12, of which 4 were waited for; matrix products, arithmetic and copies ran while one was open for 0% of the time, Pallas kernels for 28%

profile of v2, /device:TPU:0, one launch (start us, length us, event | category | flops | bytes accessed | tf_op | source)
XLA Modules:
  0.0 53.8 jit_solution(5300548862996280468)
XLA Ops:
  0.6 1.1 %pack_qkv.2._ = bf16[128,1792]{1,0:T(8,128)(2,1)S(1)} custom-call(bf16[128,10752]{1,0:T(8,128)(2,1)} %shared.5), custom_call_target="tpu_custom_call" | custom-call | bytes 917504 | tf_op jit(solution)/shard_map/pack_qkv/pallas_call | solution.py:236
  1.7 4.0 %collective-permute-start = (bf16[128,1792]{1,0:T(8,128)(2,1)S(1)}, bf16[128,1792]{1,0:T(8,128)(2,1)S(1)}, u32[]{:S(2)}, u32[]{:S(2)}) collective-permute-start(bf16[128,1792]{1,0:T(8,128)(2,1)S(1)} %pack_qkv.2._), channel_id=1, source_target_pairs={{0,3},{1,2},{2,1},{3,0},{4,7},{5,6},{6,5},{7,4},{8,11},{9,10},{10,... | collective-permute-start | bytes 1376264 | tf_op jit(solution)/shard_map/ppermute | solution.py:135
  5.7 4.2 %make_codes.1 = (bf16[128,1280]{1,0:T(8,128)(2,1)S(1)}, bf16[128,1920]{1,0:T(8,128)(2,1)S(1)}, bf16[128,1920]{1,0:T(8,128)(2,1)S(1)}, bf16[128,1920]{1,0:T(8,128)(2,1)S(1)}) custom-call(bf16[128,7168]{1,0:T(8,128)(2,1)} %inputs_ref.1, bf16[7168,384]{1,0:T(8,128)(2,1)} %down_ref.1, bf16[128,10752]{1,0:T(8,128)(2,1)} %shared.5, bf16[128,1792]{1,0:T(8,128)(2,1)S(1)} %pack_qkv.2._), custom_call_target="tpu_custom_call" | custom-call | flops 704643072 | bytes 5505024 | tf_op jit(solution)/shard_map/make_codes/pallas_call | solution.py:209
  9.8 0.0 copy-start
  9.9 0.6 %collective-permute-start.2 = (bf16[128,1920]{1,0:T(8,128)(2,1)S(1)}, bf16[128,1920]{1,0:T(8,128)(2,1)S(1)}, u32[]{:S(2)}, u32[]{:S(2)}) collective-permute-start(bf16[128,1920]{1,0:T(8,128)(2,1)S(1)} %get-tuple-element.25), channel_id=1, source_target_pairs={{0,1},{1,0},{2,3},{3,2},{4,5},{5,4},{6,7},{7,6},{8,9},{9,8},{10,11... | collective-permute-start | bytes 1474568 | tf_op jit(solution)/shard_map/ppermute | solution.py:135
  10.5 0.1 collective-permute-start.3
  10.5 2.9 %collective-permute-start.1 = (bf16[128,1280]{1,0:T(8,128)(2,1)S(1)}, bf16[128,1280]{1,0:T(8,128)(2,1)S(1)}, u32[]{:S(2)}, u32[]{:S(2)}) collective-permute-start(bf16[128,1280]{1,0:T(8,128)(2,1)S(1)} %get-tuple-element.24), channel_id=1, source_target_pairs={{0,3},{1,2},{2,1},{3,0},{4,7},{5,6},{6,5},{7,4},{8,11},{9,10},{10,... | collective-permute-start | bytes 983048 | tf_op jit(solution)/shard_map/ppermute | solution.py:135
  13.4 3.6 %collective-permute-done.refs_3_.refs_1_.refs_4_ = bf16[128,1792]{1,0:T(8,128)(2,1)S(1)} collective-permute-done((bf16[128,1792]{1,0:T(8,128)(2,1)S(1)}, bf16[128,1792]{1,0:T(8,128)(2,1)S(1)}, u32[]{:S(2)}, u32[]{:S(2)}) %collective-permute-start) | collective-permute-done | bytes 458784 | tf_op jit(solution)/shard_map/ppermute | solution.py:135
  17.1 1.3 %pack_qkv.3 = (bf16[128,1152]{1,0:T(8,128)(2,1)S(1)}, bf16[128,1152]{1,0:T(8,128)(2,1)S(1)}, bf16[128,1152]{1,0:T(8,128)(2,1)S(1)}) custom-call(bf16[128,10752]{1,0:T(8,128)(2,1)} %shared.5, bf16[128,1920]{1,0:T(8,128)(2,1)S(1)} %get-tuple-element.27.refs_7_.refs_0_, bf16[128,1792]{1,0:T(8,128)(2,1)S(1)} %collective-permute-done.refs_3_.refs_1_.refs_4_), custom_call_target="tpu_custom_call" | custom-call | bytes 1769472 | tf_op jit(solution)/shard_map/pack_qkv/pallas_call | solution.py:236
  18.4 2.1 %collective-permute-start.7 = (bf16[128,1152]{1,0:T(8,128)(2,1)S(1)}, bf16[128,1152]{1,0:T(8,128)(2,1)S(1)}, u32[]{:S(2)}, u32[]{:S(2)}) collective-permute-start(bf16[128,1152]{1,0:T(8,128)(2,1)S(1)} %get-tuple-element.33), channel_id=1, source_target_pairs={{0,1},{1,0},{2,3},{3,2},{4,5},{5,4},{6,7},{7,6},{8,9},{9,8},{10,11... | collective-permute-start | bytes 884744 | tf_op jit(solution)/shard_map/ppermute | solution.py:135
  20.5 1.5 %collective-permute-start.8 = (bf16[128,1152]{1,0:T(8,128)(2,1)S(1)}, bf16[128,1152]{1,0:T(8,128)(2,1)S(1)}, u32[]{:S(2)}, u32[]{:S(2)}) collective-permute-start(bf16[128,1152]{1,0:T(8,128)(2,1)S(1)} %get-tuple-element.34), channel_id=1, source_target_pairs={{0,2},{1,3},{2,0},{3,1},{4,6},{5,7},{6,4},{7,5},{8,10},{9,11},{10,... | collective-permute-start | bytes 884744 | tf_op jit(solution)/shard_map/ppermute | solution.py:135
  22.0 12.7 %collective-permute-done.1.refs_4_.refs_5_ = bf16[128,1280]{1,0:T(8,128)(2,1)S(1)} collective-permute-done((bf16[128,1280]{1,0:T(8,128)(2,1)S(1)}, bf16[128,1280]{1,0:T(8,128)(2,1)S(1)}, u32[]{:S(2)}, u32[]{:S(2)}) %collective-permute-start.1) | collective-permute-done | bytes 327712 | tf_op jit(solution)/shard_map/ppermute | solution.py:135
  34.7 2.7 %attend.2 = (bf16[128,384]{1,0:T(8,128)(2,1)S(1)}, bf16[128,384]{1,0:T(8,128)(2,1)S(1)}, bf16[128,384]{1,0:T(8,128)(2,1)S(1)}, bf16[128,384]{1,0:T(8,128)(2,1)S(...) custom-call(bf16[3,128,896]{2,1,0:T(8,128)(2,1)S(1)} %copy-done, ...), custom_call_target="tpu_custom_call" | custom-call | flops 536870912 | bytes 4194304 | tf_op jit(solution)/shard_map/attend/pallas_call | solution.py:373
  37.4 2.1 %collective-permute-start.4 = (bf16[128,384]{1,0:T(8,128)(2,1)S(1)}, bf16[128,384]{1,0:T(8,128)(2,1)S(1)}, u32[]{:S(2)}, u32[]{:S(2)}) collective-permute-start(bf16[128,384]{1,0:T(8,128)(2,1)S(1)} %get-tuple-element.29), channel_id=1, source_target_pairs={{0,1},{1,0},{2,3},{3,2},{4,5},{5,4},{6,7},{7,6},{8,9},{9,8},{10,11... | collective-permute-start | bytes 294920 | tf_op jit(solution)/shard_map/ppermute | solution.py:135
  39.4 1.5 %collective-permute-start.5 = (bf16[128,384]{1,0:T(8,128)(2,1)S(1)}, bf16[128,384]{1,0:T(8,128)(2,1)S(1)}, u32[]{:S(2)}, u32[]{:S(2)}) collective-permute-start(bf16[128,384]{1,0:T(8,128)(2,1)S(1)} %get-tuple-element.30), channel_id=1, source_target_pairs={{0,2},{1,3},{2,0},{3,1},{4,6},{5,7},{6,4},{7,5},{8,10},{9,11},{10,... | collective-permute-start | bytes 294920 | tf_op jit(solution)/shard_map/ppermute | solution.py:135
  41.0 0.0 collective-permute-start.6
  41.0 0.6 %collective-permute-done.7.refs_6_ = bf16[128,1152]{1,0:T(8,128)(2,1)S(1)} collective-permute-done((bf16[128,1152]{1,0:T(8,128)(2,1)S(1)}, bf16[128,1152]{1,0:T(8,128)(2,1)S(1)}, u32[]{:S(2)}, u32[]{:S(2)}) %collective-permute-start.7) | collective-permute-done | bytes 294944 | tf_op jit(solution)/shard_map/ppermute | solution.py:135
  41.6 2.1 %attend.3 = (bf16[128,512]{1,0:T(8,128)(2,1)S(1)}, bf16[128,512]{1,0:T(8,128)(2,1)S(1)}, bf16[128,512]{1,0:T(8,128)(2,1)S(1)}, bf16[128,512]{1,0:T(8,128)(2,1)S(...) custom-call(bf16[3,128,896]{2,1,0:T(8,128)(2,1)S(1)} %copy-done, f32[4]{0:T(128)S(1)} %copy-done.1, ...), custom_call_target="tpu_custom_call" | custom-call | flops 402653184 | bytes 3145728 | tf_op jit(solution)/shard_map/attend/pallas_call | solution.py:373
  43.6 1.6 %collective-permute-start.9 = (bf16[128,512]{1,0:T(8,128)(2,1)S(1)}, bf16[128,512]{1,0:T(8,128)(2,1)S(1)}, u32[]{:S(2)}, u32[]{:S(2)}) collective-permute-start(bf16[128,512]{1,0:T(8,128)(2,1)S(1)} %get-tuple-element.41), channel_id=1, source_target_pairs={{0,1},{1,0},{2,3},{3,2},{4,5},{5,4},{6,7},{7,6},{8,9},{9,8},{10,11... | collective-permute-start | bytes 393224 | tf_op jit(solution)/shard_map/ppermute | solution.py:135
  45.2 1.4 %collective-permute-start.10 = (bf16[128,512]{1,0:T(8,128)(2,1)S(1)}, bf16[128,512]{1,0:T(8,128)(2,1)S(1)}, u32[]{:S(2)}, u32[]{:S(2)}) collective-permute-start(bf16[128,512]{1,0:T(8,128)(2,1)S(1)} %get-tuple-element.42), channel_id=1, source_target_pairs={{0,2},{1,3},{2,0},{3,1},{4,6},{5,7},{6,4},{7,5},{8,10},{9,11},{10,... | collective-permute-start | bytes 393224 | tf_op jit(solution)/shard_map/ppermute | solution.py:135
  46.6 0.6 %collective-permute-start.11 = (bf16[128,512]{1,0:T(8,128)(2,1)S(1)}, bf16[128,512]{1,0:T(8,128)(2,1)S(1)}, u32[]{:S(2)}, u32[]{:S(2)}) collective-permute-start(bf16[128,512]{1,0:T(8,128)(2,1)S(1)} %get-tuple-element.43), channel_id=1, source_target_pairs={{0,3},{1,2},{2,1},{3,0},{4,7},{5,6},{6,5},{7,4},{8,11},{9,10},{10,... | collective-permute-start | bytes 393224 | tf_op jit(solution)/shard_map/ppermute | solution.py:135
  47.2 4.8 %build_cache.1 = bf16[4,40,2,3584]{3,2,1,0:T(2,128)(2,1)} custom-call(bf16[4,512,128]{2,1,0:T(8,128)(2,1)S(1)} %get-tuple-element.38.refs_11_.refs_0_, bf16[4,512,128]{2,1,0:T(8,128)(2,1)S(1)} %get-tuple-element.44.refs_1_, bf16[4,512,128]{2,1,0:T(8,128)(2,1)S(1)} %get-tuple-element.39.refs_12_.refs_2_, bf16[4,512,128]{2,1,0:T(8,128)(2,1)S(1)} %get-tuple-element.45.refs_3_, ...), custom_call_target="tpu_custom_call" | custom-call | flops 2348810240 | bytes 3670016 | tf_op jit(solution)/shard_map/build_cache/pallas_call | solution.py:452
  52.1 0.7 %collective-permute-done.10.refs_6_ = bf16[128,512]{1,0:T(8,128)(2,1)S(1)} collective-permute-done((bf16[128,512]{1,0:T(8,128)(2,1)S(1)}, bf16[128,512]{1,0:T(8,128)(2,1)S(1)}, u32[]{:S(2)}, u32[]{:S(2)}) %collective-permute-start.10) | collective-permute-done | bytes 131104 | tf_op jit(solution)/shard_map/ppermute | solution.py:135
  52.8 1.0 %join_heads.1 = bf16[128,3584]{1,0:T(8,128)(2,1)} custom-call(bf16[128,384]{1,0:T(8,128)(2,1)S(1)} %get-tuple-element.28.refs_0_, bf16[128,384]{1,0:T(8,128)(2,1)S(1)} %collective-permute-done.4.refs_1_, bf16[128,384]{1,0:T(8,128)(2,1)S(1)} %collective-permute-done.5.refs_2_, bf16[128,384]{1,0:T(8,128)(2,1)S(1)} %collective-permute-done.6.refs_3_, ...), custom_call_target="tpu_custom_call" | custom-call | bytes 1835008 | tf_op jit(solution)/shard_map/join_heads/pallas_call | solution.py:489
  (15 shorter events, 0.0 us)
Async XLA Ops:
  1.7 15.4 %collective-permute-start = (bf16[128,1792]{1,0:T(8,128)(2,1)S(1)}, bf16[128,1792]{1,0:T(8,128)(2,1)S(1)}, u32[]{:S(2)}, u32[]{:S(2)}) collective-permute-start(bf16[128,1792]{1,0:T(8,128)(2,1)S(1)} %pack_qkv.2._), channel_id=1, source_target_pairs={{0,3},{1,2},{2,1},{3,0},{4,7},{5,6},{6,5},{7,4},{8,11},{9,10},{10,... | collective-permute-start | bytes 1376264 | tf_op jit(solution)/shard_map/ppermute | solution.py:135
  9.8 24.8 %copy-start = (bf16[3,128,896]{2,1,0:T(8,128)(2,1)S(1)}, bf16[3,128,896]{2,1,0:T(8,128)(2,1)}, u32[]{:S(2)}) copy-start(bf16[3,128,896]{2,1,0:T(8,128)(2,1)} %refs_0_.3) | copy-start | bytes 2064388
  9.9 24.8 %copy-start.1 = (f32[4]{0:T(128)S(1)}, f32[4]{0:T(128)}, u32[]{:S(2)}) copy-start(f32[4]{0:T(128)} %refs_1_.3) | copy-start | bytes 52
  9.9 24.8 %copy-start.2 = (s32[8]{0:T(128)S(1)}, s32[8]{0:T(128)}, u32[]{:S(2)}) copy-start(s32[8]{0:T(128)} %refs_4_.1) | copy-start | bytes 100
  9.9 24.8 %collective-permute-start.2 = (bf16[128,1920]{1,0:T(8,128)(2,1)S(1)}, bf16[128,1920]{1,0:T(8,128)(2,1)S(1)}, u32[]{:S(2)}, u32[]{:S(2)}) collective-permute-start(bf16[128,1920]{1,0:T(8,128)(2,1)S(1)} %get-tuple-element.25), channel_id=1, source_target_pairs={{0,1},{1,0},{2,3},{3,2},{4,5},{5,4},{6,7},{7,6},{8,9},{9,8},{10,11... | collective-permute-start | bytes 1474568 | tf_op jit(solution)/shard_map/ppermute | solution.py:135
  10.5 24.2 %collective-permute-start.3 = (bf16[128,1920]{1,0:T(8,128)(2,1)S(1)}, bf16[128,1920]{1,0:T(8,128)(2,1)S(1)}, u32[]{:S(2)}, u32[]{:S(2)}) collective-permute-start(bf16[128,1920]{1,0:T(8,128)(2,1)S(1)} %get-tuple-element.26), channel_id=1, source_target_pairs={{0,2},{1,3},{2,0},{3,1},{4,6},{5,7},{6,4},{7,5},{8,10},{9,11},{10,... | collective-permute-start | bytes 1474568 | tf_op jit(solution)/shard_map/ppermute | solution.py:135
  10.5 24.1 %collective-permute-start.1 = (bf16[128,1280]{1,0:T(8,128)(2,1)S(1)}, bf16[128,1280]{1,0:T(8,128)(2,1)S(1)}, u32[]{:S(2)}, u32[]{:S(2)}) collective-permute-start(bf16[128,1280]{1,0:T(8,128)(2,1)S(1)} %get-tuple-element.24), channel_id=1, source_target_pairs={{0,3},{1,2},{2,1},{3,0},{4,7},{5,6},{6,5},{7,4},{8,11},{9,10},{10,... | collective-permute-start | bytes 983048 | tf_op jit(solution)/shard_map/ppermute | solution.py:135
  18.4 23.2 %collective-permute-start.7 = (bf16[128,1152]{1,0:T(8,128)(2,1)S(1)}, bf16[128,1152]{1,0:T(8,128)(2,1)S(1)}, u32[]{:S(2)}, u32[]{:S(2)}) collective-permute-start(bf16[128,1152]{1,0:T(8,128)(2,1)S(1)} %get-tuple-element.33), channel_id=1, source_target_pairs={{0,1},{1,0},{2,3},{3,2},{4,5},{5,4},{6,7},{7,6},{8,9},{9,8},{10,11... | collective-permute-start | bytes 884744 | tf_op jit(solution)/shard_map/ppermute | solution.py:135
  20.5 21.1 %collective-permute-start.8 = (bf16[128,1152]{1,0:T(8,128)(2,1)S(1)}, bf16[128,1152]{1,0:T(8,128)(2,1)S(1)}, u32[]{:S(2)}, u32[]{:S(2)}) collective-permute-start(bf16[128,1152]{1,0:T(8,128)(2,1)S(1)} %get-tuple-element.34), channel_id=1, source_target_pairs={{0,2},{1,3},{2,0},{3,1},{4,6},{5,7},{6,4},{7,5},{8,10},{9,11},{10,... | collective-permute-start | bytes 884744 | tf_op jit(solution)/shard_map/ppermute | solution.py:135
  37.4 9.3 %collective-permute-start.4 = (bf16[128,384]{1,0:T(8,128)(2,1)S(1)}, bf16[128,384]{1,0:T(8,128)(2,1)S(1)}, u32[]{:S(2)}, u32[]{:S(2)}) collective-permute-start(bf16[128,384]{1,0:T(8,128)(2,1)S(1)} %get-tuple-element.29), channel_id=1, source_target_pairs={{0,1},{1,0},{2,3},{3,2},{4,5},{5,4},{6,7},{7,6},{8,9},{9,8},{10,11... | collective-permute-start | bytes 294920 | tf_op jit(solution)/shard_map/ppermute | solution.py:135
  39.4 12.6 %collective-permute-start.5 = (bf16[128,384]{1,0:T(8,128)(2,1)S(1)}, bf16[128,384]{1,0:T(8,128)(2,1)S(1)}, u32[]{:S(2)}, u32[]{:S(2)}) collective-permute-start(bf16[128,384]{1,0:T(8,128)(2,1)S(1)} %get-tuple-element.30), channel_id=1, source_target_pairs={{0,2},{1,3},{2,0},{3,1},{4,6},{5,7},{6,4},{7,5},{8,10},{9,11},{10,... | collective-permute-start | bytes 294920 | tf_op jit(solution)/shard_map/ppermute | solution.py:135
  41.0 11.1 %collective-permute-start.6 = (bf16[128,384]{1,0:T(8,128)(2,1)S(1)}, bf16[128,384]{1,0:T(8,128)(2,1)S(1)}, u32[]{:S(2)}, u32[]{:S(2)}) collective-permute-start(bf16[128,384]{1,0:T(8,128)(2,1)S(1)} %get-tuple-element.31), channel_id=1, source_target_pairs={{0,3},{1,2},{2,1},{3,0},{4,7},{5,6},{6,5},{7,4},{8,11},{9,10},{10,... | collective-permute-start | bytes 294920 | tf_op jit(solution)/shard_map/ppermute | solution.py:135
  41.6 5.6 %copy-start.3 = (s32[8,24]{1,0:T(8,128)S(1)}, s32[8,24]{1,0:T(8,128)}, u32[]{:S(2)}) copy-start(s32[8,24]{1,0:T(8,128)} %refs_5_.1) | copy-start | bytes 2308
  43.6 8.4 %collective-permute-start.9 = (bf16[128,512]{1,0:T(8,128)(2,1)S(1)}, bf16[128,512]{1,0:T(8,128)(2,1)S(1)}, u32[]{:S(2)}, u32[]{:S(2)}) collective-permute-start(bf16[128,512]{1,0:T(8,128)(2,1)S(1)} %get-tuple-element.41), channel_id=1, source_target_pairs={{0,1},{1,0},{2,3},{3,2},{4,5},{5,4},{6,7},{7,6},{8,9},{9,8},{10,11... | collective-permute-start | bytes 393224 | tf_op jit(solution)/shard_map/ppermute | solution.py:135
  45.2 7.6 %collective-permute-start.10 = (bf16[128,512]{1,0:T(8,128)(2,1)S(1)}, bf16[128,512]{1,0:T(8,128)(2,1)S(1)}, u32[]{:S(2)}, u32[]{:S(2)}) collective-permute-start(bf16[128,512]{1,0:T(8,128)(2,1)S(1)} %get-tuple-element.42), channel_id=1, source_target_pairs={{0,2},{1,3},{2,0},{3,1},{4,6},{5,7},{6,4},{7,5},{8,10},{9,11},{10,... | collective-permute-start | bytes 393224 | tf_op jit(solution)/shard_map/ppermute | solution.py:135
  46.6 6.1 %collective-permute-start.11 = (bf16[128,512]{1,0:T(8,128)(2,1)S(1)}, bf16[128,512]{1,0:T(8,128)(2,1)S(1)}, u32[]{:S(2)}, u32[]{:S(2)}) collective-permute-start(bf16[128,512]{1,0:T(8,128)(2,1)S(1)} %get-tuple-element.43), channel_id=1, source_target_pairs={{0,3},{1,2},{2,1},{3,0},{4,7},{5,6},{6,5},{7,4},{8,11},{9,10},{10,... | collective-permute-start | bytes 393224 | tf_op jit(solution)/shard_map/ppermute | solution.py:135

commit v3 on v2

--- a/solution.py
+++ b/solution.py
@@ -119,6 +119,7 @@
 
 
 LANES = 128
+SLABS = 1
 BF16 = jnp.bfloat16
 F32 = jnp.float32
 ANYWHERE = pl.BlockSpec(memory_space=pl.ANY)
@@ -154,19 +155,22 @@
 
 def start_columns(shared, outs, sem, width, wanted):
     me = lax.axis_index("seq")
+    slab = shared.shape[0] // SLABS
     copies = []
     for n, (bits, kinds, tiles) in enumerate(wanted):
         span = (tiles[1] - tiles[0]) * LANES
         owner = jnp.bitwise_xor(me, bits)
         for m, c in enumerate(kinds):
             first = pl.multiple_of(c * HEADS * HD + owner * width + tiles[0] * LANES, LANES)
-            copies.append(
-                pltpu.make_async_copy(
-                    shared.at[:, pl.ds(first, span)],
-                    outs[n].at[:, pl.ds(m * span, span)],
-                    sem.at[n, m],
-                )
-            )
+            for k in range(SLABS):
+                rows = pl.ds(k * slab, slab)
+                copies.append(
+                    pltpu.make_async_copy(
+                        shared.at[rows, pl.ds(first, span)],
+                        outs[n].at[rows, pl.ds(m * span, span)],
+                        sem.at[n, m, k],
+                    )
+                )
     for copy in copies:
         copy.start()
     return copies
@@ -216,7 +220,7 @@
             pltpu.VMEM((depth, code_width), BF16),
             pltpu.SemaphoreType.DMA((steps,)),
             pltpu.SemaphoreType.DMA((steps,)),
-            pltpu.SemaphoreType.DMA((len(wanted), 3)),
+            pltpu.SemaphoreType.DMA((len(wanted), 3, SLABS)),
         ],
         compiler_params=params(20),
         cost_estimate=cost(2 * tok_rows * depth * code_width, depth * code_width * 2),
@@ -238,7 +242,7 @@
         out_shape=[jax.ShapeDtypeStruct((tok_rows, span), BF16) for span in spans],
         in_specs=[IN_HBM] + [ANYWHERE] * len(after),
         out_specs=[IN_VMEM] * len(wanted),
-        scratch_shapes=[pltpu.SemaphoreType.DMA((len(wanted), 3))],
+        scratch_shapes=[pltpu.SemaphoreType.DMA((len(wanted), 3, SLABS))],
         compiler_params=params(20),
         cost_estimate=cost(0, 2 * tok_rows * sum(spans) * 2),
         name="pack_qkv",
@@ -395,17 +399,15 @@
     heads_local = width // HD
     page_count = total_rows // PAGE + SEGS
     blocks = block_table.shape[1]
-    rows = 2 * page_count
     group = 4
 
     def body(*refs):
         key_refs, value_refs = refs[:parts], refs[parts : 2 * parts]
         lens, table, out, built, sem = refs[2 * parts :]
-        row = lax.broadcasted_iota(jnp.int32, (rows, blocks), 0)
-        page = lax.shift_right_logical(row, 1)
-        block = lax.broadcasted_iota(jnp.int32, (rows, blocks), 1)
-        first = jnp.zeros((rows, blocks), jnp.int32)
-        count = jnp.zeros((rows, blocks), jnp.int32)
+        page = lax.broadcasted_iota(jnp.int32, (page_count, blocks), 0)
+        block = lax.broadcasted_iota(jnp.int32, (page_count, blocks), 1)
+        first = jnp.zeros((page_count, blocks), jnp.int32)
+        count = jnp.zeros((page_count, blocks), jnp.int32)
         start = 0
         for s in range(SEGS):
             left = lens[s] - block * PAGE
@@ -415,30 +417,26 @@
             start = start + lens[s]
         first = jnp.sum(first, axis=1, keepdims=True)
         count = jnp.sum(count, axis=1, keepdims=True)
-        odd = jnp.bitwise_and(lax.broadcasted_iota(jnp.int32, (rows, 1), 0), 1)
-        place = lax.broadcasted_iota(jnp.int32, (group * rows, total_rows), 1)
-
-        def columns(part_refs):
+        place = lax.broadcasted_iota(jnp.int32, (group * page_count, total_rows), 1)
+
+        def gathered(part_refs):
             every = [(ref, tile) for ref, low in zip(part_refs, starts) for tile in range(low, ref.shape[0])]
             return jnp.concatenate([ref[tile] for ref, tile in every], axis=1)
 
-        all_keys, all_values = columns(key_refs), columns(value_refs)
+        all_keys, all_values = gathered(key_refs), gathered(value_refs)
         copies = []
         for r in range(0, PAGE, group):
             wanted = [jnp.where(count > r + n, first + r + n, -1) for n in range(group)]
-            for_keys = jnp.concatenate([jnp.where(odd == 0, want, -1) for want in wanted], axis=0)
-            for_values = jnp.concatenate([jnp.where(odd == 1, want, -1) for want in wanted], axis=0)
-            pick_keys = (place == for_keys).astype(F32).astype(BF16)
-            pick_values = (place == for_values).astype(F32).astype(BF16)
-            picked = jnp.dot(pick_keys, all_keys, preferred_element_type=F32) + jnp.dot(
-                pick_values, all_values, preferred_element_type=F32
-            )
+            pick = (place == jnp.concatenate(wanted, axis=0)).astype(F32).astype(BF16)
+            picked = [jnp.dot(pick, every, preferred_element_type=F32) for every in (all_keys, all_values)]
             lanes = slice(r * HD, (r + group) * HD)
             for h in range(heads_local):
-                line = jnp.concatenate(
-                    [picked[m * rows : (m + 1) * rows, h * HD : (h + 1) * HD] for m in range(group)], axis=1
-                )
-                built[h, :, :, lanes] = line.astype(BF16).reshape(page_count, 2, group * HD)
+                columns = slice(h * HD, (h + 1) * HD)
+                for c in range(2):
+                    line = jnp.concatenate(
+                        [picked[c][m * page_count : (m + 1) * page_count, columns] for m in range(group)], axis=1
+                    )
+                    built[h, :, c, lanes] = line.astype(BF16)
                 copies.append(
                     pltpu.make_async_copy(
                         built.at[h, :, :, lanes], out.at[h, :, :, lanes], sem.at[h, r // group]
@@ -456,31 +454,29 @@
         out_specs=IN_HBM,
         scratch_shapes=[pltpu.VMEM(cache, BF16), pltpu.SemaphoreType.DMA((heads_local, PAGE // group))],
         compiler_params=params(),
-        cost_estimate=cost(4 * rows * PAGE * total_rows * width, 4 * total_rows * width * 2),
+        cost_estimate=cost(4 * page_count * PAGE * total_rows * width, 4 * total_rows * width * 2),
         name="build_cache",
     )(*keys, *values, lengths, block_table)
 
 
-def join_heads(parts, group_size):
+def join_heads(hidden, parts, width, group_size):
     tok_rows = parts[0][0].shape[0]
-    width = sum(blocks[0].shape[1] for blocks in parts)
-    sources = [block for blocks in parts for block in blocks]
+    slab = tok_rows // SLABS
+    given = [] if hidden is None else [hidden]
 
     def body(*refs):
         out, sem = refs[-2:]
         me = lax.axis_index("seq")
         copies = []
-        begin = 0
-        for n, blocks in enumerate(parts):
-            span = blocks[0].shape[1]
-            for bits in range(group_size):
-                first = pl.multiple_of(jnp.bitwise_xor(me, bits) * width + begin, LANES)
+        for n, (part, bits, begin) in enumerate(parts):
+            first = pl.multiple_of(jnp.bitwise_xor(me, bits) * width + begin, LANES)
+            for k in range(SLABS):
+                rows = pl.ds(k * slab, slab)
                 copies.append(
                     pltpu.make_async_copy(
-                        refs[n * group_size + bits], out.at[:, pl.ds(first, span)], sem.at[n, bits]
+                        refs[n].at[rows, :], out.at[rows, pl.ds(first, part.shape[1])], sem.at[n, k]
                     )
                 )
-            begin += span
         for copy in copies:
             copy.start()
         for copy in copies:
@@ -489,13 +485,14 @@
     return pl.pallas_call(
         body,
         out_shape=jax.ShapeDtypeStruct((tok_rows, width * group_size), BF16),
-        in_specs=[ANYWHERE] * len(sources),
+        in_specs=[ANYWHERE] * len(parts) + [IN_HBM] * len(given),
         out_specs=IN_HBM,
-        scratch_shapes=[pltpu.SemaphoreType.DMA((len(parts), group_size))],
+        scratch_shapes=[pltpu.SemaphoreType.DMA((len(parts), SLABS))],
+        input_output_aliases={len(parts): 0} if given else {},
         compiler_params=params(),
-        cost_estimate=cost(0, 2 * tok_rows * width * group_size * 2),
+        cost_estimate=cost(0, 4 * tok_rows * sum(part.shape[1] for part, _, _ in parts)),
         name="join_heads",
-    )(*sources)
+    )(*[part for part, _, _ in parts], *map(stay, given))
 
 
 def per_device_tiled(inputs, adapter_down, adapter_up, shared_qkv, sink_logits, lengths, block_table):
@@ -530,7 +527,7 @@
         begin = tiles[n][0] * LANES
         at[first] = [(0, begin), (0, width + begin), (1, begin), (1, width)]
         places.append([at[bits] for bits in range(group_size)])
-    low_rank, carried, hidden, keys, values = None, [], [], [], []
+    low_rank, carried, keys, values, own, back = None, [], [], [], [], []
     for n in range(2):
         blocks, new_keys, new_values, low_rank, carried = attend(
             adapter_up,
@@ -544,12 +541,15 @@
             tiles[n],
             done_tiles[n],
         )
-        returned = {bits: to_partner(blocks[bits], bits, group_size) for bits in partners}
-        hidden.append([blocks[0]] + [returned[bits] for bits in range(1, group_size)])
+        begin = done_tiles[n][0] * LANES
+        own.append((blocks[0], 0, begin))
+        back.append([(to_partner(blocks[bits], bits, group_size), bits, begin) for bits in partners])
         keys, values = keys + [new_keys], values + [new_values]
     starts = [0, cut - done_cut]
     cache = build_cache(keys, values, starts, lengths, block_table)
-    return (join_heads(hidden, group_size), cache)
+    hidden = join_heads(None, own + back[0], width, group_size)
+    hidden = join_heads(hidden, back[1], width, group_size)
+    return (hidden, cache)
 
 
 def per_device(inputs, adapter_down, adapter_up, shared_qkv, sink_logits, lengths, block_table):

time: 53.9 us -> 53.4 us (level)
    pallas_call x1, Pallas kernels: 4.84 us -> 3.99 us  [build_cache(): pl.pallas_call(body, out_shape=jax.ShapeDtypeStruct(cache, BF16), in_spec...]
    pallas_call x1 -> x2, Pallas kernels: 0.98 us -> 1.59 us  [join_heads(): pl.pallas_call(body, out_shape=jax.ShapeDtypeStruct((tok_rows, width * gr...]
where the time goes in v3:
time: 53.4 us; the launch traced here: 53.2 us
  starting transfers between devices  18.3 us (34%)
  waiting for transfers between devices  17.2 us (32%)
  Pallas kernels  16.9 us (32%)
  between operations  0.76 us (1%)
    ppermute x12, starting transfers between devices, to_partner(): lax.ppermute(values, 'seq', [(i, i ^ bits) for i in range(group_size)])  18.3 us
    ppermute x12, waiting for transfers between devices, to_partner(): lax.ppermute(values, 'seq', [(i, i ^ bits) for i in range(group_size)])  17.2 us
    pallas_call x2, Pallas kernels, attend(): pl.pallas_call(body, out_shape=out_shape, in_specs=[IN_VMEM, IN_SMEM, IN_...  4.71 us
    pallas_call x1, Pallas kernels, make_codes(): pl.pallas_call(body, out_shape=[jax.ShapeDtypeStruct((tok_rows, span + co...  4.15 us
    pallas_call x1, Pallas kernels, build_cache(): pl.pallas_call(body, out_shape=jax.ShapeDtypeStruct(cache, BF16), in_spec...  3.99 us
    pallas_call x2, Pallas kernels, pack_qkv(): pl.pallas_call(body, out_shape=[jax.ShapeDtypeStruct((tok_rows, span), BF...  2.41 us
    pallas_call x2, Pallas kernels, join_heads(): pl.pallas_call(body, out_shape=jax.ShapeDtypeStruct((tok_rows, width * gr...  1.59 us
  transfers between devices with their start and end apart: 12, of which 4 were waited for; matrix products, arithmetic and copies ran while one was open for 0% of the time, Pallas kernels for 28%

profile of v3, /device:TPU:0, one launch (start us, length us, event | category | flops | bytes accessed | tf_op | source)
XLA Modules:
  0.0 53.2 jit_solution(6828859006799741125)
XLA Ops:
  0.6 1.1 %pack_qkv.2._ = bf16[128,1792]{1,0:T(8,128)(2,1)S(1)} custom-call(bf16[128,10752]{1,0:T(8,128)(2,1)} %shared.5), custom_call_target="tpu_custom_call" | custom-call | bytes 917504 | tf_op jit(solution)/shard_map/pack_qkv/pallas_call | solution.py:240
  1.7 4.0 %collective-permute-start = (bf16[128,1792]{1,0:T(8,128)(2,1)S(1)}, bf16[128,1792]{1,0:T(8,128)(2,1)S(1)}, u32[]{:S(2)}, u32[]{:S(2)}) collective-permute-start(bf16[128,1792]{1,0:T(8,128)(2,1)S(1)} %pack_qkv.2._), channel_id=1, source_target_pairs={{0,3},{1,2},{2,1},{3,0},{4,7},{5,6},{6,5},{7,4},{8,11},{9,10},{10,... | collective-permute-start | bytes 1376264 | tf_op jit(solution)/shard_map/ppermute | solution.py:136
  5.7 4.2 %make_codes.1 = (bf16[128,1280]{1,0:T(8,128)(2,1)S(1)}, bf16[128,1920]{1,0:T(8,128)(2,1)S(1)}, bf16[128,1920]{1,0:T(8,128)(2,1)S(1)}, bf16[128,1920]{1,0:T(8,128)(2,1)S(1)}) custom-call(bf16[128,7168]{1,0:T(8,128)(2,1)} %inputs_ref.1, bf16[7168,384]{1,0:T(8,128)(2,1)} %down_ref.1, bf16[128,10752]{1,0:T(8,128)(2,1)} %shared.5, bf16[128,1792]{1,0:T(8,128)(2,1)S(1)} %pack_qkv.2._), custom_call_target="tpu_custom_call" | custom-call | flops 704643072 | bytes 5505024 | tf_op jit(solution)/shard_map/make_codes/pallas_call | solution.py:213
  9.9 0.6 %collective-permute-start.2 = (bf16[128,1920]{1,0:T(8,128)(2,1)S(1)}, bf16[128,1920]{1,0:T(8,128)(2,1)S(1)}, u32[]{:S(2)}, u32[]{:S(2)}) collective-permute-start(bf16[128,1920]{1,0:T(8,128)(2,1)S(1)} %get-tuple-element.25), channel_id=1, source_target_pairs={{0,1},{1,0},{2,3},{3,2},{4,5},{5,4},{6,7},{7,6},{8,9},{9,8},{10,11... | collective-permute-start | bytes 1474568 | tf_op jit(solution)/shard_map/ppermute | solution.py:136
  10.5 0.1 collective-permute-start.3
  10.5 2.9 %collective-permute-start.1 = (bf16[128,1280]{1,0:T(8,128)(2,1)S(1)}, bf16[128,1280]{1,0:T(8,128)(2,1)S(1)}, u32[]{:S(2)}, u32[]{:S(2)}) collective-permute-start(bf16[128,1280]{1,0:T(8,128)(2,1)S(1)} %get-tuple-element.24), channel_id=1, source_target_pairs={{0,3},{1,2},{2,1},{3,0},{4,7},{5,6},{6,5},{7,4},{8,11},{9,10},{10,... | collective-permute-start | bytes 983048 | tf_op jit(solution)/shard_map/ppermute | solution.py:136
  13.4 3.6 %collective-permute-done.refs_3_.refs_1_.refs_4_ = bf16[128,1792]{1,0:T(8,128)(2,1)S(1)} collective-permute-done((bf16[128,1792]{1,0:T(8,128)(2,1)S(1)}, bf16[128,1792]{1,0:T(8,128)(2,1)S(1)}, u32[]{:S(2)}, u32[]{:S(2)}) %collective-permute-start) | collective-permute-done | bytes 458784 | tf_op jit(solution)/shard_map/ppermute | solution.py:136
  17.1 1.3 %pack_qkv.3 = (bf16[128,1152]{1,0:T(8,128)(2,1)S(1)}, bf16[128,1152]{1,0:T(8,128)(2,1)S(1)}, bf16[128,1152]{1,0:T(8,128)(2,1)S(1)}) custom-call(bf16[128,10752]{1,0:T(8,128)(2,1)} %shared.5, bf16[128,1920]{1,0:T(8,128)(2,1)S(1)} %get-tuple-element.27.refs_7_.refs_0_, bf16[128,1792]{1,0:T(8,128)(2,1)S(1)} %collective-permute-done.refs_3_.refs_1_.refs_4_), custom_call_target="tpu_custom_call" | custom-call | bytes 1769472 | tf_op jit(solution)/shard_map/pack_qkv/pallas_call | solution.py:240
  18.4 2.1 %collective-permute-start.4 = (bf16[128,1152]{1,0:T(8,128)(2,1)S(1)}, bf16[128,1152]{1,0:T(8,128)(2,1)S(1)}, u32[]{:S(2)}, u32[]{:S(2)}) collective-permute-start(bf16[128,1152]{1,0:T(8,128)(2,1)S(1)} %get-tuple-element.29), channel_id=1, source_target_pairs={{0,1},{1,0},{2,3},{3,2},{4,5},{5,4},{6,7},{7,6},{8,9},{9,8},{10,11... | collective-permute-start | bytes 884744 | tf_op jit(solution)/shard_map/ppermute | solution.py:136
  20.5 1.5 %collective-permute-start.5 = (bf16[128,1152]{1,0:T(8,128)(2,1)S(1)}, bf16[128,1152]{1,0:T(8,128)(2,1)S(1)}, u32[]{:S(2)}, u32[]{:S(2)}) collective-permute-start(bf16[128,1152]{1,0:T(8,128)(2,1)S(1)} %get-tuple-element.30), channel_id=1, source_target_pairs={{0,2},{1,3},{2,0},{3,1},{4,6},{5,7},{6,4},{7,5},{8,10},{9,11},{10,... | collective-permute-start | bytes 884744 | tf_op jit(solution)/shard_map/ppermute | solution.py:136
  22.0 12.7 %collective-permute-done.1.refs_4_.refs_5_ = bf16[128,1280]{1,0:T(8,128)(2,1)S(1)} collective-permute-done((bf16[128,1280]{1,0:T(8,128)(2,1)S(1)}, bf16[128,1280]{1,0:T(8,128)(2,1)S(1)}, u32[]{:S(2)}, u32[]{:S(2)}) %collective-permute-start.1) | collective-permute-done | bytes 327712 | tf_op jit(solution)/shard_map/ppermute | solution.py:136
  34.7 2.7 %attend.2 = (bf16[128,384]{1,0:T(8,128)(2,1)S(1)}, bf16[128,384]{1,0:T(8,128)(2,1)S(1)}, bf16[128,384]{1,0:T(8,128)(2,1)S(1)}, bf16[128,384]{1,0:T(8,128)(2,1)S(...) custom-call(bf16[3,128,896]{2,1,0:T(8,128)(2,1)S(1)} %copy-done, ...), custom_call_target="tpu_custom_call" | custom-call | flops 536870912 | bytes 4194304 | tf_op jit(solution)/shard_map/attend/pallas_call | solution.py:377
  37.4 3.0 %collective-permute-start.9 = (bf16[128,384]{1,0:T(8,128)(2,1)S(1)}, bf16[128,384]{1,0:T(8,128)(2,1)S(1)}, u32[]{:S(2)}, u32[]{:S(2)}) collective-permute-start(bf16[128,384]{1,0:T(8,128)(2,1)S(1)} %get-tuple-element.41), channel_id=1, source_target_pairs={{0,3},{1,2},{2,1},{3,0},{4,7},{5,6},{6,5},{7,4},{8,11},{9,10},{10,... | collective-permute-start | bytes 294920 | tf_op jit(solution)/shard_map/ppermute | solution.py:136
  40.4 0.5 collective-permute-start.10
  40.9 0.1 collective-permute-start.11
  41.0 0.4 collective-permute-done.4.refs_6_
  41.5 2.1 %attend.3 = (bf16[128,512]{1,0:T(8,128)(2,1)S(1)}, bf16[128,512]{1,0:T(8,128)(2,1)S(1)}, bf16[128,512]{1,0:T(8,128)(2,1)S(1)}, bf16[128,512]{1,0:T(8,128)(2,1)S(...) custom-call(bf16[3,128,896]{2,1,0:T(8,128)(2,1)S(1)} %copy-done, f32[4]{0:T(128)S(1)} %copy-done.3, ...), custom_call_target="tpu_custom_call" | custom-call | flops 402653184 | bytes 3145728 | tf_op jit(solution)/shard_map/attend/pallas_call | solution.py:377
  43.5 2.5 %collective-permute-start.6 = (bf16[128,512]{1,0:T(8,128)(2,1)S(1)}, bf16[128,512]{1,0:T(8,128)(2,1)S(1)}, u32[]{:S(2)}, u32[]{:S(2)}) collective-permute-start(bf16[128,512]{1,0:T(8,128)(2,1)S(1)} %get-tuple-element.36), channel_id=1, source_target_pairs={{0,3},{1,2},{2,1},{3,0},{4,7},{5,6},{6,5},{7,4},{8,11},{9,10},{10,... | collective-permute-start | bytes 393224 | tf_op jit(solution)/shard_map/ppermute | solution.py:136
  46.1 0.5 collective-permute-start.7
  46.6 0.5 collective-permute-start.8
  47.1 0.8 %join_heads.2.refs_3_ = bf16[128,3584]{1,0:T(8,128)(2,1)} custom-call(bf16[128,384]{1,0:T(8,128)(2,1)S(1)} %get-tuple-element.39.refs_0_, bf16[128,512]{1,0:T(8,128)(2,1)S(1)} %get-tuple-element.40.refs_1_, bf16[128,384]{1,0:T(8,128)(2,1)S(1)} %collective-permute-done.9.refs_2_, bf16[128,384]{1,0:T(8,128)(2,1)S(1)} %collective-permute-done.10.refs_3_, ...), custom_call_target="tpu_custom_call" | custom-call | bytes 1048576 | tf_op jit(solution)/shard_map/join_heads/pallas_call | solution.py:485
  47.9 4.0 %build_cache.1 = bf16[4,40,2,3584]{3,2,1,0:T(2,128)(2,1)} custom-call(bf16[4,512,128]{2,1,0:T(8,128)(2,1)S(1)} %get-tuple-element.34.refs_11_.refs_0_, bf16[4,512,128]{2,1,0:T(8,128)(2,1)S(1)} %get-tuple-element.44.refs_1_, bf16[4,512,128]{2,1,0:T(8,128)(2,1)S(1)} %get-tuple-element.35.refs_12_.refs_2_, bf16[4,512,128]{2,1,0:T(8,128)(2,1)S(1)} %get-tuple-element.45.refs_3_, ...), custom_call_target="tpu_custom_call" | custom-call | flops 1174405120 | bytes 3670016 | tf_op jit(solution)/shard_map/build_cache/pallas_call | solution.py:450
  51.9 0.5 collective-permute-done.7.refs_1_
  52.4 0.8 %join_heads.3 = bf16[128,3584]{1,0:T(8,128)(2,1)} custom-call(bf16[128,512]{1,0:T(8,128)(2,1)S(1)} %collective-permute-done.6.refs_0_, bf16[128,512]{1,0:T(8,128)(2,1)S(1)} %collective-permute-done.7.refs_1_, bf16[128,512]{1,0:T(8,128)(2,1)S(1)} %collective-permute-done.8.refs_2_, bf16[128,3584]{1,0:T(8,128)(2,1)} %join_heads.2.refs_3_), custom_call_target="tpu_custom_call", output_to_operand_aliasing={{}: (3, {})} | custom-call | bytes 786432 | tf_op jit(solution)/shard_map/join_heads/pallas_call | solution.py:485
  (16 shorter events, 0.0 us)
Async XLA Ops:
  1.7 15.4 %collective-permute-start = (bf16[128,1792]{1,0:T(8,128)(2,1)S(1)}, bf16[128,1792]{1,0:T(8,128)(2,1)S(1)}, u32[]{:S(2)}, u32[]{:S(2)}) collective-permute-start(bf16[128,1792]{1,0:T(8,128)(2,1)S(1)} %pack_qkv.2._), channel_id=1, source_target_pairs={{0,3},{1,2},{2,1},{3,0},{4,7},{5,6},{6,5},{7,4},{8,11},{9,10},{10,... | collective-permute-start | bytes 1376264 | tf_op jit(solution)/shard_map/ppermute | solution.py:136
  9.8 24.8 %copy-start = (bf16[3,128,896]{2,1,0:T(8,128)(2,1)S(1)}, bf16[3,128,896]{2,1,0:T(8,128)(2,1)}, u32[]{:S(2)}) copy-start(bf16[3,128,896]{2,1,0:T(8,128)(2,1)} %refs_0_.3) | copy-start | bytes 2064388
  9.9 24.8 %copy-start.1 = (s32[8]{0:T(128)S(1)}, s32[8]{0:T(128)}, u32[]{:S(2)}) copy-start(s32[8]{0:T(128)} %refs_4_.1) | copy-start | bytes 100
  9.9 24.8 %copy-start.3 = (f32[4]{0:T(128)S(1)}, f32[4]{0:T(128)}, u32[]{:S(2)}) copy-start(f32[4]{0:T(128)} %refs_1_.3) | copy-start | bytes 52
  9.9 24.8 %collective-permute-start.2 = (bf16[128,1920]{1,0:T(8,128)(2,1)S(1)}, bf16[128,1920]{1,0:T(8,128)(2,1)S(1)}, u32[]{:S(2)}, u32[]{:S(2)}) collective-permute-start(bf16[128,1920]{1,0:T(8,128)(2,1)S(1)} %get-tuple-element.25), channel_id=1, source_target_pairs={{0,1},{1,0},{2,3},{3,2},{4,5},{5,4},{6,7},{7,6},{8,9},{9,8},{10,11... | collective-permute-start | bytes 1474568 | tf_op jit(solution)/shard_map/ppermute | solution.py:136
  10.5 24.2 %collective-permute-start.3 = (bf16[128,1920]{1,0:T(8,128)(2,1)S(1)}, bf16[128,1920]{1,0:T(8,128)(2,1)S(1)}, u32[]{:S(2)}, u32[]{:S(2)}) collective-permute-start(bf16[128,1920]{1,0:T(8,128)(2,1)S(1)} %get-tuple-element.26), channel_id=1, source_target_pairs={{0,2},{1,3},{2,0},{3,1},{4,6},{5,7},{6,4},{7,5},{8,10},{9,11},{10,... | collective-permute-start | bytes 1474568 | tf_op jit(solution)/shard_map/ppermute | solution.py:136
  10.5 24.1 %collective-permute-start.1 = (bf16[128,1280]{1,0:T(8,128)(2,1)S(1)}, bf16[128,1280]{1,0:T(8,128)(2,1)S(1)}, u32[]{:S(2)}, u32[]{:S(2)}) collective-permute-start(bf16[128,1280]{1,0:T(8,128)(2,1)S(1)} %get-tuple-element.24), channel_id=1, source_target_pairs={{0,3},{1,2},{2,1},{3,0},{4,7},{5,6},{6,5},{7,4},{8,11},{9,10},{10,... | collective-permute-start | bytes 983048 | tf_op jit(solution)/shard_map/ppermute | solution.py:136
  18.4 23.0 %collective-permute-start.4 = (bf16[128,1152]{1,0:T(8,128)(2,1)S(1)}, bf16[128,1152]{1,0:T(8,128)(2,1)S(1)}, u32[]{:S(2)}, u32[]{:S(2)}) collective-permute-start(bf16[128,1152]{1,0:T(8,128)(2,1)S(1)} %get-tuple-element.29), channel_id=1, source_target_pairs={{0,1},{1,0},{2,3},{3,2},{4,5},{5,4},{6,7},{7,6},{8,9},{9,8},{10,11... | collective-permute-start | bytes 884744 | tf_op jit(solution)/shard_map/ppermute | solution.py:136
  20.5 21.0 %collective-permute-start.5 = (bf16[128,1152]{1,0:T(8,128)(2,1)S(1)}, bf16[128,1152]{1,0:T(8,128)(2,1)S(1)}, u32[]{:S(2)}, u32[]{:S(2)}) collective-permute-start(bf16[128,1152]{1,0:T(8,128)(2,1)S(1)} %get-tuple-element.30), channel_id=1, source_target_pairs={{0,2},{1,3},{2,0},{3,1},{4,6},{5,7},{6,4},{7,5},{8,10},{9,11},{10,... | collective-permute-start | bytes 884744 | tf_op jit(solution)/shard_map/ppermute | solution.py:136
  37.4 9.2 %collective-permute-start.9 = (bf16[128,384]{1,0:T(8,128)(2,1)S(1)}, bf16[128,384]{1,0:T(8,128)(2,1)S(1)}, u32[]{:S(2)}, u32[]{:S(2)}) collective-permute-start(bf16[128,384]{1,0:T(8,128)(2,1)S(1)} %get-tuple-element.41), channel_id=1, source_target_pairs={{0,3},{1,2},{2,1},{3,0},{4,7},{5,6},{6,5},{7,4},{8,11},{9,10},{10,... | collective-permute-start | bytes 294920 | tf_op jit(solution)/shard_map/ppermute | solution.py:136
  40.4 6.7 %collective-permute-start.10 = (bf16[128,384]{1,0:T(8,128)(2,1)S(1)}, bf16[128,384]{1,0:T(8,128)(2,1)S(1)}, u32[]{:S(2)}, u32[]{:S(2)}) collective-permute-start(bf16[128,384]{1,0:T(8,128)(2,1)S(1)} %get-tuple-element.42), channel_id=1, source_target_pairs={{0,1},{1,0},{2,3},{3,2},{4,5},{5,4},{6,7},{7,6},{8,9},{9,8},{10,11... | collective-permute-start | bytes 294920 | tf_op jit(solution)/shard_map/ppermute | solution.py:136
  40.9 6.2 %collective-permute-start.11 = (bf16[128,384]{1,0:T(8,128)(2,1)S(1)}, bf16[128,384]{1,0:T(8,128)(2,1)S(1)}, u32[]{:S(2)}, u32[]{:S(2)}) collective-permute-start(bf16[128,384]{1,0:T(8,128)(2,1)S(1)} %get-tuple-element.43), channel_id=1, source_target_pairs={{0,2},{1,3},{2,0},{3,1},{4,6},{5,7},{6,4},{7,5},{8,10},{9,11},{10,... | collective-permute-start | bytes 294920 | tf_op jit(solution)/shard_map/ppermute | solution.py:136
  41.5 6.5 %copy-start.2 = (s32[8,24]{1,0:T(8,128)S(1)}, s32[8,24]{1,0:T(8,128)}, u32[]{:S(2)}) copy-start(s32[8,24]{1,0:T(8,128)} %refs_5_.1) | copy-start | bytes 2308
  43.5 8.4 %collective-permute-start.6 = (bf16[128,512]{1,0:T(8,128)(2,1)S(1)}, bf16[128,512]{1,0:T(8,128)(2,1)S(1)}, u32[]{:S(2)}, u32[]{:S(2)}) collective-permute-start(bf16[128,512]{1,0:T(8,128)(2,1)S(1)} %get-tuple-element.36), channel_id=1, source_target_pairs={{0,3},{1,2},{2,1},{3,0},{4,7},{5,6},{6,5},{7,4},{8,11},{9,10},{10,... | collective-permute-start | bytes 393224 | tf_op jit(solution)/shard_map/ppermute | solution.py:136
  46.1 6.4 %collective-permute-start.7 = (bf16[128,512]{1,0:T(8,128)(2,1)S(1)}, bf16[128,512]{1,0:T(8,128)(2,1)S(1)}, u32[]{:S(2)}, u32[]{:S(2)}) collective-permute-start(bf16[128,512]{1,0:T(8,128)(2,1)S(1)} %get-tuple-element.37), channel_id=1, source_target_pairs={{0,1},{1,0},{2,3},{3,2},{4,5},{5,4},{6,7},{7,6},{8,9},{9,8},{10,11... | collective-permute-start | bytes 393224 | tf_op jit(solution)/shard_map/ppermute | solution.py:136
  46.6 5.9 %collective-permute-start.8 = (bf16[128,512]{1,0:T(8,128)(2,1)S(1)}, bf16[128,512]{1,0:T(8,128)(2,1)S(1)}, u32[]{:S(2)}, u32[]{:S(2)}) collective-permute-start(bf16[128,512]{1,0:T(8,128)(2,1)S(1)} %get-tuple-element.38), channel_id=1, source_target_pairs={{0,2},{1,3},{2,0},{3,1},{4,6},{5,7},{6,4},{7,5},{8,10},{9,11},{10,... | collective-permute-start | bytes 393224 | tf_op jit(solution)/shard_map/ppermute | solution.py:136

commit v4 on v3

--- a/solution.py
+++ b/solution.py
@@ -543,7 +543,7 @@
         )
         begin = done_tiles[n][0] * LANES
         own.append((blocks[0], 0, begin))
-        back.append([(to_partner(blocks[bits], bits, group_size), bits, begin) for bits in partners])
+        back.append([(to_partner(blocks[bits], bits, group_size), bits, begin) for bits in [partners[2], partners[0], partners[1]]])
         keys, values = keys + [new_keys], values + [new_values]
     starts = [0, cut - done_cut]
     cache = build_cache(keys, values, starts, lengths, block_table)

time: 53.4 us -> 53.2 us (level)
  transfers between devices with their start and end apart: 12 -> 12, of which waited for: 4 -> 5; matrix products, arithmetic and copies ran while one was open for 0% -> 0% of each run, Pallas kernels for 28% -> 28%
where the time goes in v4:
time: 53.2 us; the launch traced here: 53.1 us
  starting transfers between devices  18.3 us (34%)
  waiting for transfers between devices  17.1 us (32%)
  Pallas kernels  16.8 us (32%)
  between operations  0.76 us (1%)
    ppermute x12, starting transfers between devices, to_partner(): lax.ppermute(values, 'seq', [(i, i ^ bits) for i in range(group_size)])  18.3 us
    ppermute x12, waiting for transfers between devices, to_partner(): lax.ppermute(values, 'seq', [(i, i ^ bits) for i in range(group_size)])  17.1 us
    pallas_call x2, Pallas kernels, attend(): pl.pallas_call(body, out_shape=out_shape, in_specs=[IN_VMEM, IN_SMEM, IN_...  4.7 us
    pallas_call x1, Pallas kernels, make_codes(): pl.pallas_call(body, out_shape=[jax.ShapeDtypeStruct((tok_rows, span + co...  4.15 us
    pallas_call x1, Pallas kernels, build_cache(): pl.pallas_call(body, out_shape=jax.ShapeDtypeStruct(cache, BF16), in_spec...  3.99 us
    pallas_call x2, Pallas kernels, pack_qkv(): pl.pallas_call(body, out_shape=[jax.ShapeDtypeStruct((tok_rows, span), BF...  2.41 us
    pallas_call x2, Pallas kernels, join_heads(): pl.pallas_call(body, out_shape=jax.ShapeDtypeStruct((tok_rows, width * gr...  1.59 us
  transfers between devices with their start and end apart: 12, of which 5 were waited for; matrix products, arithmetic and copies ran while one was open for 0% of the time, Pallas kernels for 28%

profile of v4, /device:TPU:0, one launch (start us, length us, event | category | flops | bytes accessed | tf_op | source)
XLA Modules:
  0.0 53.1 jit_solution(2076433338221367771)
XLA Ops:
  0.6 1.1 %pack_qkv.2._ = bf16[128,1792]{1,0:T(8,128)(2,1)S(1)} custom-call(bf16[128,10752]{1,0:T(8,128)(2,1)} %shared.5), custom_call_target="tpu_custom_call" | custom-call | bytes 917504 | tf_op jit(solution)/shard_map/pack_qkv/pallas_call | solution.py:240
  1.7 4.0 %collective-permute-start = (bf16[128,1792]{1,0:T(8,128)(2,1)S(1)}, bf16[128,1792]{1,0:T(8,128)(2,1)S(1)}, u32[]{:S(2)}, u32[]{:S(2)}) collective-permute-start(bf16[128,1792]{1,0:T(8,128)(2,1)S(1)} %pack_qkv.2._), channel_id=1, source_target_pairs={{0,3},{1,2},{2,1},{3,0},{4,7},{5,6},{6,5},{7,4},{8,11},{9,10},{10,... | collective-permute-start | bytes 1376264 | tf_op jit(solution)/shard_map/ppermute | solution.py:136
  5.7 4.2 %make_codes.1 = (bf16[128,1280]{1,0:T(8,128)(2,1)S(1)}, bf16[128,1920]{1,0:T(8,128)(2,1)S(1)}, bf16[128,1920]{1,0:T(8,128)(2,1)S(1)}, bf16[128,1920]{1,0:T(8,128)(2,1)S(1)}) custom-call(bf16[128,7168]{1,0:T(8,128)(2,1)} %inputs_ref.1, bf16[7168,384]{1,0:T(8,128)(2,1)} %down_ref.1, bf16[128,10752]{1,0:T(8,128)(2,1)} %shared.5, bf16[128,1792]{1,0:T(8,128)(2,1)S(1)} %pack_qkv.2._), custom_call_target="tpu_custom_call" | custom-call | flops 704643072 | bytes 5505024 | tf_op jit(solution)/shard_map/make_codes/pallas_call | solution.py:213
  9.9 0.6 %collective-permute-start.2 = (bf16[128,1920]{1,0:T(8,128)(2,1)S(1)}, bf16[128,1920]{1,0:T(8,128)(2,1)S(1)}, u32[]{:S(2)}, u32[]{:S(2)}) collective-permute-start(bf16[128,1920]{1,0:T(8,128)(2,1)S(1)} %get-tuple-element.25), channel_id=1, source_target_pairs={{0,1},{1,0},{2,3},{3,2},{4,5},{5,4},{6,7},{7,6},{8,9},{9,8},{10,11... | collective-permute-start | bytes 1474568 | tf_op jit(solution)/shard_map/ppermute | solution.py:136
  10.5 2.9 %collective-permute-start.1 = (bf16[128,1280]{1,0:T(8,128)(2,1)S(1)}, bf16[128,1280]{1,0:T(8,128)(2,1)S(1)}, u32[]{:S(2)}, u32[]{:S(2)}) collective-permute-start(bf16[128,1280]{1,0:T(8,128)(2,1)S(1)} %get-tuple-element.24), channel_id=1, source_target_pairs={{0,3},{1,2},{2,1},{3,0},{4,7},{5,6},{6,5},{7,4},{8,11},{9,10},{10,... | collective-permute-start | bytes 983048 | tf_op jit(solution)/shard_map/ppermute | solution.py:136
  13.4 3.6 %collective-permute-done.refs_3_.refs_1_.refs_4_ = bf16[128,1792]{1,0:T(8,128)(2,1)S(1)} collective-permute-done((bf16[128,1792]{1,0:T(8,128)(2,1)S(1)}, bf16[128,1792]{1,0:T(8,128)(2,1)S(1)}, u32[]{:S(2)}, u32[]{:S(2)}) %collective-permute-start) | collective-permute-done | bytes 458784 | tf_op jit(solution)/shard_map/ppermute | solution.py:136
  17.1 1.3 %pack_qkv.3 = (bf16[128,1152]{1,0:T(8,128)(2,1)S(1)}, bf16[128,1152]{1,0:T(8,128)(2,1)S(1)}, bf16[128,1152]{1,0:T(8,128)(2,1)S(1)}) custom-call(bf16[128,10752]{1,0:T(8,128)(2,1)} %shared.5, bf16[128,1920]{1,0:T(8,128)(2,1)S(1)} %get-tuple-element.27.refs_7_.refs_0_, bf16[128,1792]{1,0:T(8,128)(2,1)S(1)} %collective-permute-done.refs_3_.refs_1_.refs_4_), custom_call_target="tpu_custom_call" | custom-call | bytes 1769472 | tf_op jit(solution)/shard_map/pack_qkv/pallas_call | solution.py:240
  18.4 2.1 %collective-permute-start.4 = (bf16[128,1152]{1,0:T(8,128)(2,1)S(1)}, bf16[128,1152]{1,0:T(8,128)(2,1)S(1)}, u32[]{:S(2)}, u32[]{:S(2)}) collective-permute-start(bf16[128,1152]{1,0:T(8,128)(2,1)S(1)} %get-tuple-element.29), channel_id=1, source_target_pairs={{0,1},{1,0},{2,3},{3,2},{4,5},{5,4},{6,7},{7,6},{8,9},{9,8},{10,11... | collective-permute-start | bytes 884744 | tf_op jit(solution)/shard_map/ppermute | solution.py:136
  20.5 1.5 %collective-permute-start.5 = (bf16[128,1152]{1,0:T(8,128)(2,1)S(1)}, bf16[128,1152]{1,0:T(8,128)(2,1)S(1)}, u32[]{:S(2)}, u32[]{:S(2)}) collective-permute-start(bf16[128,1152]{1,0:T(8,128)(2,1)S(1)} %get-tuple-element.30), channel_id=1, source_target_pairs={{0,2},{1,3},{2,0},{3,1},{4,6},{5,7},{6,4},{7,5},{8,10},{9,11},{10,... | collective-permute-start | bytes 884744 | tf_op jit(solution)/shard_map/ppermute | solution.py:136
  22.0 12.7 %collective-permute-done.1.refs_4_.refs_5_ = bf16[128,1280]{1,0:T(8,128)(2,1)S(1)} collective-permute-done((bf16[128,1280]{1,0:T(8,128)(2,1)S(1)}, bf16[128,1280]{1,0:T(8,128)(2,1)S(1)}, u32[]{:S(2)}, u32[]{:S(2)}) %collective-permute-start.1) | collective-permute-done | bytes 327712 | tf_op jit(solution)/shard_map/ppermute | solution.py:136
  34.7 2.7 %attend.2 = (bf16[128,384]{1,0:T(8,128)(2,1)S(1)}, bf16[128,384]{1,0:T(8,128)(2,1)S(1)}, bf16[128,384]{1,0:T(8,128)(2,1)S(1)}, bf16[128,384]{1,0:T(8,128)(2,1)S(...) custom-call(bf16[3,128,896]{2,1,0:T(8,128)(2,1)S(1)} %copy-done, ...), custom_call_target="tpu_custom_call" | custom-call | flops 536870912 | bytes 4194304 | tf_op jit(solution)/shard_map/attend/pallas_call | solution.py:377
  37.4 2.1 %collective-permute-start.9 = (bf16[128,384]{1,0:T(8,128)(2,1)S(1)}, bf16[128,384]{1,0:T(8,128)(2,1)S(1)}, u32[]{:S(2)}, u32[]{:S(2)}) collective-permute-start(bf16[128,384]{1,0:T(8,128)(2,1)S(1)} %get-tuple-element.41), channel_id=1, source_target_pairs={{0,2},{1,3},{2,0},{3,1},{4,6},{5,7},{6,4},{7,5},{8,10},{9,11},{10,... | collective-permute-start | bytes 294920 | tf_op jit(solution)/shard_map/ppermute | solution.py:136
  39.5 1.4 %collective-permute-start.10 = (bf16[128,384]{1,0:T(8,128)(2,1)S(1)}, bf16[128,384]{1,0:T(8,128)(2,1)S(1)}, u32[]{:S(2)}, u32[]{:S(2)}) collective-permute-start(bf16[128,384]{1,0:T(8,128)(2,1)S(1)} %get-tuple-element.42), channel_id=1, source_target_pairs={{0,3},{1,2},{2,1},{3,0},{4,7},{5,6},{6,5},{7,4},{8,11},{9,10},{10,... | collective-permute-start | bytes 294920 | tf_op jit(solution)/shard_map/ppermute | solution.py:136
  40.9 0.1 collective-permute-start.11
  41.0 0.1 collective-permute-done.4.refs_6_
  41.1 2.1 %attend.3 = (bf16[128,512]{1,0:T(8,128)(2,1)S(1)}, bf16[128,512]{1,0:T(8,128)(2,1)S(1)}, bf16[128,512]{1,0:T(8,128)(2,1)S(1)}, bf16[128,512]{1,0:T(8,128)(2,1)S(...) custom-call(bf16[3,128,896]{2,1,0:T(8,128)(2,1)S(1)} %copy-done, f32[4]{0:T(128)S(1)} %copy-done.3, ...), custom_call_target="tpu_custom_call" | custom-call | flops 402653184 | bytes 3145728 | tf_op jit(solution)/shard_map/attend/pallas_call | solution.py:377
  43.2 1.9 %collective-permute-start.6 = (bf16[128,512]{1,0:T(8,128)(2,1)S(1)}, bf16[128,512]{1,0:T(8,128)(2,1)S(1)}, u32[]{:S(2)}, u32[]{:S(2)}) collective-permute-start(bf16[128,512]{1,0:T(8,128)(2,1)S(1)} %get-tuple-element.36), channel_id=1, source_target_pairs={{0,2},{1,3},{2,0},{3,1},{4,6},{5,7},{6,4},{7,5},{8,10},{9,11},{10,... | collective-permute-start | bytes 393224 | tf_op jit(solution)/shard_map/ppermute | solution.py:136
  45.1 1.4 %collective-permute-start.7 = (bf16[128,512]{1,0:T(8,128)(2,1)S(1)}, bf16[128,512]{1,0:T(8,128)(2,1)S(1)}, u32[]{:S(2)}, u32[]{:S(2)}) collective-permute-start(bf16[128,512]{1,0:T(8,128)(2,1)S(1)} %get-tuple-element.37), channel_id=1, source_target_pairs={{0,3},{1,2},{2,1},{3,0},{4,7},{5,6},{6,5},{7,4},{8,11},{9,10},{10,... | collective-permute-start | bytes 393224 | tf_op jit(solution)/shard_map/ppermute | solution.py:136
  46.5 0.2 collective-permute-start.8
  46.7 0.8 %join_heads.2.refs_3_ = bf16[128,3584]{1,0:T(8,128)(2,1)} custom-call(bf16[128,384]{1,0:T(8,128)(2,1)S(1)} %get-tuple-element.39.refs_0_, bf16[128,512]{1,0:T(8,128)(2,1)S(1)} %get-tuple-element.40.refs_1_, bf16[128,384]{1,0:T(8,128)(2,1)S(1)} %collective-permute-done.9.refs_2_, bf16[128,384]{1,0:T(8,128)(2,1)S(1)} %collective-permute-done.10.refs_3_, ...), custom_call_target="tpu_custom_call" | custom-call | bytes 1048576 | tf_op jit(solution)/shard_map/join_heads/pallas_call | solution.py:485
  47.6 4.0 %build_cache.1 = bf16[4,40,2,3584]{3,2,1,0:T(2,128)(2,1)} custom-call(bf16[4,512,128]{2,1,0:T(8,128)(2,1)S(1)} %get-tuple-element.34.refs_11_.refs_0_, bf16[4,512,128]{2,1,0:T(8,128)(2,1)S(1)} %get-tuple-element.44.refs_1_, bf16[4,512,128]{2,1,0:T(8,128)(2,1)S(1)} %get-tuple-element.35.refs_12_.refs_2_, bf16[4,512,128]{2,1,0:T(8,128)(2,1)S(1)} %get-tuple-element.45.refs_3_, ...), custom_call_target="tpu_custom_call" | custom-call | flops 1174405120 | bytes 3670016 | tf_op jit(solution)/shard_map/build_cache/pallas_call | solution.py:450
  51.6 0.3 collective-permute-done.7.refs_1_
  51.9 0.4 collective-permute-done.8.refs_2_
  52.3 0.8 %join_heads.3 = bf16[128,3584]{1,0:T(8,128)(2,1)} custom-call(bf16[128,512]{1,0:T(8,128)(2,1)S(1)} %collective-permute-done.6.refs_0_, bf16[128,512]{1,0:T(8,128)(2,1)S(1)} %collective-permute-done.7.refs_1_, bf16[128,512]{1,0:T(8,128)(2,1)S(1)} %collective-permute-done.8.refs_2_, bf16[128,3584]{1,0:T(8,128)(2,1)} %join_heads.2.refs_3_), custom_call_target="tpu_custom_call", output_to_operand_aliasing={{}: (3, {})} | custom-call | bytes 786432 | tf_op jit(solution)/shard_map/join_heads/pallas_call | solution.py:485
  (16 shorter events, 0.1 us)
Async XLA Ops:
  1.7 15.4 %collective-permute-start = (bf16[128,1792]{1,0:T(8,128)(2,1)S(1)}, bf16[128,1792]{1,0:T(8,128)(2,1)S(1)}, u32[]{:S(2)}, u32[]{:S(2)}) collective-permute-start(bf16[128,1792]{1,0:T(8,128)(2,1)S(1)} %pack_qkv.2._), channel_id=1, source_target_pairs={{0,3},{1,2},{2,1},{3,0},{4,7},{5,6},{6,5},{7,4},{8,11},{9,10},{10,... | collective-permute-start | bytes 1376264 | tf_op jit(solution)/shard_map/ppermute | solution.py:136
  9.8 24.8 %copy-start = (bf16[3,128,896]{2,1,0:T(8,128)(2,1)S(1)}, bf16[3,128,896]{2,1,0:T(8,128)(2,1)}, u32[]{:S(2)}) copy-start(bf16[3,128,896]{2,1,0:T(8,128)(2,1)} %refs_0_.3) | copy-start | bytes 2064388
  9.9 24.8 %copy-start.1 = (s32[8]{0:T(128)S(1)}, s32[8]{0:T(128)}, u32[]{:S(2)}) copy-start(s32[8]{0:T(128)} %refs_4_.1) | copy-start | bytes 100
  9.9 24.8 %copy-start.3 = (f32[4]{0:T(128)S(1)}, f32[4]{0:T(128)}, u32[]{:S(2)}) copy-start(f32[4]{0:T(128)} %refs_1_.3) | copy-start | bytes 52
  9.9 24.8 %collective-permute-start.2 = (bf16[128,1920]{1,0:T(8,128)(2,1)S(1)}, bf16[128,1920]{1,0:T(8,128)(2,1)S(1)}, u32[]{:S(2)}, u32[]{:S(2)}) collective-permute-start(bf16[128,1920]{1,0:T(8,128)(2,1)S(1)} %get-tuple-element.25), channel_id=1, source_target_pairs={{0,1},{1,0},{2,3},{3,2},{4,5},{5,4},{6,7},{7,6},{8,9},{9,8},{10,11... | collective-permute-start | bytes 1474568 | tf_op jit(solution)/shard_map/ppermute | solution.py:136
  10.5 24.2 %collective-permute-start.3 = (bf16[128,1920]{1,0:T(8,128)(2,1)S(1)}, bf16[128,1920]{1,0:T(8,128)(2,1)S(1)}, u32[]{:S(2)}, u32[]{:S(2)}) collective-permute-start(bf16[128,1920]{1,0:T(8,128)(2,1)S(1)} %get-tuple-element.26), channel_id=1, source_target_pairs={{0,2},{1,3},{2,0},{3,1},{4,6},{5,7},{6,4},{7,5},{8,10},{9,11},{10,... | collective-permute-start | bytes 1474568 | tf_op jit(solution)/shard_map/ppermute | solution.py:136
  10.5 24.1 %collective-permute-start.1 = (bf16[128,1280]{1,0:T(8,128)(2,1)S(1)}, bf16[128,1280]{1,0:T(8,128)(2,1)S(1)}, u32[]{:S(2)}, u32[]{:S(2)}) collective-permute-start(bf16[128,1280]{1,0:T(8,128)(2,1)S(1)} %get-tuple-element.24), channel_id=1, source_target_pairs={{0,3},{1,2},{2,1},{3,0},{4,7},{5,6},{6,5},{7,4},{8,11},{9,10},{10,... | collective-permute-start | bytes 983048 | tf_op jit(solution)/shard_map/ppermute | solution.py:136
  18.4 22.7 %collective-permute-start.4 = (bf16[128,1152]{1,0:T(8,128)(2,1)S(1)}, bf16[128,1152]{1,0:T(8,128)(2,1)S(1)}, u32[]{:S(2)}, u32[]{:S(2)}) collective-permute-start(bf16[128,1152]{1,0:T(8,128)(2,1)S(1)} %get-tuple-element.29), channel_id=1, source_target_pairs={{0,1},{1,0},{2,3},{3,2},{4,5},{5,4},{6,7},{7,6},{8,9},{9,8},{10,11... | collective-permute-start | bytes 884744 | tf_op jit(solution)/shard_map/ppermute | solution.py:136
  20.5 20.6 %collective-permute-start.5 = (bf16[128,1152]{1,0:T(8,128)(2,1)S(1)}, bf16[128,1152]{1,0:T(8,128)(2,1)S(1)}, u32[]{:S(2)}, u32[]{:S(2)}) collective-permute-start(bf16[128,1152]{1,0:T(8,128)(2,1)S(1)} %get-tuple-element.30), channel_id=1, source_target_pairs={{0,2},{1,3},{2,0},{3,1},{4,6},{5,7},{6,4},{7,5},{8,10},{9,11},{10,... | collective-permute-start | bytes 884744 | tf_op jit(solution)/shard_map/ppermute | solution.py:136
  37.4 9.2 %collective-permute-start.9 = (bf16[128,384]{1,0:T(8,128)(2,1)S(1)}, bf16[128,384]{1,0:T(8,128)(2,1)S(1)}, u32[]{:S(2)}, u32[]{:S(2)}) collective-permute-start(bf16[128,384]{1,0:T(8,128)(2,1)S(1)} %get-tuple-element.41), channel_id=1, source_target_pairs={{0,2},{1,3},{2,0},{3,1},{4,6},{5,7},{6,4},{7,5},{8,10},{9,11},{10,... | collective-permute-start | bytes 294920 | tf_op jit(solution)/shard_map/ppermute | solution.py:136
  39.5 7.3 %collective-permute-start.10 = (bf16[128,384]{1,0:T(8,128)(2,1)S(1)}, bf16[128,384]{1,0:T(8,128)(2,1)S(1)}, u32[]{:S(2)}, u32[]{:S(2)}) collective-permute-start(bf16[128,384]{1,0:T(8,128)(2,1)S(1)} %get-tuple-element.42), channel_id=1, source_target_pairs={{0,3},{1,2},{2,1},{3,0},{4,7},{5,6},{6,5},{7,4},{8,11},{9,10},{10,... | collective-permute-start | bytes 294920 | tf_op jit(solution)/shard_map/ppermute | solution.py:136
  40.9 5.8 %collective-permute-start.11 = (bf16[128,384]{1,0:T(8,128)(2,1)S(1)}, bf16[128,384]{1,0:T(8,128)(2,1)S(1)}, u32[]{:S(2)}, u32[]{:S(2)}) collective-permute-start(bf16[128,384]{1,0:T(8,128)(2,1)S(1)} %get-tuple-element.43), channel_id=1, source_target_pairs={{0,1},{1,0},{2,3},{3,2},{4,5},{5,4},{6,7},{7,6},{8,9},{9,8},{10,11... | collective-permute-start | bytes 294920 | tf_op jit(solution)/shard_map/ppermute | solution.py:136
  41.1 6.5 %copy-start.2 = (s32[8,24]{1,0:T(8,128)S(1)}, s32[8,24]{1,0:T(8,128)}, u32[]{:S(2)}) copy-start(s32[8,24]{1,0:T(8,128)} %refs_5_.1) | copy-start | bytes 2308
  43.2 8.4 %collective-permute-start.6 = (bf16[128,512]{1,0:T(8,128)(2,1)S(1)}, bf16[128,512]{1,0:T(8,128)(2,1)S(1)}, u32[]{:S(2)}, u32[]{:S(2)}) collective-permute-start(bf16[128,512]{1,0:T(8,128)(2,1)S(1)} %get-tuple-element.36), channel_id=1, source_target_pairs={{0,2},{1,3},{2,0},{3,1},{4,6},{5,7},{6,4},{7,5},{8,10},{9,11},{10,... | collective-permute-start | bytes 393224 | tf_op jit(solution)/shard_map/ppermute | solution.py:136
  45.1 6.8 %collective-permute-start.7 = (bf16[128,512]{1,0:T(8,128)(2,1)S(1)}, bf16[128,512]{1,0:T(8,128)(2,1)S(1)}, u32[]{:S(2)}, u32[]{:S(2)}) collective-permute-start(bf16[128,512]{1,0:T(8,128)(2,1)S(1)} %get-tuple-element.37), channel_id=1, source_target_pairs={{0,3},{1,2},{2,1},{3,0},{4,7},{5,6},{6,5},{7,4},{8,11},{9,10},{10,... | collective-permute-start | bytes 393224 | tf_op jit(solution)/shard_map/ppermute | solution.py:136
  46.5 5.8 %collective-permute-start.8 = (bf16[128,512]{1,0:T(8,128)(2,1)S(1)}, bf16[128,512]{1,0:T(8,128)(2,1)S(1)}, u32[]{:S(2)}, u32[]{:S(2)}) collective-permute-start(bf16[128,512]{1,0:T(8,128)(2,1)S(1)} %get-tuple-element.38), channel_id=1, source_target_pairs={{0,1},{1,0},{2,3},{3,2},{4,5},{5,4},{6,7},{7,6},{8,9},{9,8},{10,11... | collective-permute-start | bytes 393224 | tf_op jit(solution)/shard_map/ppermute | solution.py:136

commit v5 on v4

--- a/solution.py
+++ b/solution.py
@@ -543,7 +543,7 @@
         )
         begin = done_tiles[n][0] * LANES
         own.append((blocks[0], 0, begin))
-        back.append([(to_partner(blocks[bits], bits, group_size), bits, begin) for bits in [partners[2], partners[0], partners[1]]])
+        back.append([(to_partner(blocks[bits], bits, group_size), bits, begin) for bits in ([partners[i] for i in ((2, 0, 1) if n else (2, 1, 0))])])
         keys, values = keys + [new_keys], values + [new_values]
     starts = [0, cut - done_cut]
     cache = build_cache(keys, values, starts, lengths, block_table)

time: 53.2 us -> 52.6 us (0.989)
  waiting for transfers between devices: 17.1 us -> 16.5 us
    ppermute x12, waiting for transfers between devices: 17.1 us -> 16.5 us  [to_partner(): lax.ppermute(values, 'seq', [(i, i ^ bits) for i in range(group_size)])]
  transfers between devices with their start and end apart: 12 -> 12, of which waited for: 5 -> 3; matrix products, arithmetic and copies ran while one was open for 0% -> 0% of each run, Pallas kernels for 28% -> 29%
where the time goes in v5:
time: 52.6 us; the launch traced here: 52.5 us
  starting transfers between devices  18.3 us (35%)
  Pallas kernels  16.8 us (32%)
  waiting for transfers between devices  16.5 us (31%)
  between operations  0.76 us (1%)
    ppermute x12, starting transfers between devices, to_partner(): lax.ppermute(values, 'seq', [(i, i ^ bits) for i in range(group_size)])  18.3 us
    ppermute x12, waiting for transfers between devices, to_partner(): lax.ppermute(values, 'seq', [(i, i ^ bits) for i in range(group_size)])  16.5 us
    pallas_call x2, Pallas kernels, attend(): pl.pallas_call(body, out_shape=out_shape, in_specs=[IN_VMEM, IN_SMEM, IN_...  4.7 us
    pallas_call x1, Pallas kernels, make_codes(): pl.pallas_call(body, out_shape=[jax.ShapeDtypeStruct((tok_rows, span + co...  4.15 us
    pallas_call x1, Pallas kernels, build_cache(): pl.pallas_call(body, out_shape=jax.ShapeDtypeStruct(cache, BF16), in_spec...  3.99 us
    pallas_call x2, Pallas kernels, pack_qkv(): pl.pallas_call(body, out_shape=[jax.ShapeDtypeStruct((tok_rows, span), BF...  2.41 us
    pallas_call x2, Pallas kernels, join_heads(): pl.pallas_call(body, out_shape=jax.ShapeDtypeStruct((tok_rows, width * gr...  1.59 us
  transfers between devices with their start and end apart: 12, of which 3 were waited for; matrix products, arithmetic and copies ran while one was open for 0% of the time, Pallas kernels for 29%

profile of v5, /device:TPU:0, one launch (start us, length us, event | category | flops | bytes accessed | tf_op | source)
XLA Modules:
  0.0 52.5 jit_solution(4779295957874405006)
XLA Ops:
  0.6 1.1 %pack_qkv.2._ = bf16[128,1792]{1,0:T(8,128)(2,1)S(1)} custom-call(bf16[128,10752]{1,0:T(8,128)(2,1)} %shared.5), custom_call_target="tpu_custom_call" | custom-call | bytes 917504 | tf_op jit(solution)/shard_map/pack_qkv/pallas_call | solution.py:240
  1.7 4.0 %collective-permute-start = (bf16[128,1792]{1,0:T(8,128)(2,1)S(1)}, bf16[128,1792]{1,0:T(8,128)(2,1)S(1)}, u32[]{:S(2)}, u32[]{:S(2)}) collective-permute-start(bf16[128,1792]{1,0:T(8,128)(2,1)S(1)} %pack_qkv.2._), channel_id=1, source_target_pairs={{0,3},{1,2},{2,1},{3,0},{4,7},{5,6},{6,5},{7,4},{8,11},{9,10},{10,... | collective-permute-start | bytes 1376264 | tf_op jit(solution)/shard_map/ppermute | solution.py:136
  5.7 4.2 %make_codes.1 = (bf16[128,1280]{1,0:T(8,128)(2,1)S(1)}, bf16[128,1920]{1,0:T(8,128)(2,1)S(1)}, bf16[128,1920]{1,0:T(8,128)(2,1)S(1)}, bf16[128,1920]{1,0:T(8,128)(2,1)S(1)}) custom-call(bf16[128,7168]{1,0:T(8,128)(2,1)} %inputs_ref.1, bf16[7168,384]{1,0:T(8,128)(2,1)} %down_ref.1, bf16[128,10752]{1,0:T(8,128)(2,1)} %shared.5, bf16[128,1792]{1,0:T(8,128)(2,1)S(1)} %pack_qkv.2._), custom_call_target="tpu_custom_call" | custom-call | flops 704643072 | bytes 5505024 | tf_op jit(solution)/shard_map/make_codes/pallas_call | solution.py:213
  9.9 0.6 %collective-permute-start.2 = (bf16[128,1920]{1,0:T(8,128)(2,1)S(1)}, bf16[128,1920]{1,0:T(8,128)(2,1)S(1)}, u32[]{:S(2)}, u32[]{:S(2)}) collective-permute-start(bf16[128,1920]{1,0:T(8,128)(2,1)S(1)} %get-tuple-element.25), channel_id=1, source_target_pairs={{0,1},{1,0},{2,3},{3,2},{4,5},{5,4},{6,7},{7,6},{8,9},{9,8},{10,11... | collective-permute-start | bytes 1474568 | tf_op jit(solution)/shard_map/ppermute | solution.py:136
  10.5 0.1 collective-permute-start.3
  10.5 2.9 %collective-permute-start.1 = (bf16[128,1280]{1,0:T(8,128)(2,1)S(1)}, bf16[128,1280]{1,0:T(8,128)(2,1)S(1)}, u32[]{:S(2)}, u32[]{:S(2)}) collective-permute-start(bf16[128,1280]{1,0:T(8,128)(2,1)S(1)} %get-tuple-element.24), channel_id=1, source_target_pairs={{0,3},{1,2},{2,1},{3,0},{4,7},{5,6},{6,5},{7,4},{8,11},{9,10},{10,... | collective-permute-start | bytes 983048 | tf_op jit(solution)/shard_map/ppermute | solution.py:136
  13.4 3.6 %collective-permute-done.refs_3_.refs_1_.refs_4_ = bf16[128,1792]{1,0:T(8,128)(2,1)S(1)} collective-permute-done((bf16[128,1792]{1,0:T(8,128)(2,1)S(1)}, bf16[128,1792]{1,0:T(8,128)(2,1)S(1)}, u32[]{:S(2)}, u32[]{:S(2)}) %collective-permute-start) | collective-permute-done | bytes 458784 | tf_op jit(solution)/shard_map/ppermute | solution.py:136
  17.1 1.3 %pack_qkv.3 = (bf16[128,1152]{1,0:T(8,128)(2,1)S(1)}, bf16[128,1152]{1,0:T(8,128)(2,1)S(1)}, bf16[128,1152]{1,0:T(8,128)(2,1)S(1)}) custom-call(bf16[128,10752]{1,0:T(8,128)(2,1)} %shared.5, bf16[128,1920]{1,0:T(8,128)(2,1)S(1)} %get-tuple-element.27.refs_7_.refs_0_, bf16[128,1792]{1,0:T(8,128)(2,1)S(1)} %collective-permute-done.refs_3_.refs_1_.refs_4_), custom_call_target="tpu_custom_call" | custom-call | bytes 1769472 | tf_op jit(solution)/shard_map/pack_qkv/pallas_call | solution.py:240
  18.4 2.1 %collective-permute-start.4 = (bf16[128,1152]{1,0:T(8,128)(2,1)S(1)}, bf16[128,1152]{1,0:T(8,128)(2,1)S(1)}, u32[]{:S(2)}, u32[]{:S(2)}) collective-permute-start(bf16[128,1152]{1,0:T(8,128)(2,1)S(1)} %get-tuple-element.29), channel_id=1, source_target_pairs={{0,1},{1,0},{2,3},{3,2},{4,5},{5,4},{6,7},{7,6},{8,9},{9,8},{10,11... | collective-permute-start | bytes 884744 | tf_op jit(solution)/shard_map/ppermute | solution.py:136
  20.5 1.5 %collective-permute-start.5 = (bf16[128,1152]{1,0:T(8,128)(2,1)S(1)}, bf16[128,1152]{1,0:T(8,128)(2,1)S(1)}, u32[]{:S(2)}, u32[]{:S(2)}) collective-permute-start(bf16[128,1152]{1,0:T(8,128)(2,1)S(1)} %get-tuple-element.30), channel_id=1, source_target_pairs={{0,2},{1,3},{2,0},{3,1},{4,6},{5,7},{6,4},{7,5},{8,10},{9,11},{10,... | collective-permute-start | bytes 884744 | tf_op jit(solution)/shard_map/ppermute | solution.py:136
  22.0 12.7 %collective-permute-done.1.refs_4_.refs_5_ = bf16[128,1280]{1,0:T(8,128)(2,1)S(1)} collective-permute-done((bf16[128,1280]{1,0:T(8,128)(2,1)S(1)}, bf16[128,1280]{1,0:T(8,128)(2,1)S(1)}, u32[]{:S(2)}, u32[]{:S(2)}) %collective-permute-start.1) | collective-permute-done | bytes 327712 | tf_op jit(solution)/shard_map/ppermute | solution.py:136
  34.7 2.7 %attend.2 = (bf16[128,384]{1,0:T(8,128)(2,1)S(1)}, bf16[128,384]{1,0:T(8,128)(2,1)S(1)}, bf16[128,384]{1,0:T(8,128)(2,1)S(1)}, bf16[128,384]{1,0:T(8,128)(2,1)S(...) custom-call(bf16[3,128,896]{2,1,0:T(8,128)(2,1)S(1)} %copy-done, ...), custom_call_target="tpu_custom_call" | custom-call | flops 536870912 | bytes 4194304 | tf_op jit(solution)/shard_map/attend/pallas_call | solution.py:377
  37.4 2.1 %collective-permute-start.9 = (bf16[128,384]{1,0:T(8,128)(2,1)S(1)}, bf16[128,384]{1,0:T(8,128)(2,1)S(1)}, u32[]{:S(2)}, u32[]{:S(2)}) collective-permute-start(bf16[128,384]{1,0:T(8,128)(2,1)S(1)} %get-tuple-element.41), channel_id=1, source_target_pairs={{0,2},{1,3},{2,0},{3,1},{4,6},{5,7},{6,4},{7,5},{8,10},{9,11},{10,... | collective-permute-start | bytes 294920 | tf_op jit(solution)/shard_map/ppermute | solution.py:136
  39.5 1.5 %collective-permute-start.10 = (bf16[128,384]{1,0:T(8,128)(2,1)S(1)}, bf16[128,384]{1,0:T(8,128)(2,1)S(1)}, u32[]{:S(2)}, u32[]{:S(2)}) collective-permute-start(bf16[128,384]{1,0:T(8,128)(2,1)S(1)} %get-tuple-element.42), channel_id=1, source_target_pairs={{0,1},{1,0},{2,3},{3,2},{4,5},{5,4},{6,7},{7,6},{8,9},{9,8},{10,11... | collective-permute-start | bytes 294920 | tf_op jit(solution)/shard_map/ppermute | solution.py:136
  41.0 0.0 collective-permute-start.11
  41.0 0.2 collective-permute-done.4.refs_6_
  41.2 2.1 %attend.3 = (bf16[128,512]{1,0:T(8,128)(2,1)S(1)}, bf16[128,512]{1,0:T(8,128)(2,1)S(1)}, bf16[128,512]{1,0:T(8,128)(2,1)S(1)}, bf16[128,512]{1,0:T(8,128)(2,1)S(...) custom-call(bf16[3,128,896]{2,1,0:T(8,128)(2,1)S(1)} %copy-done, f32[4]{0:T(128)S(1)} %copy-done.3, ...), custom_call_target="tpu_custom_call" | custom-call | flops 402653184 | bytes 3145728 | tf_op jit(solution)/shard_map/attend/pallas_call | solution.py:377
  43.2 1.9 %collective-permute-start.6 = (bf16[128,512]{1,0:T(8,128)(2,1)S(1)}, bf16[128,512]{1,0:T(8,128)(2,1)S(1)}, u32[]{:S(2)}, u32[]{:S(2)}) collective-permute-start(bf16[128,512]{1,0:T(8,128)(2,1)S(1)} %get-tuple-element.36), channel_id=1, source_target_pairs={{0,2},{1,3},{2,0},{3,1},{4,6},{5,7},{6,4},{7,5},{8,10},{9,11},{10,... | collective-permute-start | bytes 393224 | tf_op jit(solution)/shard_map/ppermute | solution.py:136
  45.1 1.4 %collective-permute-start.7 = (bf16[128,512]{1,0:T(8,128)(2,1)S(1)}, bf16[128,512]{1,0:T(8,128)(2,1)S(1)}, u32[]{:S(2)}, u32[]{:S(2)}) collective-permute-start(bf16[128,512]{1,0:T(8,128)(2,1)S(1)} %get-tuple-element.37), channel_id=1, source_target_pairs={{0,3},{1,2},{2,1},{3,0},{4,7},{5,6},{6,5},{7,4},{8,11},{9,10},{10,... | collective-permute-start | bytes 393224 | tf_op jit(solution)/shard_map/ppermute | solution.py:136
  46.5 0.3 collective-permute-start.8
  46.8 0.8 %join_heads.2.refs_3_ = bf16[128,3584]{1,0:T(8,128)(2,1)} custom-call(bf16[128,384]{1,0:T(8,128)(2,1)S(1)} %get-tuple-element.39.refs_0_, bf16[128,512]{1,0:T(8,128)(2,1)S(1)} %get-tuple-element.40.refs_1_, bf16[128,384]{1,0:T(8,128)(2,1)S(1)} %collective-permute-done.9.refs_2_, bf16[128,384]{1,0:T(8,128)(2,1)S(1)} %collective-permute-done.10.refs_3_, ...), custom_call_target="tpu_custom_call" | custom-call | bytes 1048576 | tf_op jit(solution)/shard_map/join_heads/pallas_call | solution.py:485
  47.6 4.0 %build_cache.1 = bf16[4,40,2,3584]{3,2,1,0:T(2,128)(2,1)} custom-call(bf16[4,512,128]{2,1,0:T(8,128)(2,1)S(1)} %get-tuple-element.34.refs_11_.refs_0_, bf16[4,512,128]{2,1,0:T(8,128)(2,1)S(1)} %get-tuple-element.44.refs_1_, bf16[4,512,128]{2,1,0:T(8,128)(2,1)S(1)} %get-tuple-element.35.refs_12_.refs_2_, bf16[4,512,128]{2,1,0:T(8,128)(2,1)S(1)} %get-tuple-element.45.refs_3_, ...), custom_call_target="tpu_custom_call" | custom-call | flops 1174405120 | bytes 3670016 | tf_op jit(solution)/shard_map/build_cache/pallas_call | solution.py:450
  51.7 0.0 collective-permute-done.8.refs_2_
  51.7 0.8 %join_heads.3 = bf16[128,3584]{1,0:T(8,128)(2,1)} custom-call(bf16[128,512]{1,0:T(8,128)(2,1)S(1)} %collective-permute-done.6.refs_0_, bf16[128,512]{1,0:T(8,128)(2,1)S(1)} %collective-permute-done.7.refs_1_, bf16[128,512]{1,0:T(8,128)(2,1)S(1)} %collective-permute-done.8.refs_2_, bf16[128,3584]{1,0:T(8,128)(2,1)} %join_heads.2.refs_3_), custom_call_target="tpu_custom_call", output_to_operand_aliasing={{}: (3, {})} | custom-call | bytes 786432 | tf_op jit(solution)/shard_map/join_heads/pallas_call | solution.py:485
  (16 shorter events, 0.0 us)
Async XLA Ops:
  1.7 15.4 %collective-permute-start = (bf16[128,1792]{1,0:T(8,128)(2,1)S(1)}, bf16[128,1792]{1,0:T(8,128)(2,1)S(1)}, u32[]{:S(2)}, u32[]{:S(2)}) collective-permute-start(bf16[128,1792]{1,0:T(8,128)(2,1)S(1)} %pack_qkv.2._), channel_id=1, source_target_pairs={{0,3},{1,2},{2,1},{3,0},{4,7},{5,6},{6,5},{7,4},{8,11},{9,10},{10,... | collective-permute-start | bytes 1376264 | tf_op jit(solution)/shard_map/ppermute | solution.py:136
  9.8 24.8 %copy-start = (bf16[3,128,896]{2,1,0:T(8,128)(2,1)S(1)}, bf16[3,128,896]{2,1,0:T(8,128)(2,1)}, u32[]{:S(2)}) copy-start(bf16[3,128,896]{2,1,0:T(8,128)(2,1)} %refs_0_.3) | copy-start | bytes 2064388
  9.9 24.8 %copy-start.1 = (s32[8]{0:T(128)S(1)}, s32[8]{0:T(128)}, u32[]{:S(2)}) copy-start(s32[8]{0:T(128)} %refs_4_.1) | copy-start | bytes 100
  9.9 24.8 %copy-start.3 = (f32[4]{0:T(128)S(1)}, f32[4]{0:T(128)}, u32[]{:S(2)}) copy-start(f32[4]{0:T(128)} %refs_1_.3) | copy-start | bytes 52
  9.9 24.8 %collective-permute-start.2 = (bf16[128,1920]{1,0:T(8,128)(2,1)S(1)}, bf16[128,1920]{1,0:T(8,128)(2,1)S(1)}, u32[]{:S(2)}, u32[]{:S(2)}) collective-permute-start(bf16[128,1920]{1,0:T(8,128)(2,1)S(1)} %get-tuple-element.25), channel_id=1, source_target_pairs={{0,1},{1,0},{2,3},{3,2},{4,5},{5,4},{6,7},{7,6},{8,9},{9,8},{10,11... | collective-permute-start | bytes 1474568 | tf_op jit(solution)/shard_map/ppermute | solution.py:136
  10.5 24.2 %collective-permute-start.3 = (bf16[128,1920]{1,0:T(8,128)(2,1)S(1)}, bf16[128,1920]{1,0:T(8,128)(2,1)S(1)}, u32[]{:S(2)}, u32[]{:S(2)}) collective-permute-start(bf16[128,1920]{1,0:T(8,128)(2,1)S(1)} %get-tuple-element.26), channel_id=1, source_target_pairs={{0,2},{1,3},{2,0},{3,1},{4,6},{5,7},{6,4},{7,5},{8,10},{9,11},{10,... | collective-permute-start | bytes 1474568 | tf_op jit(solution)/shard_map/ppermute | solution.py:136
  10.5 24.1 %collective-permute-start.1 = (bf16[128,1280]{1,0:T(8,128)(2,1)S(1)}, bf16[128,1280]{1,0:T(8,128)(2,1)S(1)}, u32[]{:S(2)}, u32[]{:S(2)}) collective-permute-start(bf16[128,1280]{1,0:T(8,128)(2,1)S(1)} %get-tuple-element.24), channel_id=1, source_target_pairs={{0,3},{1,2},{2,1},{3,0},{4,7},{5,6},{6,5},{7,4},{8,11},{9,10},{10,... | collective-permute-start | bytes 983048 | tf_op jit(solution)/shard_map/ppermute | solution.py:136
  18.4 22.8 %collective-permute-start.4 = (bf16[128,1152]{1,0:T(8,128)(2,1)S(1)}, bf16[128,1152]{1,0:T(8,128)(2,1)S(1)}, u32[]{:S(2)}, u32[]{:S(2)}) collective-permute-start(bf16[128,1152]{1,0:T(8,128)(2,1)S(1)} %get-tuple-element.29), channel_id=1, source_target_pairs={{0,1},{1,0},{2,3},{3,2},{4,5},{5,4},{6,7},{7,6},{8,9},{9,8},{10,11... | collective-permute-start | bytes 884744 | tf_op jit(solution)/shard_map/ppermute | solution.py:136
  20.5 20.7 %collective-permute-start.5 = (bf16[128,1152]{1,0:T(8,128)(2,1)S(1)}, bf16[128,1152]{1,0:T(8,128)(2,1)S(1)}, u32[]{:S(2)}, u32[]{:S(2)}) collective-permute-start(bf16[128,1152]{1,0:T(8,128)(2,1)S(1)} %get-tuple-element.30), channel_id=1, source_target_pairs={{0,2},{1,3},{2,0},{3,1},{4,6},{5,7},{6,4},{7,5},{8,10},{9,11},{10,... | collective-permute-start | bytes 884744 | tf_op jit(solution)/shard_map/ppermute | solution.py:136
  37.4 9.2 %collective-permute-start.9 = (bf16[128,384]{1,0:T(8,128)(2,1)S(1)}, bf16[128,384]{1,0:T(8,128)(2,1)S(1)}, u32[]{:S(2)}, u32[]{:S(2)}) collective-permute-start(bf16[128,384]{1,0:T(8,128)(2,1)S(1)} %get-tuple-element.41), channel_id=1, source_target_pairs={{0,2},{1,3},{2,0},{3,1},{4,6},{5,7},{6,4},{7,5},{8,10},{9,11},{10,... | collective-permute-start | bytes 294920 | tf_op jit(solution)/shard_map/ppermute | solution.py:136
  39.5 7.3 %collective-permute-start.10 = (bf16[128,384]{1,0:T(8,128)(2,1)S(1)}, bf16[128,384]{1,0:T(8,128)(2,1)S(1)}, u32[]{:S(2)}, u32[]{:S(2)}) collective-permute-start(bf16[128,384]{1,0:T(8,128)(2,1)S(1)} %get-tuple-element.42), channel_id=1, source_target_pairs={{0,1},{1,0},{2,3},{3,2},{4,5},{5,4},{6,7},{7,6},{8,9},{9,8},{10,11... | collective-permute-start | bytes 294920 | tf_op jit(solution)/shard_map/ppermute | solution.py:136
  41.0 5.8 %collective-permute-start.11 = (bf16[128,384]{1,0:T(8,128)(2,1)S(1)}, bf16[128,384]{1,0:T(8,128)(2,1)S(1)}, u32[]{:S(2)}, u32[]{:S(2)}) collective-permute-start(bf16[128,384]{1,0:T(8,128)(2,1)S(1)} %get-tuple-element.43), channel_id=1, source_target_pairs={{0,3},{1,2},{2,1},{3,0},{4,7},{5,6},{6,5},{7,4},{8,11},{9,10},{10,... | collective-permute-start | bytes 294920 | tf_op jit(solution)/shard_map/ppermute | solution.py:136
  41.2 6.5 %copy-start.2 = (s32[8,24]{1,0:T(8,128)S(1)}, s32[8,24]{1,0:T(8,128)}, u32[]{:S(2)}) copy-start(s32[8,24]{1,0:T(8,128)} %refs_5_.1) | copy-start | bytes 2308
  43.2 8.4 %collective-permute-start.6 = (bf16[128,512]{1,0:T(8,128)(2,1)S(1)}, bf16[128,512]{1,0:T(8,128)(2,1)S(1)}, u32[]{:S(2)}, u32[]{:S(2)}) collective-permute-start(bf16[128,512]{1,0:T(8,128)(2,1)S(1)} %get-tuple-element.36), channel_id=1, source_target_pairs={{0,2},{1,3},{2,0},{3,1},{4,6},{5,7},{6,4},{7,5},{8,10},{9,11},{10,... | collective-permute-start | bytes 393224 | tf_op jit(solution)/shard_map/ppermute | solution.py:136
  45.1 6.6 %collective-permute-start.7 = (bf16[128,512]{1,0:T(8,128)(2,1)S(1)}, bf16[128,512]{1,0:T(8,128)(2,1)S(1)}, u32[]{:S(2)}, u32[]{:S(2)}) collective-permute-start(bf16[128,512]{1,0:T(8,128)(2,1)S(1)} %get-tuple-element.37), channel_id=1, source_target_pairs={{0,3},{1,2},{2,1},{3,0},{4,7},{5,6},{6,5},{7,4},{8,11},{9,10},{10,... | collective-permute-start | bytes 393224 | tf_op jit(solution)/shard_map/ppermute | solution.py:136
  46.5 5.2 %collective-permute-start.8 = (bf16[128,512]{1,0:T(8,128)(2,1)S(1)}, bf16[128,512]{1,0:T(8,128)(2,1)S(1)}, u32[]{:S(2)}, u32[]{:S(2)}) collective-permute-start(bf16[128,512]{1,0:T(8,128)(2,1)S(1)} %get-tuple-element.38), channel_id=1, source_target_pairs={{0,1},{1,0},{2,3},{3,2},{4,5},{5,4},{6,7},{7,6},{8,9},{9,8},{10,11... | collective-permute-start | bytes 393224 | tf_op jit(solution)/shard_map/ppermute | solution.py:136

commit v6 on v5

--- a/solution.py
+++ b/solution.py
@@ -392,18 +392,12 @@
     return blocks, keys, values, next_low, [*leftovers, keys, values]
 
 
-def build_cache(keys, values, starts, lengths, block_table):
-    total_rows = keys[0].shape[1]
-    parts = len(keys)
-    width = sum(part.shape[0] - start for part, start in zip(keys, starts)) * LANES
-    heads_local = width // HD
+def page_picks(lengths, block_table, total_rows):
     page_count = total_rows // PAGE + SEGS
     blocks = block_table.shape[1]
     group = 4
 
-    def body(*refs):
-        key_refs, value_refs = refs[:parts], refs[parts : 2 * parts]
-        lens, table, out, built, sem = refs[2 * parts :]
+    def body(lens, table, picks):
         page = lax.broadcasted_iota(jnp.int32, (page_count, blocks), 0)
         block = lax.broadcasted_iota(jnp.int32, (page_count, blocks), 1)
         first = jnp.zeros((page_count, blocks), jnp.int32)
@@ -418,7 +412,33 @@
         first = jnp.sum(first, axis=1, keepdims=True)
         count = jnp.sum(count, axis=1, keepdims=True)
         place = lax.broadcasted_iota(jnp.int32, (group * page_count, total_rows), 1)
-
+        for r in range(0, PAGE, group):
+            wanted = [jnp.where(count > r + n, first + r + n, -1) for n in range(group)]
+            pick = (place == jnp.concatenate(wanted, axis=0)).astype(F32).astype(BF16)
+            picks[r * page_count : (r + group) * page_count, :] = pick
+
+    return pl.pallas_call(
+        body,
+        out_shape=jax.ShapeDtypeStruct((PAGE * page_count, total_rows), BF16),
+        in_specs=[IN_SMEM, IN_VMEM],
+        out_specs=IN_VMEM,
+        compiler_params=params(),
+        cost_estimate=cost(4 * PAGE * page_count * total_rows, 2 * PAGE * page_count * total_rows),
+        name="page_picks",
+    )(lengths, block_table)
+
+
+def build_cache(keys, values, starts, picks):
+    total_rows = keys[0].shape[1]
+    parts = len(keys)
+    width = sum(part.shape[0] - start for part, start in zip(keys, starts)) * LANES
+    heads_local = width // HD
+    page_count = picks.shape[0] // PAGE
+    group = 4
+
+    def body(*refs):
+        key_refs, value_refs = refs[:parts], refs[parts : 2 * parts]
+        picks_ref, out, built, sem = refs[2 * parts :]
         def gathered(part_refs):
             every = [(ref, tile) for ref, low in zip(part_refs, starts) for tile in range(low, ref.shape[0])]
             return jnp.concatenate([ref[tile] for ref, tile in every], axis=1)
@@ -426,8 +446,7 @@
         all_keys, all_values = gathered(key_refs), gathered(value_refs)
         copies = []
         for r in range(0, PAGE, group):
-            wanted = [jnp.where(count > r + n, first + r + n, -1) for n in range(group)]
-            pick = (place == jnp.concatenate(wanted, axis=0)).astype(F32).astype(BF16)
+            pick = picks_ref[r * page_count : (r + group) * page_count, :]
             picked = [jnp.dot(pick, every, preferred_element_type=F32) for every in (all_keys, all_values)]
             lanes = slice(r * HD, (r + group) * HD)
             for h in range(heads_local):
@@ -450,13 +469,13 @@
     return pl.pallas_call(
         body,
         out_shape=jax.ShapeDtypeStruct(cache, BF16),
-        in_specs=[IN_VMEM] * (2 * parts) + [IN_SMEM, IN_VMEM],
+        in_specs=[IN_VMEM] * (2 * parts + 1),
         out_specs=IN_HBM,
         scratch_shapes=[pltpu.VMEM(cache, BF16), pltpu.SemaphoreType.DMA((heads_local, PAGE // group))],
         compiler_params=params(),
         cost_estimate=cost(4 * page_count * PAGE * total_rows * width, 4 * total_rows * width * 2),
         name="build_cache",
-    )(*keys, *values, lengths, block_table)
+    )(*keys, *values, picks)
 
 
 def join_heads(hidden, parts, width, group_size):
@@ -518,7 +537,8 @@
     parts = map_partners(partners, parts, group_size)
     arrived = [[early, *parts]]
     wanted = [(bits, every, tiles[1]) for bits in others + [0]]
-    later = pack_qkv(shared_qkv, [parts[-1], early], width, wanted)
+    picks = page_picks(lengths, block_table, inputs.shape[0] * group_size)
+    later = pack_qkv(shared_qkv, [parts[-1], early, picks], width, wanted)
     arrived.append([early, parts[0], *map_partners(others, later, group_size)])
     places = []
     for n in range(2):
@@ -546,7 +566,7 @@
         back.append([(to_partner(blocks[bits], bits, group_size), bits, begin) for bits in ([partners[i] for i in ((2, 0, 1) if n else (2, 1, 0))])])
         keys, values = keys + [new_keys], values + [new_values]
     starts = [0, cut - done_cut]
-    cache = build_cache(keys, values, starts, lengths, block_table)
+    cache = build_cache(keys, values, starts, picks)
     hidden = join_heads(None, own + back[0], width, group_size)
     hidden = join_heads(hidden, back[1], width, group_size)
     return (hidden, cache)

time: 52.6 us -> 52.7 us (level)
    pallas_call x0 -> x1, Pallas kernels: none -> 0.87 us  [page_picks(): pl.pallas_call(body, out_shape=jax.ShapeDtypeStruct((PAGE * page_count, t...]
    pallas_call x1, Pallas kernels: 3.99 us -> 3.17 us  [build_cache(): pl.pallas_call(body, out_shape=jax.ShapeDtypeStruct(cache, BF16), in_spec...]
  transfers between devices with their start and end apart: 12 -> 12, of which waited for: 3 -> 5; matrix products, arithmetic and copies ran while one was open for 0% -> 0% of each run, Pallas kernels for 29% -> 29%
where the time goes in v6:
time: 52.7 us; the launch traced here: 52.5 us
  starting transfers between devices  18.3 us (35%)
  Pallas kernels  16.9 us (32%)
  waiting for transfers between devices  16.5 us (31%)
  between operations  0.74 us (1%)
    ppermute x12, starting transfers between devices, to_partner(): lax.ppermute(values, 'seq', [(i, i ^ bits) for i in range(group_size)])  18.3 us
    ppermute x12, waiting for transfers between devices, to_partner(): lax.ppermute(values, 'seq', [(i, i ^ bits) for i in range(group_size)])  16.5 us
    pallas_call x2, Pallas kernels, attend(): pl.pallas_call(body, out_shape=out_shape, in_specs=[IN_VMEM, IN_SMEM, IN_...  4.71 us
    pallas_call x1, Pallas kernels, make_codes(): pl.pallas_call(body, out_shape=[jax.ShapeDtypeStruct((tok_rows, span + co...  4.15 us
    pallas_call x1, Pallas kernels, build_cache(): pl.pallas_call(body, out_shape=jax.ShapeDtypeStruct(cache, BF16), in_spec...  3.17 us
    pallas_call x2, Pallas kernels, pack_qkv(): pl.pallas_call(body, out_shape=[jax.ShapeDtypeStruct((tok_rows, span), BF...  2.41 us
    pallas_call x2, Pallas kernels, join_heads(): pl.pallas_call(body, out_shape=jax.ShapeDtypeStruct((tok_rows, width * gr...  1.59 us
  transfers between devices with their start and end apart: 12, of which 5 were waited for; matrix products, arithmetic and copies ran while one was open for 0% of the time, Pallas kernels for 29%

profile of v6, /device:TPU:0, one launch (start us, length us, event | category | flops | bytes accessed | tf_op | source)
XLA Modules:
  0.0 52.5 jit_solution(14205411480128005411)
XLA Ops:
  0.6 1.1 %pack_qkv.2._ = bf16[128,1792]{1,0:T(8,128)(2,1)S(1)} custom-call(bf16[128,10752]{1,0:T(8,128)(2,1)} %shared.5), custom_call_target="tpu_custom_call" | custom-call | bytes 917504 | tf_op jit(solution)/shard_map/pack_qkv/pallas_call | solution.py:240
  1.7 4.0 %collective-permute-start = (bf16[128,1792]{1,0:T(8,128)(2,1)S(1)}, bf16[128,1792]{1,0:T(8,128)(2,1)S(1)}, u32[]{:S(2)}, u32[]{:S(2)}) collective-permute-start(bf16[128,1792]{1,0:T(8,128)(2,1)S(1)} %pack_qkv.2._), channel_id=1, source_target_pairs={{0,3},{1,2},{2,1},{3,0},{4,7},{5,6},{6,5},{7,4},{8,11},{9,10},{10,... | collective-permute-start | bytes 1376264 | tf_op jit(solution)/shard_map/ppermute | solution.py:136
  5.7 4.2 %make_codes.1 = (bf16[128,1280]{1,0:T(8,128)(2,1)S(1)}, bf16[128,1920]{1,0:T(8,128)(2,1)S(1)}, bf16[128,1920]{1,0:T(8,128)(2,1)S(1)}, bf16[128,1920]{1,0:T(8,128)(2,1)S(1)}) custom-call(bf16[128,7168]{1,0:T(8,128)(2,1)} %inputs_ref.1, bf16[7168,384]{1,0:T(8,128)(2,1)} %down_ref.1, bf16[128,10752]{1,0:T(8,128)(2,1)} %shared.5, bf16[128,1792]{1,0:T(8,128)(2,1)S(1)} %pack_qkv.2._), custom_call_target="tpu_custom_call" | custom-call | flops 704643072 | bytes 5505024 | tf_op jit(solution)/shard_map/make_codes/pallas_call | solution.py:213
  9.9 0.6 %collective-permute-start.2 = (bf16[128,1920]{1,0:T(8,128)(2,1)S(1)}, bf16[128,1920]{1,0:T(8,128)(2,1)S(1)}, u32[]{:S(2)}, u32[]{:S(2)}) collective-permute-start(bf16[128,1920]{1,0:T(8,128)(2,1)S(1)} %get-tuple-element.25), channel_id=1, source_target_pairs={{0,1},{1,0},{2,3},{3,2},{4,5},{5,4},{6,7},{7,6},{8,9},{9,8},{10,11... | collective-permute-start | bytes 1474568 | tf_op jit(solution)/shard_map/ppermute | solution.py:136
  10.5 2.9 %collective-permute-start.1 = (bf16[128,1280]{1,0:T(8,128)(2,1)S(1)}, bf16[128,1280]{1,0:T(8,128)(2,1)S(1)}, u32[]{:S(2)}, u32[]{:S(2)}) collective-permute-start(bf16[128,1280]{1,0:T(8,128)(2,1)S(1)} %get-tuple-element.24), channel_id=1, source_target_pairs={{0,3},{1,2},{2,1},{3,0},{4,7},{5,6},{6,5},{7,4},{8,11},{9,10},{10,... | collective-permute-start | bytes 983048 | tf_op jit(solution)/shard_map/ppermute | solution.py:136
  13.4 0.9 %page_picks.1.refs_2_.refs_4_ = bf16[640,512]{1,0:T(8,128)(2,1)S(1)} custom-call(s32[8]{0:T(128)S(1)} %copy-done.1, s32[8,24]{1,0:T(8,128)S(1)} %copy-done.2), custom_call_target="tpu_custom_call" | custom-call | flops 1310720 | bytes 655360 | tf_op jit(solution)/shard_map/page_picks/pallas_call | solution.py:420
  14.3 2.8 %collective-permute-done.refs_3_.refs_1_.refs_4_ = bf16[128,1792]{1,0:T(8,128)(2,1)S(1)} collective-permute-done((bf16[128,1792]{1,0:T(8,128)(2,1)S(1)}, bf16[128,1792]{1,0:T(8,128)(2,1)S(1)}, u32[]{:S(2)}, u32[]{:S(2)}) %collective-permute-start) | collective-permute-done | bytes 458784 | tf_op jit(solution)/shard_map/ppermute | solution.py:136
  17.1 1.3 %pack_qkv.3 = (bf16[128,1152]{1,0:T(8,128)(2,1)S(1)}, bf16[128,1152]{1,0:T(8,128)(2,1)S(1)}, bf16[128,1152]{1,0:T(8,128)(2,1)S(1)}) custom-call(bf16[128,10752]{1,0:T(8,128)(2,1)} %shared.5, bf16[128,1920]{1,0:T(8,128)(2,1)S(1)} %get-tuple-element.27.refs_7_.refs_0_, bf16[128,1792]{1,0:T(8,128)(2,1)S(1)} %collective-permute-done.refs_3_.refs_1_.refs_4_, ...), custom_call_target="tpu_custom_call" | custom-call | bytes 1769472 | tf_op jit(solution)/shard_map/pack_qkv/pallas_call | solution.py:240
  18.4 2.1 %collective-permute-start.4 = (bf16[128,1152]{1,0:T(8,128)(2,1)S(1)}, bf16[128,1152]{1,0:T(8,128)(2,1)S(1)}, u32[]{:S(2)}, u32[]{:S(2)}) collective-permute-start(bf16[128,1152]{1,0:T(8,128)(2,1)S(1)} %get-tuple-element.29), channel_id=1, source_target_pairs={{0,1},{1,0},{2,3},{3,2},{4,5},{5,4},{6,7},{7,6},{8,9},{9,8},{10,11... | collective-permute-start | bytes 884744 | tf_op jit(solution)/shard_map/ppermute | solution.py:136
  20.5 1.5 %collective-permute-start.5 = (bf16[128,1152]{1,0:T(8,128)(2,1)S(1)}, bf16[128,1152]{1,0:T(8,128)(2,1)S(1)}, u32[]{:S(2)}, u32[]{:S(2)}) collective-permute-start(bf16[128,1152]{1,0:T(8,128)(2,1)S(1)} %get-tuple-element.30), channel_id=1, source_target_pairs={{0,2},{1,3},{2,0},{3,1},{4,6},{5,7},{6,4},{7,5},{8,10},{9,11},{10,... | collective-permute-start | bytes 884744 | tf_op jit(solution)/shard_map/ppermute | solution.py:136
  22.0 12.7 %collective-permute-done.1.refs_4_.refs_5_ = bf16[128,1280]{1,0:T(8,128)(2,1)S(1)} collective-permute-done((bf16[128,1280]{1,0:T(8,128)(2,1)S(1)}, bf16[128,1280]{1,0:T(8,128)(2,1)S(1)}, u32[]{:S(2)}, u32[]{:S(2)}) %collective-permute-start.1) | collective-permute-done | bytes 327712 | tf_op jit(solution)/shard_map/ppermute | solution.py:136
  34.7 2.7 %attend.2 = (bf16[128,384]{1,0:T(8,128)(2,1)S(1)}, bf16[128,384]{1,0:T(8,128)(2,1)S(1)}, bf16[128,384]{1,0:T(8,128)(2,1)S(1)}, bf16[128,384]{1,0:T(8,128)(2,1)S(...) custom-call(bf16[3,128,896]{2,1,0:T(8,128)(2,1)S(1)} %copy-done, ...), custom_call_target="tpu_custom_call" | custom-call | flops 536870912 | bytes 4194304 | tf_op jit(solution)/shard_map/attend/pallas_call | solution.py:377
  37.4 2.1 %collective-permute-start.9 = (bf16[128,384]{1,0:T(8,128)(2,1)S(1)}, bf16[128,384]{1,0:T(8,128)(2,1)S(1)}, u32[]{:S(2)}, u32[]{:S(2)}) collective-permute-start(bf16[128,384]{1,0:T(8,128)(2,1)S(1)} %get-tuple-element.41), channel_id=1, source_target_pairs={{0,2},{1,3},{2,0},{3,1},{4,6},{5,7},{6,4},{7,5},{8,10},{9,11},{10,... | collective-permute-start | bytes 294920 | tf_op jit(solution)/shard_map/ppermute | solution.py:136
  39.5 1.5 %collective-permute-start.10 = (bf16[128,384]{1,0:T(8,128)(2,1)S(1)}, bf16[128,384]{1,0:T(8,128)(2,1)S(1)}, u32[]{:S(2)}, u32[]{:S(2)}) collective-permute-start(bf16[128,384]{1,0:T(8,128)(2,1)S(1)} %get-tuple-element.42), channel_id=1, source_target_pairs={{0,1},{1,0},{2,3},{3,2},{4,5},{5,4},{6,7},{7,6},{8,9},{9,8},{10,11... | collective-permute-start | bytes 294920 | tf_op jit(solution)/shard_map/ppermute | solution.py:136
  41.0 0.2 collective-permute-done.4.refs_6_
  41.2 2.1 %attend.3 = (bf16[128,512]{1,0:T(8,128)(2,1)S(1)}, bf16[128,512]{1,0:T(8,128)(2,1)S(1)}, bf16[128,512]{1,0:T(8,128)(2,1)S(1)}, bf16[128,512]{1,0:T(8,128)(2,1)S(...) custom-call(bf16[3,128,896]{2,1,0:T(8,128)(2,1)S(1)} %copy-done, f32[4]{0:T(128)S(1)} %copy-done.3, ...), custom_call_target="tpu_custom_call" | custom-call | flops 402653184 | bytes 3145728 | tf_op jit(solution)/shard_map/attend/pallas_call | solution.py:377
  43.3 1.8 %collective-permute-start.6 = (bf16[128,512]{1,0:T(8,128)(2,1)S(1)}, bf16[128,512]{1,0:T(8,128)(2,1)S(1)}, u32[]{:S(2)}, u32[]{:S(2)}) collective-permute-start(bf16[128,512]{1,0:T(8,128)(2,1)S(1)} %get-tuple-element.36), channel_id=1, source_target_pairs={{0,2},{1,3},{2,0},{3,1},{4,6},{5,7},{6,4},{7,5},{8,10},{9,11},{10,... | collective-permute-start | bytes 393224 | tf_op jit(solution)/shard_map/ppermute | solution.py:136
  45.1 1.4 %collective-permute-start.7 = (bf16[128,512]{1,0:T(8,128)(2,1)S(1)}, bf16[128,512]{1,0:T(8,128)(2,1)S(1)}, u32[]{:S(2)}, u32[]{:S(2)}) collective-permute-start(bf16[128,512]{1,0:T(8,128)(2,1)S(1)} %get-tuple-element.37), channel_id=1, source_target_pairs={{0,3},{1,2},{2,1},{3,0},{4,7},{5,6},{6,5},{7,4},{8,11},{9,10},{10,... | collective-permute-start | bytes 393224 | tf_op jit(solution)/shard_map/ppermute | solution.py:136
  46.5 0.3 collective-permute-start.8
  46.8 0.8 %join_heads.2.refs_3_ = bf16[128,3584]{1,0:T(8,128)(2,1)} custom-call(bf16[128,384]{1,0:T(8,128)(2,1)S(1)} %get-tuple-element.39.refs_0_, bf16[128,512]{1,0:T(8,128)(2,1)S(1)} %get-tuple-element.40.refs_1_, bf16[128,384]{1,0:T(8,128)(2,1)S(1)} %collective-permute-done.9.refs_2_, bf16[128,384]{1,0:T(8,128)(2,1)S(1)} %collective-permute-done.10.refs_3_, ...), custom_call_target="tpu_custom_call" | custom-call | bytes 1048576 | tf_op jit(solution)/shard_map/join_heads/pallas_call | solution.py:504
  47.7 3.2 %build_cache.1 = bf16[4,40,2,3584]{3,2,1,0:T(2,128)(2,1)} custom-call(bf16[4,512,128]{2,1,0:T(8,128)(2,1)S(1)} %get-tuple-element.34.refs_11_.refs_0_, bf16[4,512,128]{2,1,0:T(8,128)(2,1)S(1)} %get-tuple-element.44.refs_1_, bf16[4,512,128]{2,1,0:T(8,128)(2,1)S(1)} %get-tuple-element.35.refs_12_.refs_2_, bf16[4,512,128]{2,1,0:T(8,128)(2,1)S(1)} %get-tuple-element.45.refs_3_, ...), custom_call_target="tpu_custom_call" | custom-call | flops 1174405120 | bytes 3670016 | tf_op jit(solution)/shard_map/build_cache/pallas_call | solution.py:469
  50.8 0.7 %collective-permute-done.7.refs_1_ = bf16[128,512]{1,0:T(8,128)(2,1)S(1)} collective-permute-done((bf16[128,512]{1,0:T(8,128)(2,1)S(1)}, bf16[128,512]{1,0:T(8,128)(2,1)S(1)}, u32[]{:S(2)}, u32[]{:S(2)}) %collective-permute-start.7) | collective-permute-done | bytes 131104 | tf_op jit(solution)/shard_map/ppermute | solution.py:136
  51.5 0.2 collective-permute-done.8.refs_2_
  51.7 0.8 %join_heads.3 = bf16[128,3584]{1,0:T(8,128)(2,1)} custom-call(bf16[128,512]{1,0:T(8,128)(2,1)S(1)} %collective-permute-done.6.refs_0_, bf16[128,512]{1,0:T(8,128)(2,1)S(1)} %collective-permute-done.7.refs_1_, bf16[128,512]{1,0:T(8,128)(2,1)S(1)} %collective-permute-done.8.refs_2_, bf16[128,3584]{1,0:T(8,128)(2,1)} %join_heads.2.refs_3_), custom_call_target="tpu_custom_call", output_to_operand_aliasing={{}: (3, {})} | custom-call | bytes 786432 | tf_op jit(solution)/shard_map/join_heads/pallas_call | solution.py:504
  (17 shorter events, 0.2 us)
Async XLA Ops:
  1.7 11.7 %copy-start.1 = (s32[8]{0:T(128)S(1)}, s32[8]{0:T(128)}, u32[]{:S(2)}) copy-start(s32[8]{0:T(128)} %refs_2_.3) | copy-start | bytes 100
  1.7 11.7 %copy-start.2 = (s32[8,24]{1,0:T(8,128)S(1)}, s32[8,24]{1,0:T(8,128)}, u32[]{:S(2)}) copy-start(s32[8,24]{1,0:T(8,128)} %table.1) | copy-start | bytes 2308
  1.7 15.4 %collective-permute-start = (bf16[128,1792]{1,0:T(8,128)(2,1)S(1)}, bf16[128,1792]{1,0:T(8,128)(2,1)S(1)}, u32[]{:S(2)}, u32[]{:S(2)}) collective-permute-start(bf16[128,1792]{1,0:T(8,128)(2,1)S(1)} %pack_qkv.2._), channel_id=1, source_target_pairs={{0,3},{1,2},{2,1},{3,0},{4,7},{5,6},{6,5},{7,4},{8,11},{9,10},{10,... | collective-permute-start | bytes 1376264 | tf_op jit(solution)/shard_map/ppermute | solution.py:136
  9.9 24.8 %collective-permute-start.2 = (bf16[128,1920]{1,0:T(8,128)(2,1)S(1)}, bf16[128,1920]{1,0:T(8,128)(2,1)S(1)}, u32[]{:S(2)}, u32[]{:S(2)}) collective-permute-start(bf16[128,1920]{1,0:T(8,128)(2,1)S(1)} %get-tuple-element.25), channel_id=1, source_target_pairs={{0,1},{1,0},{2,3},{3,2},{4,5},{5,4},{6,7},{7,6},{8,9},{9,8},{10,11... | collective-permute-start | bytes 1474568 | tf_op jit(solution)/shard_map/ppermute | solution.py:136
  10.5 24.2 %collective-permute-start.3 = (bf16[128,1920]{1,0:T(8,128)(2,1)S(1)}, bf16[128,1920]{1,0:T(8,128)(2,1)S(1)}, u32[]{:S(2)}, u32[]{:S(2)}) collective-permute-start(bf16[128,1920]{1,0:T(8,128)(2,1)S(1)} %get-tuple-element.26), channel_id=1, source_target_pairs={{0,2},{1,3},{2,0},{3,1},{4,6},{5,7},{6,4},{7,5},{8,10},{9,11},{10,... | collective-permute-start | bytes 1474568 | tf_op jit(solution)/shard_map/ppermute | solution.py:136
  10.5 24.2 %copy-start = (bf16[3,128,896]{2,1,0:T(8,128)(2,1)S(1)}, bf16[3,128,896]{2,1,0:T(8,128)(2,1)}, u32[]{:S(2)}) copy-start(bf16[3,128,896]{2,1,0:T(8,128)(2,1)} %refs_0_.3) | copy-start | bytes 2064388
  10.5 24.2 %copy-start.3 = (f32[4]{0:T(128)S(1)}, f32[4]{0:T(128)}, u32[]{:S(2)}) copy-start(f32[4]{0:T(128)} %refs_1_.3) | copy-start | bytes 52
  10.5 24.2 %collective-permute-start.1 = (bf16[128,1280]{1,0:T(8,128)(2,1)S(1)}, bf16[128,1280]{1,0:T(8,128)(2,1)S(1)}, u32[]{:S(2)}, u32[]{:S(2)}) collective-permute-start(bf16[128,1280]{1,0:T(8,128)(2,1)S(1)} %get-tuple-element.24), channel_id=1, source_target_pairs={{0,3},{1,2},{2,1},{3,0},{4,7},{5,6},{6,5},{7,4},{8,11},{9,10},{10,... | collective-permute-start | bytes 983048 | tf_op jit(solution)/shard_map/ppermute | solution.py:136
  18.4 22.8 %collective-permute-start.4 = (bf16[128,1152]{1,0:T(8,128)(2,1)S(1)}, bf16[128,1152]{1,0:T(8,128)(2,1)S(1)}, u32[]{:S(2)}, u32[]{:S(2)}) collective-permute-start(bf16[128,1152]{1,0:T(8,128)(2,1)S(1)} %get-tuple-element.29), channel_id=1, source_target_pairs={{0,1},{1,0},{2,3},{3,2},{4,5},{5,4},{6,7},{7,6},{8,9},{9,8},{10,11... | collective-permute-start | bytes 884744 | tf_op jit(solution)/shard_map/ppermute | solution.py:136
  20.5 20.7 %collective-permute-start.5 = (bf16[128,1152]{1,0:T(8,128)(2,1)S(1)}, bf16[128,1152]{1,0:T(8,128)(2,1)S(1)}, u32[]{:S(2)}, u32[]{:S(2)}) collective-permute-start(bf16[128,1152]{1,0:T(8,128)(2,1)S(1)} %get-tuple-element.30), channel_id=1, source_target_pairs={{0,2},{1,3},{2,0},{3,1},{4,6},{5,7},{6,4},{7,5},{8,10},{9,11},{10,... | collective-permute-start | bytes 884744 | tf_op jit(solution)/shard_map/ppermute | solution.py:136
  37.4 9.2 %collective-permute-start.9 = (bf16[128,384]{1,0:T(8,128)(2,1)S(1)}, bf16[128,384]{1,0:T(8,128)(2,1)S(1)}, u32[]{:S(2)}, u32[]{:S(2)}) collective-permute-start(bf16[128,384]{1,0:T(8,128)(2,1)S(1)} %get-tuple-element.41), channel_id=1, source_target_pairs={{0,2},{1,3},{2,0},{3,1},{4,6},{5,7},{6,4},{7,5},{8,10},{9,11},{10,... | collective-permute-start | bytes 294920 | tf_op jit(solution)/shard_map/ppermute | solution.py:136
  39.5 7.3 %collective-permute-start.10 = (bf16[128,384]{1,0:T(8,128)(2,1)S(1)}, bf16[128,384]{1,0:T(8,128)(2,1)S(1)}, u32[]{:S(2)}, u32[]{:S(2)}) collective-permute-start(bf16[128,384]{1,0:T(8,128)(2,1)S(1)} %get-tuple-element.42), channel_id=1, source_target_pairs={{0,1},{1,0},{2,3},{3,2},{4,5},{5,4},{6,7},{7,6},{8,9},{9,8},{10,11... | collective-permute-start | bytes 294920 | tf_op jit(solution)/shard_map/ppermute | solution.py:136
  41.0 5.9 %collective-permute-start.11 = (bf16[128,384]{1,0:T(8,128)(2,1)S(1)}, bf16[128,384]{1,0:T(8,128)(2,1)S(1)}, u32[]{:S(2)}, u32[]{:S(2)}) collective-permute-start(bf16[128,384]{1,0:T(8,128)(2,1)S(1)} %get-tuple-element.43), channel_id=1, source_target_pairs={{0,3},{1,2},{2,1},{3,0},{4,7},{5,6},{6,5},{7,4},{8,11},{9,10},{10,... | collective-permute-start | bytes 294920 | tf_op jit(solution)/shard_map/ppermute | solution.py:136
  43.3 7.6 %collective-permute-start.6 = (bf16[128,512]{1,0:T(8,128)(2,1)S(1)}, bf16[128,512]{1,0:T(8,128)(2,1)S(1)}, u32[]{:S(2)}, u32[]{:S(2)}) collective-permute-start(bf16[128,512]{1,0:T(8,128)(2,1)S(1)} %get-tuple-element.36), channel_id=1, source_target_pairs={{0,2},{1,3},{2,0},{3,1},{4,6},{5,7},{6,4},{7,5},{8,10},{9,11},{10,... | collective-permute-start | bytes 393224 | tf_op jit(solution)/shard_map/ppermute | solution.py:136
  45.1 6.4 %collective-permute-start.7 = (bf16[128,512]{1,0:T(8,128)(2,1)S(1)}, bf16[128,512]{1,0:T(8,128)(2,1)S(1)}, u32[]{:S(2)}, u32[]{:S(2)}) collective-permute-start(bf16[128,512]{1,0:T(8,128)(2,1)S(1)} %get-tuple-element.37), channel_id=1, source_target_pairs={{0,3},{1,2},{2,1},{3,0},{4,7},{5,6},{6,5},{7,4},{8,11},{9,10},{10,... | collective-permute-start | bytes 393224 | tf_op jit(solution)/shard_map/ppermute | solution.py:136
  46.5 5.2 %collective-permute-start.8 = (bf16[128,512]{1,0:T(8,128)(2,1)S(1)}, bf16[128,512]{1,0:T(8,128)(2,1)S(1)}, u32[]{:S(2)}, u32[]{:S(2)}) collective-permute-start(bf16[128,512]{1,0:T(8,128)(2,1)S(1)} %get-tuple-element.38), channel_id=1, source_target_pairs={{0,1},{1,0},{2,3},{3,2},{4,5},{5,4},{6,7},{7,6},{8,9},{9,8},{10,11... | collective-permute-start | bytes 393224 | tf_op jit(solution)/shard_map/ppermute | solution.py:136

commit v7 on v6

--- a/solution.py
+++ b/solution.py
@@ -563,7 +563,7 @@
         )
         begin = done_tiles[n][0] * LANES
         own.append((blocks[0], 0, begin))
-        back.append([(to_partner(blocks[bits], bits, group_size), bits, begin) for bits in ([partners[i] for i in ((2, 0, 1) if n else (2, 1, 0))])])
+        back.append([(to_partner(blocks[bits], bits, group_size), bits, begin) for bits in ([partners[i] for i in ((2, 0, 1) if n else (1, 2, 0))])])
         keys, values = keys + [new_keys], values + [new_values]
     starts = [0, cut - done_cut]
     cache = build_cache(keys, values, starts, picks)

time: 52.7 us -> 52.7 us (level)
  no operation moved by 1% of the time
where the time goes in v7:
time: 52.7 us; the launch traced here: 52.5 us
  starting transfers between devices  18.3 us (35%)
  Pallas kernels  16.9 us (32%)
  waiting for transfers between devices  16.6 us (31%)
  between operations  0.74 us (1%)
    ppermute x12, starting transfers between devices, to_partner(): lax.ppermute(values, 'seq', [(i, i ^ bits) for i in range(group_size)])  18.3 us
    ppermute x12, waiting for transfers between devices, to_partner(): lax.ppermute(values, 'seq', [(i, i ^ bits) for i in range(group_size)])  16.6 us
    pallas_call x2, Pallas kernels, attend(): pl.pallas_call(body, out_shape=out_shape, in_specs=[IN_VMEM, IN_SMEM, IN_...  4.71 us
    pallas_call x1, Pallas kernels, make_codes(): pl.pallas_call(body, out_shape=[jax.ShapeDtypeStruct((tok_rows, span + co...  4.15 us
    pallas_call x1, Pallas kernels, build_cache(): pl.pallas_call(body, out_shape=jax.ShapeDtypeStruct(cache, BF16), in_spec...  3.16 us
    pallas_call x2, Pallas kernels, pack_qkv(): pl.pallas_call(body, out_shape=[jax.ShapeDtypeStruct((tok_rows, span), BF...  2.41 us
    pallas_call x2, Pallas kernels, join_heads(): pl.pallas_call(body, out_shape=jax.ShapeDtypeStruct((tok_rows, width * gr...  1.59 us
  transfers between devices with their start and end apart: 12, of which 5 were waited for; matrix products, arithmetic and copies ran while one was open for 0% of the time, Pallas kernels for 29%

profile of v7, /device:TPU:0, one launch (start us, length us, event | category | flops | bytes accessed | tf_op | source)
XLA Modules:
  0.0 52.5 jit_solution(17565051455770639598)
XLA Ops:
  0.6 1.1 %pack_qkv.2._ = bf16[128,1792]{1,0:T(8,128)(2,1)S(1)} custom-call(bf16[128,10752]{1,0:T(8,128)(2,1)} %shared.5), custom_call_target="tpu_custom_call" | custom-call | bytes 917504 | tf_op jit(solution)/shard_map/pack_qkv/pallas_call | solution.py:240
  1.7 4.0 %collective-permute-start = (bf16[128,1792]{1,0:T(8,128)(2,1)S(1)}, bf16[128,1792]{1,0:T(8,128)(2,1)S(1)}, u32[]{:S(2)}, u32[]{:S(2)}) collective-permute-start(bf16[128,1792]{1,0:T(8,128)(2,1)S(1)} %pack_qkv.2._), channel_id=1, source_target_pairs={{0,3},{1,2},{2,1},{3,0},{4,7},{5,6},{6,5},{7,4},{8,11},{9,10},{10,... | collective-permute-start | bytes 1376264 | tf_op jit(solution)/shard_map/ppermute | solution.py:136
  5.7 4.2 %make_codes.1 = (bf16[128,1280]{1,0:T(8,128)(2,1)S(1)}, bf16[128,1920]{1,0:T(8,128)(2,1)S(1)}, bf16[128,1920]{1,0:T(8,128)(2,1)S(1)}, bf16[128,1920]{1,0:T(8,128)(2,1)S(1)}) custom-call(bf16[128,7168]{1,0:T(8,128)(2,1)} %inputs_ref.1, bf16[7168,384]{1,0:T(8,128)(2,1)} %down_ref.1, bf16[128,10752]{1,0:T(8,128)(2,1)} %shared.5, bf16[128,1792]{1,0:T(8,128)(2,1)S(1)} %pack_qkv.2._), custom_call_target="tpu_custom_call" | custom-call | flops 704643072 | bytes 5505024 | tf_op jit(solution)/shard_map/make_codes/pallas_call | solution.py:213
  9.9 0.6 %collective-permute-start.2 = (bf16[128,1920]{1,0:T(8,128)(2,1)S(1)}, bf16[128,1920]{1,0:T(8,128)(2,1)S(1)}, u32[]{:S(2)}, u32[]{:S(2)}) collective-permute-start(bf16[128,1920]{1,0:T(8,128)(2,1)S(1)} %get-tuple-element.25), channel_id=1, source_target_pairs={{0,1},{1,0},{2,3},{3,2},{4,5},{5,4},{6,7},{7,6},{8,9},{9,8},{10,11... | collective-permute-start | bytes 1474568 | tf_op jit(solution)/shard_map/ppermute | solution.py:136
  10.5 2.9 %collective-permute-start.1 = (bf16[128,1280]{1,0:T(8,128)(2,1)S(1)}, bf16[128,1280]{1,0:T(8,128)(2,1)S(1)}, u32[]{:S(2)}, u32[]{:S(2)}) collective-permute-start(bf16[128,1280]{1,0:T(8,128)(2,1)S(1)} %get-tuple-element.24), channel_id=1, source_target_pairs={{0,3},{1,2},{2,1},{3,0},{4,7},{5,6},{6,5},{7,4},{8,11},{9,10},{10,... | collective-permute-start | bytes 983048 | tf_op jit(solution)/shard_map/ppermute | solution.py:136
  13.4 0.9 %page_picks.1.refs_2_.refs_4_ = bf16[640,512]{1,0:T(8,128)(2,1)S(1)} custom-call(s32[8]{0:T(128)S(1)} %copy-done.1, s32[8,24]{1,0:T(8,128)S(1)} %copy-done.2), custom_call_target="tpu_custom_call" | custom-call | flops 1310720 | bytes 655360 | tf_op jit(solution)/shard_map/page_picks/pallas_call | solution.py:420
  14.3 2.8 %collective-permute-done.refs_3_.refs_1_.refs_4_ = bf16[128,1792]{1,0:T(8,128)(2,1)S(1)} collective-permute-done((bf16[128,1792]{1,0:T(8,128)(2,1)S(1)}, bf16[128,1792]{1,0:T(8,128)(2,1)S(1)}, u32[]{:S(2)}, u32[]{:S(2)}) %collective-permute-start) | collective-permute-done | bytes 458784 | tf_op jit(solution)/shard_map/ppermute | solution.py:136
  17.1 1.3 %pack_qkv.3 = (bf16[128,1152]{1,0:T(8,128)(2,1)S(1)}, bf16[128,1152]{1,0:T(8,128)(2,1)S(1)}, bf16[128,1152]{1,0:T(8,128)(2,1)S(1)}) custom-call(bf16[128,10752]{1,0:T(8,128)(2,1)} %shared.5, bf16[128,1920]{1,0:T(8,128)(2,1)S(1)} %get-tuple-element.27.refs_7_.refs_0_, bf16[128,1792]{1,0:T(8,128)(2,1)S(1)} %collective-permute-done.refs_3_.refs_1_.refs_4_, ...), custom_call_target="tpu_custom_call" | custom-call | bytes 1769472 | tf_op jit(solution)/shard_map/pack_qkv/pallas_call | solution.py:240
  18.4 2.1 %collective-permute-start.4 = (bf16[128,1152]{1,0:T(8,128)(2,1)S(1)}, bf16[128,1152]{1,0:T(8,128)(2,1)S(1)}, u32[]{:S(2)}, u32[]{:S(2)}) collective-permute-start(bf16[128,1152]{1,0:T(8,128)(2,1)S(1)} %get-tuple-element.29), channel_id=1, source_target_pairs={{0,1},{1,0},{2,3},{3,2},{4,5},{5,4},{6,7},{7,6},{8,9},{9,8},{10,11... | collective-permute-start | bytes 884744 | tf_op jit(solution)/shard_map/ppermute | solution.py:136
  20.5 1.5 %collective-permute-start.5 = (bf16[128,1152]{1,0:T(8,128)(2,1)S(1)}, bf16[128,1152]{1,0:T(8,128)(2,1)S(1)}, u32[]{:S(2)}, u32[]{:S(2)}) collective-permute-start(bf16[128,1152]{1,0:T(8,128)(2,1)S(1)} %get-tuple-element.30), channel_id=1, source_target_pairs={{0,2},{1,3},{2,0},{3,1},{4,6},{5,7},{6,4},{7,5},{8,10},{9,11},{10,... | collective-permute-start | bytes 884744 | tf_op jit(solution)/shard_map/ppermute | solution.py:136
  22.0 12.7 %collective-permute-done.1.refs_4_.refs_5_ = bf16[128,1280]{1,0:T(8,128)(2,1)S(1)} collective-permute-done((bf16[128,1280]{1,0:T(8,128)(2,1)S(1)}, bf16[128,1280]{1,0:T(8,128)(2,1)S(1)}, u32[]{:S(2)}, u32[]{:S(2)}) %collective-permute-start.1) | collective-permute-done | bytes 327712 | tf_op jit(solution)/shard_map/ppermute | solution.py:136
  34.7 2.7 %attend.2 = (bf16[128,384]{1,0:T(8,128)(2,1)S(1)}, bf16[128,384]{1,0:T(8,128)(2,1)S(1)}, bf16[128,384]{1,0:T(8,128)(2,1)S(1)}, bf16[128,384]{1,0:T(8,128)(2,1)S(...) custom-call(bf16[3,128,896]{2,1,0:T(8,128)(2,1)S(1)} %copy-done, ...), custom_call_target="tpu_custom_call" | custom-call | flops 536870912 | bytes 4194304 | tf_op jit(solution)/shard_map/attend/pallas_call | solution.py:377
  37.4 2.1 %collective-permute-start.9 = (bf16[128,384]{1,0:T(8,128)(2,1)S(1)}, bf16[128,384]{1,0:T(8,128)(2,1)S(1)}, u32[]{:S(2)}, u32[]{:S(2)}) collective-permute-start(bf16[128,384]{1,0:T(8,128)(2,1)S(1)} %get-tuple-element.41), channel_id=1, source_target_pairs={{0,1},{1,0},{2,3},{3,2},{4,5},{5,4},{6,7},{7,6},{8,9},{9,8},{10,11... | collective-permute-start | bytes 294920 | tf_op jit(solution)/shard_map/ppermute | solution.py:136
  39.4 1.5 %collective-permute-start.10 = (bf16[128,384]{1,0:T(8,128)(2,1)S(1)}, bf16[128,384]{1,0:T(8,128)(2,1)S(1)}, u32[]{:S(2)}, u32[]{:S(2)}) collective-permute-start(bf16[128,384]{1,0:T(8,128)(2,1)S(1)} %get-tuple-element.42), channel_id=1, source_target_pairs={{0,2},{1,3},{2,0},{3,1},{4,6},{5,7},{6,4},{7,5},{8,10},{9,11},{10,... | collective-permute-start | bytes 294920 | tf_op jit(solution)/shard_map/ppermute | solution.py:136
  41.0 0.6 %collective-permute-done.4.refs_6_ = bf16[128,1152]{1,0:T(8,128)(2,1)S(1)} collective-permute-done((bf16[128,1152]{1,0:T(8,128)(2,1)S(1)}, bf16[128,1152]{1,0:T(8,128)(2,1)S(1)}, u32[]{:S(2)}, u32[]{:S(2)}) %collective-permute-start.4) | collective-permute-done | bytes 294944 | tf_op jit(solution)/shard_map/ppermute | solution.py:136
  41.6 2.1 %attend.3 = (bf16[128,512]{1,0:T(8,128)(2,1)S(1)}, bf16[128,512]{1,0:T(8,128)(2,1)S(1)}, bf16[128,512]{1,0:T(8,128)(2,1)S(1)}, bf16[128,512]{1,0:T(8,128)(2,1)S(...) custom-call(bf16[3,128,896]{2,1,0:T(8,128)(2,1)S(1)} %copy-done, f32[4]{0:T(128)S(1)} %copy-done.3, ...), custom_call_target="tpu_custom_call" | custom-call | flops 402653184 | bytes 3145728 | tf_op jit(solution)/shard_map/attend/pallas_call | solution.py:377
  43.7 1.5 %collective-permute-start.6 = (bf16[128,512]{1,0:T(8,128)(2,1)S(1)}, bf16[128,512]{1,0:T(8,128)(2,1)S(1)}, u32[]{:S(2)}, u32[]{:S(2)}) collective-permute-start(bf16[128,512]{1,0:T(8,128)(2,1)S(1)} %get-tuple-element.36), channel_id=1, source_target_pairs={{0,2},{1,3},{2,0},{3,1},{4,6},{5,7},{6,4},{7,5},{8,10},{9,11},{10,... | collective-permute-start | bytes 393224 | tf_op jit(solution)/shard_map/ppermute | solution.py:136
  45.1 1.6 %collective-permute-start.7 = (bf16[128,512]{1,0:T(8,128)(2,1)S(1)}, bf16[128,512]{1,0:T(8,128)(2,1)S(1)}, u32[]{:S(2)}, u32[]{:S(2)}) collective-permute-start(bf16[128,512]{1,0:T(8,128)(2,1)S(1)} %get-tuple-element.37), channel_id=1, source_target_pairs={{0,3},{1,2},{2,1},{3,0},{4,7},{5,6},{6,5},{7,4},{8,11},{9,10},{10,... | collective-permute-start | bytes 393224 | tf_op jit(solution)/shard_map/ppermute | solution.py:136
  46.7 0.5 %collective-permute-start.8 = (bf16[128,512]{1,0:T(8,128)(2,1)S(1)}, bf16[128,512]{1,0:T(8,128)(2,1)S(1)}, u32[]{:S(2)}, u32[]{:S(2)}) collective-permute-start(bf16[128,512]{1,0:T(8,128)(2,1)S(1)} %get-tuple-element.38), channel_id=1, source_target_pairs={{0,1},{1,0},{2,3},{3,2},{4,5},{5,4},{6,7},{7,6},{8,9},{9,8},{10,11... | collective-permute-start | bytes 393224 | tf_op jit(solution)/shard_map/ppermute | solution.py:136
  47.2 0.8 %join_heads.2.refs_3_ = bf16[128,3584]{1,0:T(8,128)(2,1)} custom-call(bf16[128,384]{1,0:T(8,128)(2,1)S(1)} %get-tuple-element.39.refs_0_, bf16[128,512]{1,0:T(8,128)(2,1)S(1)} %get-tuple-element.40.refs_1_, bf16[128,384]{1,0:T(8,128)(2,1)S(1)} %collective-permute-done.9.refs_2_, bf16[128,384]{1,0:T(8,128)(2,1)S(1)} %collective-permute-done.10.refs_3_, ...), custom_call_target="tpu_custom_call" | custom-call | bytes 1048576 | tf_op jit(solution)/shard_map/join_heads/pallas_call | solution.py:504
  48.0 3.2 %build_cache.1 = bf16[4,40,2,3584]{3,2,1,0:T(2,128)(2,1)} custom-call(bf16[4,512,128]{2,1,0:T(8,128)(2,1)S(1)} %get-tuple-element.34.refs_11_.refs_0_, bf16[4,512,128]{2,1,0:T(8,128)(2,1)S(1)} %get-tuple-element.44.refs_1_, bf16[4,512,128]{2,1,0:T(8,128)(2,1)S(1)} %get-tuple-element.35.refs_12_.refs_2_, bf16[4,512,128]{2,1,0:T(8,128)(2,1)S(1)} %get-tuple-element.45.refs_3_, ...), custom_call_target="tpu_custom_call" | custom-call | flops 1174405120 | bytes 3670016 | tf_op jit(solution)/shard_map/build_cache/pallas_call | solution.py:469
  51.2 0.3 collective-permute-done.7.refs_1_
  51.5 0.3 collective-permute-done.8.refs_2_
  51.8 0.8 %join_heads.3 = bf16[128,3584]{1,0:T(8,128)(2,1)} custom-call(bf16[128,512]{1,0:T(8,128)(2,1)S(1)} %collective-permute-done.6.refs_0_, bf16[128,512]{1,0:T(8,128)(2,1)S(1)} %collective-permute-done.7.refs_1_, bf16[128,512]{1,0:T(8,128)(2,1)S(1)} %collective-permute-done.8.refs_2_, bf16[128,3584]{1,0:T(8,128)(2,1)} %join_heads.2.refs_3_), custom_call_target="tpu_custom_call", output_to_operand_aliasing={{}: (3, {})} | custom-call | bytes 786432 | tf_op jit(solution)/shard_map/join_heads/pallas_call | solution.py:504
  (17 shorter events, 0.1 us)
Async XLA Ops:
  1.7 11.7 %copy-start.1 = (s32[8]{0:T(128)S(1)}, s32[8]{0:T(128)}, u32[]{:S(2)}) copy-start(s32[8]{0:T(128)} %refs_2_.3) | copy-start | bytes 100
  1.7 11.7 %copy-start.2 = (s32[8,24]{1,0:T(8,128)S(1)}, s32[8,24]{1,0:T(8,128)}, u32[]{:S(2)}) copy-start(s32[8,24]{1,0:T(8,128)} %table.1) | copy-start | bytes 2308
  1.7 15.4 %collective-permute-start = (bf16[128,1792]{1,0:T(8,128)(2,1)S(1)}, bf16[128,1792]{1,0:T(8,128)(2,1)S(1)}, u32[]{:S(2)}, u32[]{:S(2)}) collective-permute-start(bf16[128,1792]{1,0:T(8,128)(2,1)S(1)} %pack_qkv.2._), channel_id=1, source_target_pairs={{0,3},{1,2},{2,1},{3,0},{4,7},{5,6},{6,5},{7,4},{8,11},{9,10},{10,... | collective-permute-start | bytes 1376264 | tf_op jit(solution)/shard_map/ppermute | solution.py:136
  9.9 24.8 %collective-permute-start.2 = (bf16[128,1920]{1,0:T(8,128)(2,1)S(1)}, bf16[128,1920]{1,0:T(8,128)(2,1)S(1)}, u32[]{:S(2)}, u32[]{:S(2)}) collective-permute-start(bf16[128,1920]{1,0:T(8,128)(2,1)S(1)} %get-tuple-element.25), channel_id=1, source_target_pairs={{0,1},{1,0},{2,3},{3,2},{4,5},{5,4},{6,7},{7,6},{8,9},{9,8},{10,11... | collective-permute-start | bytes 1474568 | tf_op jit(solution)/shard_map/ppermute | solution.py:136
  10.5 24.2 %collective-permute-start.3 = (bf16[128,1920]{1,0:T(8,128)(2,1)S(1)}, bf16[128,1920]{1,0:T(8,128)(2,1)S(1)}, u32[]{:S(2)}, u32[]{:S(2)}) collective-permute-start(bf16[128,1920]{1,0:T(8,128)(2,1)S(1)} %get-tuple-element.26), channel_id=1, source_target_pairs={{0,2},{1,3},{2,0},{3,1},{4,6},{5,7},{6,4},{7,5},{8,10},{9,11},{10,... | collective-permute-start | bytes 1474568 | tf_op jit(solution)/shard_map/ppermute | solution.py:136
  10.5 24.2 %copy-start = (bf16[3,128,896]{2,1,0:T(8,128)(2,1)S(1)}, bf16[3,128,896]{2,1,0:T(8,128)(2,1)}, u32[]{:S(2)}) copy-start(bf16[3,128,896]{2,1,0:T(8,128)(2,1)} %refs_0_.3) | copy-start | bytes 2064388
  10.5 24.2 %copy-start.3 = (f32[4]{0:T(128)S(1)}, f32[4]{0:T(128)}, u32[]{:S(2)}) copy-start(f32[4]{0:T(128)} %refs_1_.3) | copy-start | bytes 52
  10.5 24.2 %collective-permute-start.1 = (bf16[128,1280]{1,0:T(8,128)(2,1)S(1)}, bf16[128,1280]{1,0:T(8,128)(2,1)S(1)}, u32[]{:S(2)}, u32[]{:S(2)}) collective-permute-start(bf16[128,1280]{1,0:T(8,128)(2,1)S(1)} %get-tuple-element.24), channel_id=1, source_target_pairs={{0,3},{1,2},{2,1},{3,0},{4,7},{5,6},{6,5},{7,4},{8,11},{9,10},{10,... | collective-permute-start | bytes 983048 | tf_op jit(solution)/shard_map/ppermute | solution.py:136
  18.4 23.2 %collective-permute-start.4 = (bf16[128,1152]{1,0:T(8,128)(2,1)S(1)}, bf16[128,1152]{1,0:T(8,128)(2,1)S(1)}, u32[]{:S(2)}, u32[]{:S(2)}) collective-permute-start(bf16[128,1152]{1,0:T(8,128)(2,1)S(1)} %get-tuple-element.29), channel_id=1, source_target_pairs={{0,1},{1,0},{2,3},{3,2},{4,5},{5,4},{6,7},{7,6},{8,9},{9,8},{10,11... | collective-permute-start | bytes 884744 | tf_op jit(solution)/shard_map/ppermute | solution.py:136
  20.5 21.1 %collective-permute-start.5 = (bf16[128,1152]{1,0:T(8,128)(2,1)S(1)}, bf16[128,1152]{1,0:T(8,128)(2,1)S(1)}, u32[]{:S(2)}, u32[]{:S(2)}) collective-permute-start(bf16[128,1152]{1,0:T(8,128)(2,1)S(1)} %get-tuple-element.30), channel_id=1, source_target_pairs={{0,2},{1,3},{2,0},{3,1},{4,6},{5,7},{6,4},{7,5},{8,10},{9,11},{10,... | collective-permute-start | bytes 884744 | tf_op jit(solution)/shard_map/ppermute | solution.py:136
  37.4 9.3 %collective-permute-start.9 = (bf16[128,384]{1,0:T(8,128)(2,1)S(1)}, bf16[128,384]{1,0:T(8,128)(2,1)S(1)}, u32[]{:S(2)}, u32[]{:S(2)}) collective-permute-start(bf16[128,384]{1,0:T(8,128)(2,1)S(1)} %get-tuple-element.41), channel_id=1, source_target_pairs={{0,1},{1,0},{2,3},{3,2},{4,5},{5,4},{6,7},{7,6},{8,9},{9,8},{10,11... | collective-permute-start | bytes 294920 | tf_op jit(solution)/shard_map/ppermute | solution.py:136
  39.4 7.8 %collective-permute-start.10 = (bf16[128,384]{1,0:T(8,128)(2,1)S(1)}, bf16[128,384]{1,0:T(8,128)(2,1)S(1)}, u32[]{:S(2)}, u32[]{:S(2)}) collective-permute-start(bf16[128,384]{1,0:T(8,128)(2,1)S(1)} %get-tuple-element.42), channel_id=1, source_target_pairs={{0,2},{1,3},{2,0},{3,1},{4,6},{5,7},{6,4},{7,5},{8,10},{9,11},{10,... | collective-permute-start | bytes 294920 | tf_op jit(solution)/shard_map/ppermute | solution.py:136
  41.0 6.2 %collective-permute-start.11 = (bf16[128,384]{1,0:T(8,128)(2,1)S(1)}, bf16[128,384]{1,0:T(8,128)(2,1)S(1)}, u32[]{:S(2)}, u32[]{:S(2)}) collective-permute-start(bf16[128,384]{1,0:T(8,128)(2,1)S(1)} %get-tuple-element.43), channel_id=1, source_target_pairs={{0,3},{1,2},{2,1},{3,0},{4,7},{5,6},{6,5},{7,4},{8,11},{9,10},{10,... | collective-permute-start | bytes 294920 | tf_op jit(solution)/shard_map/ppermute | solution.py:136
  43.7 7.6 %collective-permute-start.6 = (bf16[128,512]{1,0:T(8,128)(2,1)S(1)}, bf16[128,512]{1,0:T(8,128)(2,1)S(1)}, u32[]{:S(2)}, u32[]{:S(2)}) collective-permute-start(bf16[128,512]{1,0:T(8,128)(2,1)S(1)} %get-tuple-element.36), channel_id=1, source_target_pairs={{0,2},{1,3},{2,0},{3,1},{4,6},{5,7},{6,4},{7,5},{8,10},{9,11},{10,... | collective-permute-start | bytes 393224 | tf_op jit(solution)/shard_map/ppermute | solution.py:136
  45.1 6.4 %collective-permute-start.7 = (bf16[128,512]{1,0:T(8,128)(2,1)S(1)}, bf16[128,512]{1,0:T(8,128)(2,1)S(1)}, u32[]{:S(2)}, u32[]{:S(2)}) collective-permute-start(bf16[128,512]{1,0:T(8,128)(2,1)S(1)} %get-tuple-element.37), channel_id=1, source_target_pairs={{0,3},{1,2},{2,1},{3,0},{4,7},{5,6},{6,5},{7,4},{8,11},{9,10},{10,... | collective-permute-start | bytes 393224 | tf_op jit(solution)/shard_map/ppermute | solution.py:136
  46.7 5.1 %collective-permute-start.8 = (bf16[128,512]{1,0:T(8,128)(2,1)S(1)}, bf16[128,512]{1,0:T(8,128)(2,1)S(1)}, u32[]{:S(2)}, u32[]{:S(2)}) collective-permute-start(bf16[128,512]{1,0:T(8,128)(2,1)S(1)} %get-tuple-element.38), channel_id=1, source_target_pairs={{0,1},{1,0},{2,3},{3,2},{4,5},{5,4},{6,7},{7,6},{8,9},{9,8},{10,11... | collective-permute-start | bytes 393224 | tf_op jit(solution)/shard_map/ppermute | solution.py:136
